TPU v7x, 32 devices: a whole 2x2x4 slice. The times are simulated.
32 devices in a mesh: seq: 8 (over z, core), head: 2 (over y), batch: 2 (over x).
Axes of the slice: x: 2, y: 2, z: 4, core: 2. Of those that a mesh axis runs over, the one named last changes fastest.
Arguments:
- queries: bfloat16 [4096, 1024], P(('batch', 'seq'), 'head'), parts along dimension 0, may hold values from -16 to 16, as said below
- key_rows: bfloat16 [4096, 256], P(('batch', 'seq'), 'head'), parts along dimension 0, may hold values from -16 to 16
- value_rows: bfloat16 [4096, 256], P(('batch', 'seq'), 'head'), parts along dimension 0, may hold values from -6 to 6
- out_grad: bfloat16 [4096, 1024], P(('batch', 'seq'), 'head'), parts along dimension 0, may hold values from -6 to 6
- tile_ids: int32 [32], P('batch'), parts along dimension 0, may hold values from 0 to 15, each once
- tile_mask: int32 [32, 16], P('batch'), parts along dimension 0, may hold values from 0 to 1, as said below
Outputs:
- attended: bfloat16 [4096, 1024], P(('batch', 'seq'), 'head'), parts along dimension 0
- query_grad: float32 [4096, 1024], P(('batch', 'seq'), 'head'), parts along dimension 0
- key_grad: float32 [4096, 256], P(('batch', 'seq'), 'head'), parts along dimension 0
- value_grad: float32 [4096, 256], P(('batch', 'seq'), 'head'), parts along dimension 0
There are 2 independent parts, one for each index of `batch`. A program takes and returns all parts, laid end to end along the dimension named above; each array names one. Nothing has to cross between parts.
Inputs may be any that keep to these rules, and one draw needn't show every extreme that they name: `queries`: in the hidden draw a few query rows equal scaled key rows of the same tile. `tile_mask`: 1 only where the key tile's index is at most the query tile's; 1 on the diagonal.
All inputs are finite; a program needn't handle non-finite values.
Results may differ from a plain program's by a relative error of at most 0.03.
Values may be sent and summed in bfloat16 or wider, within the bound.
No kernel may reach another device: no remote copies, remote signals or barrier semaphores. Data moves between devices by JAX's collectives and lax.ppermute only.
A program may use at most 64 MiB of HBM per device.

v0:
```python
import functools
import math

import jax
import jax.numpy as jnp
from jax import lax
from jax.experimental import pallas as pl
from jax.experimental.pallas import tpu as pltpu
from jax.sharding import PartitionSpec as P

HD = 128
TILE = 128
FAR_BELOW = -1e30
LOG2E = 1.4426950408889634
NT_DIMS = (((1,), (1,)), ((), ()))
VMEM_LIMIT = 32 * 1024 * 1024

SMEM_SPEC = pl.BlockSpec(memory_space=pltpu.SMEM)
VMEM_SPEC = pl.BlockSpec(memory_space=pltpu.VMEM)
ANY_SPEC = pl.BlockSpec(memory_space=pl.ANY)


def call(kernel, in_specs, out_shape, out_specs, scratch=(), flops=0, moved=0, aliases=None):
    return pl.pallas_call(
        kernel,
        in_specs=in_specs,
        out_shape=out_shape,
        out_specs=out_specs,
        scratch_shapes=list(scratch),
        input_output_aliases=aliases or {},
        compiler_params=pltpu.CompilerParams(vmem_limit_bytes=VMEM_LIMIT),
        cost_estimate=pl.CostEstimate(flops=flops, bytes_accessed=moved, transcendentals=0),
    )


def tile_rows(first_row, tile):
    return pl.ds(pl.multiple_of(first_row + tile * TILE, TILE), TILE)


def info_size(tile_total, tiles, slots):
    return 2 * tile_total + 2 + (slots + tiles) * tiles


def pairs_of(chips):
    return [(step, step + 1) for step in range(1, chips - 1, 2)]


def list_kernel(tile_total, tiles, slots, table_ref, *refs):
    sources, (info_ref, full_ref, half_ref, spare_ref, *refs) = refs[:4], refs[4:]
    any_ref, loaded, sems = refs[0], refs[1:5], refs[5:]
    del spare_ref
    rank = lax.axis_index("seq")
    copies = [
        pltpu.make_async_copy(source, target, sem)
        for source, target, sem in zip(sources, loaded, sems)
    ]
    for copy in copies:
        copy.start()

    def ids(position):
        return table_ref[tile_total, position]

    def mask(query_tile, key_tile):
        return table_ref[query_tile, key_tile]

    for place in range(1, tile_total + 2):
        info_ref[place] = 0
    for tile in range(tile_total):
        users = mask(0, tile)
        for other in range(1, tile_total):
            users = users + mask(other, tile)
        any_ref[tile] = users
    count = jnp.int32(0)
    for position in range(tile_total):
        key_tile = ids(position)
        away = any_ref[key_tile]
        for local in range(tiles):
            away = away - mask(ids(position // tiles * tiles + local), key_tile)
        info_ref[1 + count] = position
        info_ref[tile_total + 2 + position] = jnp.where(away > 0, count, -1)
        count = count + jnp.where(away > 0, 1, 0)
    info_ref[0] = count
    my_tiles = [ids(rank * tiles + b) for b in range(tiles)]
    place = 2 * tile_total + 2
    for slot in range(slots):
        position = info_ref[1 + slot]
        usable = ((slot < count) & (position // tiles != rank)).astype(jnp.int32)
        for b in range(tiles):
            info_ref[place] = usable * mask(my_tiles[b], ids(position))
            place += 1
    for a in range(tiles):
        for b in range(tiles):
            info_ref[place] = mask(my_tiles[b], my_tiles[a])
            place += 1
    for copy in copies:
        copy.wait()
    odd = rank % 2
    for kind in range(2):
        part = odd ^ kind
        target = full_ref.at[pl.ds(part * slots, slots)]
        pick(tiles, slots, 0, info_ref, loaded[kind], loaded[2 + kind], target)
    half_ref[...] = full_ref[:slots]


def pick(tiles, slots, base, info_ref, own_ref, other_ref, out_ref):
    rank = lax.axis_index("seq")
    for slot in range(slots):
        position = info_ref[1 + base + slot]
        home = position // tiles
        rows = tile_rows(0, position % tiles)
        out_ref[slot] = jnp.zeros_like(out_ref[slot])

        @pl.when(home == rank)
        def _():
            out_ref[slot] = own_ref[rows, :]

        @pl.when(home == rank ^ 1)
        def _():
            out_ref[slot] = other_ref[rows, :]


def select_kernel(tiles, slots, info_ref, round_ref, *refs):
    key_ref, value_ref, key_other, value_other, out_ref = refs
    rank = lax.axis_index("seq")
    for kind, own, other in ((0, key_ref, key_other), (1, value_ref, value_other)):

        @pl.when(rank % 2 == kind)
        def _():
            pick(tiles, slots, round_ref[0] * slots, info_ref, own, other, out_ref)


def add_sums(tiles, slots, tile_total, base, info_ref, grads, outs, sums_of):
    rank = lax.axis_index("seq")
    odd = rank % 2
    for grad, out in zip(grads, outs):
        out[...] = grad[...]
    for tile in range(tiles):
        slot = info_ref[tile_total + 2 + rank * tiles + tile] - base
        rows = tile_rows(0, tile)

        @pl.when((slot >= 0) & (slot < slots))
        def _():
            totals = []
            for part in range(2):
                total = None
                for source in sums_of(part, slot):
                    source = source.astype(jnp.float32)
                    total = source if total is None else total + source
                totals.append(total)
            for kind, out in enumerate(outs):
                out[rows, :] += jnp.where(odd == kind, totals[0], totals[1])


def close_kernel(tiles, slots, chips, tile_total, info_ref, *refs):
    grads, (chip_ref, *sums), outs = refs[:2], refs[2:-2], refs[-2:]
    half = len(sums) // 2
    arrived, handed = sums[:half], sums[half:]

    def sums_of(part, slot):
        yield chip_ref[part * slots + slot]
        for own, other in zip(arrived[:-1], handed[:-1]):
            yield own[part * slots + slot]
            yield other[(1 - part) * slots + slot]
        yield (handed if part else arrived)[-1][slot]

    add_sums(tiles, slots, tile_total, 0, info_ref, grads, outs, sums_of)


def later_kernel(tiles, slots, tile_total, info_ref, round_ref, *refs):
    grads, sums, outs = refs[:2], refs[2:-2], refs[-2:]

    def sums_of(part, slot):
        yield sums[part][slot]

    base = round_ref[0] * slots
    add_sums(tiles, slots, tile_total, base, info_ref, grads, outs, sums_of)


def causal_bias():
    later = lax.broadcasted_iota(jnp.int32, (TILE, TILE), 1)
    return jnp.where(lax.broadcasted_iota(jnp.int32, (TILE, TILE), 0) <= later, 0.0, FAR_BELOW)


def block_bias(allowed):
    return jnp.full((TILE, TILE), jnp.where(allowed, 0.0, FAR_BELOW), jnp.float32)


def own_bias(tiles, bias_ref, allowed):
    for a in range(tiles):
        for b in range(tiles):
            bias = causal_bias() if a == b else block_bias(allowed(a, b) == 1)
            bias_ref[pl.ds(a * TILE, TILE), pl.ds(b * TILE, TILE)] = bias


def stacked(ref, heads):
    return jnp.concatenate([ref[:, h * HD : (h + 1) * HD] for h in range(heads)], axis=0)


def dot(one, other):
    return jnp.dot(one, other, preferred_element_type=jnp.float32)


def dot_t(one, other):
    return lax.dot_general(one, other, NT_DIMS, preferred_element_type=jnp.float32)


def own_scores(tiles, slots, heads, tile_total, info_ref, bias_ref, keys, query):
    place = 2 * tile_total + 2 + slots * tiles
    own_bias(tiles, bias_ref, lambda a, b: info_ref[place + a * tiles + b])
    bias = jnp.concatenate([bias_ref[...]] * heads, axis=1)
    return dot_t(keys, query) * (HD**-0.5 * LOG2E) + bias


def own_kernel(
    tiles,
    slots,
    heads,
    tile_total,
    info_ref,
    query_ref,
    grad_ref,
    key_ref,
    value_ref,
    order_ref,
    max_ref,
    total_ref,
    weighted_ref,
    grad_t_ref,
    bias_ref,
):
    del order_ref
    query = stacked(query_ref, heads)
    scores = own_scores(tiles, slots, heads, tile_total, info_ref, bias_ref, key_ref[...], query)
    row_max = jnp.max(scores, axis=0, keepdims=True)
    terms = jnp.exp2(scores - row_max)
    max_ref[...] = row_max
    total_ref[...] = jnp.sum(terms, axis=0, keepdims=True)
    weighted_ref[...] = dot(value_ref[...].T, terms.astype(jnp.bfloat16))
    grad_t_ref[...] = stacked(grad_ref, heads).T


def gathered_kernel(
    chips,
    tiles,
    slots,
    heads,
    tile_total,
    info_ref,
    table_any,
    query_ref,
    grad_ref,
    key_ref,
    value_ref,
    key_other,
    value_other,
    max_own,
    total_own,
    weighted_own,
    grad_t_ref,
    more_ref,
    *refs,
):
    count = len(pairs_of(chips)) + 1
    arrived, handed, refs = refs[:count], refs[count : 2 * count], refs[2 * count :]
    parts_ref, max_ref, inverse_ref, delta_ref, out_t_ref, dscores_ref, *refs = refs
    slot_keys, *refs = refs
    more_out, attended_full, query_full, key_full, value_full, *refs = refs
    bias_ref, held_ref, sum_ref, score_ref, staged_ref, *refs = refs
    attended_ref, query_out, table_ref, copy_sem = refs
    keys_ref, values_ref = held_ref.at[0], held_ref.at[1]
    key_sum, value_sum = sum_ref.at[0], sum_ref.at[1]
    rank = lax.axis_index("seq")
    odd = rank % 2
    rows = tiles * TILE
    chunk = slots * TILE
    factor = HD**-0.5
    scale = factor * LOG2E
    needed = info_ref[0]
    columns = [pl.ds(h * HD, HD) for h in range(heads)]

    def repack(target, part, first_row):
        kind = odd ^ part
        for slot in range(slots):
            total = sum_ref[kind, tile_rows(first_row, slot), :]
            target[slot] = (total * jnp.where(kind == 0, factor, 1.0)).astype(jnp.bfloat16)

    for slot in range(slots):
        for b in range(tiles):
            allowed = info_ref[2 * tile_total + 2 + slot * tiles + b] == 1
            bias_ref[pl.ds(slot * TILE, TILE), pl.ds(b * TILE, TILE)] = block_bias(allowed)
        position = info_ref[1 + slot]
        away = (position // (2 * tiles)) ^ (rank // 2)
        at = tile_rows(0, slot)

        @pl.when(away == 0)
        def _():
            source = tile_rows(0, position % tiles)
            keys_ref[at, :] = key_other[source, :]
            values_ref[at, :] = value_other[source, :]

        @pl.when(away == chips - 1)
        def _():
            held_ref[odd, at, :] = arrived[-1][slot]
            held_ref[odd ^ 1, at, :] = handed[-1][slot]

        for index, pair in enumerate(pairs_of(chips)):
            for core, step in enumerate(pair):

                @pl.when((away == step) & (odd == core))
                def _():
                    held_ref[odd, at, :] = arrived[index][slot]
                    held_ref[odd ^ 1, at, :] = arrived[index][slots + slot]

                @pl.when((away == step) & (odd != core))
                def _():
                    held_ref[odd ^ 1, at, :] = handed[index][slot]
                    held_ref[odd, at, :] = handed[index][slots + slot]

    first = pl.ds(0, chunk)

    @pl.when(needed <= slots)
    def _():
        keys = keys_ref[first, :]
        values = values_ref[first, :]
        slot_keys[...] = keys
        query = stacked(query_ref, heads)
        grad = stacked(grad_ref, heads)
        bias = jnp.concatenate([bias_ref[first, :]] * heads, axis=1)
        scores = dot_t(keys, query) * scale + bias
        dprobs = dot_t(values, grad)
        row_max = jnp.maximum(max_own[...], jnp.max(scores, axis=0, keepdims=True))
        shrink = jnp.exp2(max_own[...] - row_max)
        terms = jnp.exp2(scores - row_max)
        inverse = 1.0 / (total_own[...] * shrink + jnp.sum(terms, axis=0, keepdims=True))
        weighted = weighted_own[...] * shrink + dot(values.T, terms.astype(jnp.bfloat16))
        out = (weighted * inverse).astype(jnp.bfloat16)
        delta = jnp.sum(
            grad_t_ref[...].astype(jnp.float32) * out.astype(jnp.float32), axis=0, keepdims=True
        )
        probs = terms * inverse
        dscores = (probs * (dprobs - delta)).astype(jnp.bfloat16)
        value_sum[first, :] = dot(probs.astype(jnp.bfloat16), grad)
        key_sum[first, :] = dot(dscores, query)
        out_t_ref[...] = out
        max_ref[...] = row_max
        inverse_ref[...] = inverse
        delta_ref[...] = delta
        dscores_ref[...] = dscores

    @pl.when(needed > slots)
    def _():
        used = (needed + slots - 1) // slots
        own_first = pl.multiple_of(used * chunk, chunk)
        own_rows = pl.ds(own_first, rows)
        copy = pltpu.make_async_copy(table_any, table_ref, copy_sem)
        copy.start()
        copy.wait()

        def ids(position):
            return table_ref[tile_total, position]

        def allowed(a, b):
            return table_ref[ids(rank * tiles + b), ids(rank * tiles + a)]

        own_bias(tiles, bias_ref.at[own_rows, :], allowed)
        keys_ref[own_rows, :] = key_ref[...]
        values_ref[own_rows, :] = value_ref[...]

        def fetch(index, carry):
            copy = pltpu.make_async_copy(more_ref.at[index - 1], staged_ref, copy_sem)
            copy.start()
            copy.wait()
            first_row = pl.multiple_of(index * chunk, chunk)
            for slot in range(slots):
                for part in range(2):
                    held_ref[odd ^ part, tile_rows(first_row, slot), :] = staged_ref[part, slot]
                listed = index * slots + slot
                position = info_ref[1 + listed]
                usable = (listed < needed) & (position // tiles != rank)
                for b in range(tiles):
                    seen = table_ref[ids(rank * tiles + b), ids(position)] == 1
                    bias_ref[tile_rows(first_row, slot), pl.ds(b * TILE, TILE)] = block_bias(
                        usable & seen
                    )
            return carry

        lax.fori_loop(1, used, fetch, 0)
        key_sum[...] = jnp.zeros_like(key_sum)
        value_sum[...] = jnp.zeros_like(value_sum)
        blocks = used * slots + tiles

        for h in range(heads):
            query = query_ref[:, columns[h]]
            grad = grad_ref[:, columns[h]]

            def score(index, row_max):
                at = tile_rows(0, index)
                scores = dot_t(keys_ref[at, :], query) * scale + bias_ref[at, :]
                score_ref[at, :] = scores
                return jnp.maximum(row_max, jnp.max(scores, axis=0, keepdims=True))

            row_max = lax.fori_loop(0, blocks, score, jnp.full((1, rows), FAR_BELOW, jnp.float32))

            def forward(index, carry):
                total, weighted = carry
                at = tile_rows(0, index)
                terms = jnp.exp2(score_ref[at, :] - row_max)
                score_ref[at, :] = terms
                weighted = weighted + dot(values_ref[at, :].T, terms.astype(jnp.bfloat16))
                return total + jnp.sum(terms, axis=0, keepdims=True), weighted

            zeros = jnp.zeros((HD, rows), jnp.float32)
            start = (jnp.zeros((1, rows), jnp.float32), zeros)
            total, weighted = lax.fori_loop(0, blocks, forward, start)
            inverse = 1.0 / total
            out = (weighted * inverse).astype(jnp.bfloat16)
            attended_ref[:, columns[h]] = out.T
            grad_t = grad_t_ref[:, pl.ds(h * rows, rows)].astype(jnp.float32)
            delta = jnp.sum(grad_t * out.astype(jnp.float32), axis=0, keepdims=True)

            def backward(index, query_t):
                at = tile_rows(0, index)
                probs = score_ref[at, :] * inverse
                dprobs = dot_t(values_ref[at, :], grad)
                dscores = (probs * (dprobs - delta)).astype(jnp.bfloat16)
                key_sum[at, :] += dot(dscores, query)
                value_sum[at, :] += dot(probs.astype(jnp.bfloat16), grad)
                return query_t + dot(keys_ref[at, :].T, dscores)

            query_t = lax.fori_loop(0, blocks, backward, zeros)
            query_out[:, columns[h]] = (query_t * factor).T

        key_sum[own_rows, :] = key_sum[own_rows, :] * factor
        for source, target in (
            (attended_ref, attended_full),
            (query_out, query_full),
            (key_sum.at[own_rows, :], key_full),
            (value_sum.at[own_rows, :], value_full),
        ):
            copy = pltpu.make_async_copy(source, target, copy_sem)
            copy.start()
            copy.wait()

        def store(index, carry):
            for part in range(2):
                repack(staged_ref.at[part], part, pl.multiple_of(index * chunk, chunk))
            copy = pltpu.make_async_copy(staged_ref, more_out.at[index - 1], copy_sem)
            copy.start()
            copy.wait()
            return carry

        lax.fori_loop(1, used, store, 0)

    for part in range(2):
        repack(parts_ref.at[pl.ds(part * slots, slots)], part, 0)


def rest_kernel(
    tiles,
    slots,
    heads,
    tile_total,
    info_ref,
    query_ref,
    grad_ref,
    key_ref,
    value_ref,
    max_ref,
    inverse_ref,
    delta_ref,
    out_t_ref,
    dscores_ref,
    slot_keys,
    attended_full,
    query_full,
    key_full,
    value_full,
    order_ref,
    attended_ref,
    query_out,
    key_out,
    value_out,
    order_out,
    bias_ref,
    copy_sem,
):
    del order_ref, order_out
    factor = HD**-0.5
    rows = tiles * TILE

    @pl.when(info_ref[0] <= slots)
    def _():
        keys = key_ref[...]
        query = stacked(query_ref, heads)
        grad = stacked(grad_ref, heads)
        scores = own_scores(tiles, slots, heads, tile_total, info_ref, bias_ref, keys, query)
        probs = jnp.exp2(scores - max_ref[...]) * inverse_ref[...]
        dprobs = dot_t(value_ref[...], grad)
        dscores = (probs * (dprobs - delta_ref[...])).astype(jnp.bfloat16)
        value_out[...] = dot(probs.astype(jnp.bfloat16), grad)
        key_out[...] = dot(dscores, query) * factor
        query_t = (dot(keys.T, dscores) + dot(slot_keys[...].T, dscores_ref[...])) * factor
        for h in range(heads):
            columns = pl.ds(h * HD, HD)
            attended_ref[:, columns] = out_t_ref[:, pl.ds(h * rows, rows)].T
            query_out[:, columns] = query_t[:, h * rows : (h + 1) * rows].T

    @pl.when(info_ref[0] > slots)
    def _():
        for source, target in (
            (attended_full, attended_ref),
            (query_full, query_out),
            (key_full, key_out),
            (value_full, value_out),
        ):
            copy = pltpu.make_async_copy(source, target, copy_sem)
            copy.start()
            copy.wait()


def per_device(queries, key_rows, value_rows, out_grad, tile_ids, tile_mask):
    row_count = queries.shape[0]
    heads = queries.shape[1] // HD
    ranks = lax.axis_size("seq")
    chips = ranks // 2
    assert key_rows.shape[1] == HD and ranks > 1 and ranks & (ranks - 1) == 0
    tiles = row_count // TILE
    tile_total = tile_ids.shape[0]
    slots = tiles
    rounds = math.ceil(tile_total / slots)
    slot_shape = (slots, TILE, HD)
    buffer = (rounds - 1, 2) + slot_shape
    shape = jax.ShapeDtypeStruct
    bf16, f32 = jnp.bfloat16, jnp.float32

    def swap(values, step):
        return lax.ppermute(values, "seq", [(source, source ^ step) for source in range(ranks)])

    def across(values):
        return [swap(values, 2 * step) for step in range(1, chips)]

    def trade(full, half):
        got = []
        for pair in pairs_of(chips):
            routes = [(source, source ^ 2 * pair[source % 2]) for source in range(ranks)]
            got.append(lax.ppermute(full, "seq", routes))
        return got + [swap(half, 2 * (chips - 1))]

    def add(*values):
        total = values[0].astype(f32)
        for value in values[1:]:
            total = total + value.astype(f32)
        return total.astype(bf16)

    table = jnp.pad(tile_mask, ((0, 1), (0, 0)))
    table = table + jnp.pad(tile_ids[None], ((tile_total, 0), (0, 0)))
    key_other, value_other = swap(key_rows, 1), swap(value_rows, 1)
    chip_rows = (key_rows, value_rows, key_other, value_other)
    info, chosen, chosen_half, spare = call(
        functools.partial(list_kernel, tile_total, tiles, slots),
        [SMEM_SPEC] + [ANY_SPEC] * 4,
        (
            shape((info_size(tile_total, tiles, slots),), jnp.int32),
            shape((2 * slots, TILE, HD), bf16),
            shape(slot_shape, bf16),
            shape(buffer, bf16),
        ),
        (SMEM_SPEC, VMEM_SPEC, VMEM_SPEC, ANY_SPEC),
        scratch=(
            pltpu.SMEM((tile_total,), jnp.int32),
            *[pltpu.VMEM(key_rows.shape, bf16)] * 4,
            *[pltpu.SemaphoreType.DMA] * 4,
        ),
        moved=4 * 1024 * 1024,
    )(table, *chip_rows)
    used = (info[0] + slots - 1) // slots

    def select(index):
        return call(
            functools.partial(select_kernel, tiles, slots),
            [SMEM_SPEC] * 2 + [VMEM_SPEC] * 4,
            shape(slot_shape, bf16),
            VMEM_SPEC,
            moved=5 * row_count * HD * 2,
        )(info, index.reshape(1), *chip_rows)

    arrived = trade(chosen, chosen_half)
    handed = [swap(values, 1) for values in arrived]

    def gather_more(index, buffered):
        chosen = select(index)
        total = add(chosen, *across(chosen))
        pair = jnp.stack([total, swap(total, 1)])
        return lax.dynamic_update_index_in_dim(buffered, pair, index - 1, 0)

    more = lax.fori_loop(1, used, gather_more, spare)

    all_rows = row_count + rounds * slots * TILE
    columns = heads * row_count
    line = shape((1, columns), f32)
    work = 2 * columns * row_count * HD
    max_own, total_own, weighted, grad_t = call(
        functools.partial(own_kernel, tiles, slots, heads, tile_total),
        [SMEM_SPEC] + [VMEM_SPEC] * 4 + [ANY_SPEC],
        (line, line, shape((HD, columns), f32), shape((HD, columns), bf16)),
        (VMEM_SPEC,) * 4,
        scratch=(pltpu.VMEM((row_count, row_count), f32),),
        flops=24 * work,
        moved=4 * row_count * heads * HD,
    )(info, queries, out_grad, key_rows, value_rows, more)

    full = (
        shape(queries.shape, bf16),
        shape(queries.shape, f32),
        shape(key_rows.shape, f32),
        shape(value_rows.shape, f32),
    )
    parts, row_max, inverse, delta, out_t, dscores, slot_keys, more_terms, *full_values = call(
        functools.partial(gathered_kernel, chips, tiles, slots, heads, tile_total),
        [SMEM_SPEC, ANY_SPEC] + [VMEM_SPEC] * 10 + [ANY_SPEC] + [VMEM_SPEC] * (2 * len(arrived)),
        (
            shape((2 * slots, TILE, HD), bf16),
            line,
            line,
            line,
            shape((HD, columns), bf16),
            shape((slots * TILE, columns), bf16),
            shape((slots * TILE, HD), bf16),
            shape(buffer, bf16),
        )
        + full,
        (VMEM_SPEC,) * 7 + (ANY_SPEC,) * 5,
        scratch=(
            pltpu.VMEM((all_rows, row_count), f32),
            pltpu.VMEM((2, all_rows, HD), bf16),
            pltpu.VMEM((2, all_rows, HD), f32),
            pltpu.VMEM((all_rows, row_count), f32),
            pltpu.VMEM((2,) + slot_shape, bf16),
            pltpu.VMEM(queries.shape, bf16),
            pltpu.VMEM(queries.shape, f32),
            pltpu.SMEM(table.shape, jnp.int32),
            pltpu.SemaphoreType.DMA,
        ),
        flops=24 * work,
        moved=4 * row_count * heads * HD,
    )(
        info,
        table,
        queries,
        out_grad,
        *chip_rows,
        max_own,
        total_own,
        weighted,
        grad_t,
        more,
        *arrived,
        *handed,
    )

    partner = swap(parts, 1)
    half_sum = add(parts[:slots], partner[slots:])
    chip_sum = jnp.concatenate([half_sum, add(parts[slots:], partner[:slots])])
    back = trade(chip_sum, half_sum)
    attended, query_grad, key_own, value_own, back[0] = call(
        functools.partial(rest_kernel, tiles, slots, heads, tile_total),
        [SMEM_SPEC] + [VMEM_SPEC] * 10 + [ANY_SPEC] * 5,
        full + (shape(back[0].shape, bf16),),
        (VMEM_SPEC,) * 4 + (ANY_SPEC,),
        scratch=(pltpu.VMEM((row_count, row_count), f32), pltpu.SemaphoreType.DMA),
        flops=32 * work,
        moved=8 * row_count * heads * HD,
        aliases={15: 4},
    )(
        info,
        queries,
        out_grad,
        key_rows,
        value_rows,
        row_max,
        inverse,
        delta,
        out_t,
        dscores,
        slot_keys,
        *full_values,
        back[0],
    )
    sums = [chip_sum] + back + [swap(values, 1) for values in back]

    def close(kernel, lead, grads, sums):
        return call(
            kernel,
            [SMEM_SPEC] * len(lead) + [VMEM_SPEC] * (2 + len(sums)),
            (shape(key_rows.shape, f32), shape(value_rows.shape, f32)),
            (VMEM_SPEC,) * 2,
            moved=5 * row_count * HD * 4,
        )(*lead, *grads, *sums)

    def reduce_more(index, grads):
        terms = lax.dynamic_index_in_dim(more_terms, index - 1, 0, keepdims=False)
        part = add(terms[0], swap(terms[1], 1))
        total = add(part, *across(part))
        kernel = functools.partial(later_kernel, tiles, slots, tile_total)
        return tuple(close(kernel, (info, index.reshape(1)), grads, (total, swap(total, 1))))

    kernel = functools.partial(close_kernel, tiles, slots, chips, tile_total)
    grads = tuple(close(kernel, (info,), (key_own, value_own), sums))
    key_grad, value_grad = lax.fori_loop(1, used, reduce_more, grads)
    return attended, query_grad, key_grad, value_grad


def solution(mesh):
    return jax.shard_map(
        per_device,
        mesh=mesh,
        in_specs=(
            P(("batch", "seq"), "head"),
            P(("batch", "seq"), "head"),
            P(("batch", "seq"), "head"),
            P(("batch", "seq"), "head"),
            P("batch"),
            P("batch", None),
        ),
        out_specs=(P(("batch", "seq"), "head"),) * 4,
        check_vma=False,
    )
```

profile of v0, /device:TPU:0, one launch (start us, length us, event | category | flops | bytes accessed | tf_op | source)
XLA Modules:
  0.0 35.2 jit_solution(444213781949377927)
XLA Ops:
  0.6 0.5 %collective-permute-start.10 = (bf16[256,128]{1,0:T(8,128)(2,1)}, bf16[256,128]{1,0:T(8,128)(2,1)S(1)}, u32[]{:S(2)}, u32[]{:S(2)}) collective-permute-start(bf16[256,128]{1,0:T(8,128)(2,1)} %value_ref.5), channel_id=1, source_target_pairs={{0,4},{4,0},{8,12},{12,8},{16,20},{20,16},{24,28},{28,24},{1,5},{5... | collective-permute-start | bytes 196616 | tf_op jit(solution)/shard_map/ppermute | solution.py:537
  1.2 0.1 collective-permute-start.9
  1.2 0.0 copy-done.6
  1.3 0.7 %pad_add_fusion.table_ref.table_any = s32[17,16]{1,0:T(8,128)S(1)} fusion(s32[1,16]{1,0:T(1,128)S(1)} %bitcast.35, s32[16,16]{1,0:T(8,128)} %param.15), kind=kLoop, calls=%fused_computation.11 | loop fusion | flops 272 | bytes 2176 | tf_op jit(solution)/shard_map/add | solution.py:556
  2.0 0.3 collective-permute-done.10.refs_3_.value_other
  2.3 0.4 %collective-permute-done.9.refs_2_.key_other = bf16[256,128]{1,0:T(8,128)(2,1)S(1)} collective-permute-done((bf16[256,128]{1,0:T(8,128)(2,1)}, bf16[256,128]{1,0:T(8,128)(2,1)S(1)}, u32[]{:S(2)}, u32[]{:S(2)}) %collective-permute-start.9) | collective-permute-done | bytes 65568 | tf_op jit(solution)/shard_map/ppermute | solution.py:537
  2.6 2.3 %shard_map.93 = (s32[42]{0:T(128)S(1)}, bf16[4,128,128]{2,1,0:T(8,128)(2,1)S(1)}, bf16[2,128,128]{2,1,0:T(8,128)(2,1)S(1)}, bf16[7,2,2,128,128]{4,3,2,1,0:T(8,128)(2,1)S(1)}) custom-call(s32[17,16]{1,0:T(8,128)S(1)} %pad_add_fusion.table_ref.table_any, bf16[256,128]{1,0:T(8,128)(2,1)} %key_ref.5, bf16[256,128]{1,0:T(8,128)(2,1)} %value_ref.5, ...), custom_call_target="tpu_custom_call" | custom-call | bytes 4194304 | tf_op jit(solution)/shard_map/pallas_call | solution.py:559
  4.9 2.8 %collective-permute-start.11 = (bf16[4,128,128]{2,1,0:T(8,128)(2,1)S(1)}, bf16[4,128,128]{2,1,0:T(8,128)(2,1)S(1)}, u32[]{:S(2)}, u32[]{:S(2)}) collective-permute-start(bf16[4,128,128]{2,1,0:T(8,128)(2,1)S(1)} %get-tuple-element.333), channel_id=1, source_target_pairs={{0,8},{4,20},{8,0},{12,28},{16,24},{20,4},{24,16},{28,12},{1,9},{5... | collective-permute-start | bytes 393224 | tf_op jit(solution)/shard_map/ppermute | solution.py:546
  7.7 2.5 %collective-permute-start.12 = (bf16[2,128,128]{2,1,0:T(8,128)(2,1)S(1)}, bf16[2,128,128]{2,1,0:T(8,128)(2,1)S(1)}, u32[]{:S(2)}, u32[]{:S(2)}) collective-permute-start(bf16[2,128,128]{2,1,0:T(8,128)(2,1)S(1)} %get-tuple-element.334), channel_id=1, source_target_pairs={{0,24},{4,28},{8,16},{12,20},{16,8},{20,12},{24,0},{28,4},{1,25},{... | collective-permute-start | bytes 196616 | tf_op jit(solution)/shard_map/ppermute | solution.py:537
  10.3 5.0 %collective-permute-done.12.refs_1_ = bf16[2,128,128]{2,1,0:T(8,128)(2,1)S(1)} collective-permute-done((bf16[2,128,128]{2,1,0:T(8,128)(2,1)S(1)}, bf16[2,128,128]{2,1,0:T(8,128)(2,1)S(1)}, u32[]{:S(2)}, u32[]{:S(2)}) %collective-permute-start.12) | collective-permute-done | bytes 65568 | tf_op jit(solution)/shard_map/ppermute | solution.py:537
  15.3 0.0 collective-permute-start.14
  15.3 0.0 collective-permute-done.11.refs_0_
  15.3 0.5 %collective-permute-start.13 = (bf16[4,128,128]{2,1,0:T(8,128)(2,1)S(1)}, bf16[4,128,128]{2,1,0:T(8,128)(2,1)S(1)}, u32[]{:S(2)}, u32[]{:S(2)}) collective-permute-start(bf16[4,128,128]{2,1,0:T(8,128)(2,1)S(1)} %collective-permute-done.11.refs_0_), channel_id=1, source_target_pairs={{0,4},{4,0},{8,12},{12,8},{16,20},{20,16},{24,28},{28,24},{1,5},{5... | collective-permute-start | bytes 393224 | tf_op jit(solution)/shard_map/ppermute | solution.py:537
  15.8 0.9 %copy-done = bf16[256,512]{1,0:T(8,128)(2,1)S(1)} copy-done((bf16[256,512]{1,0:T(8,128)(2,1)S(1)}, bf16[256,512]{1,0:T(8,128)(2,1)}, u32[]{:S(2)}) %copy-start) | copy-done | bytes 262168
  16.8 0.1 copy-done.1
  16.8 1.2 %shard_map.94 = (f32[1,1024]{1,0:T(1,128)S(1)}, f32[1,1024]{1,0:T(1,128)S(1)}, f32[128,1024]{1,0:T(8,128)S(1)}, bf16[128,1024]{1,0:T(8,128)(2,1)S(1)}) custom-call(s32[42]{0:T(128)S(1)} %get-tuple-element.591, bf16[256,512]{1,0:T(8,128)(2,1)S(1)} %copy-done, bf16[256,512]{1,0:T(8,128)(2,1)S(1)} %copy-done.1, bf16[256,128]{1,0:T(8,128)(2,1)S(1)} %get-tuple-element.573, ...), custom_call_target="tpu_custom_call" | custom-call | flops 1610612736 | bytes 524288 | tf_op jit(solution)/shard_map/pallas_call | solution.py:602
  18.0 0.0 collective-permute-done.14.refs_3_
  18.0 2.0 %shard_map.95 = (bf16[4,128,128]{2,1,0:T(8,128)(2,1)S(1)}, f32[1,1024]{1,0:T(1,128)S(1)}, f32[1,1024]{1,0:T(1,128)S(1)}, f32[1,1024]{1,0:T(1,128)S(1)}, bf16[128...) custom-call(s32[42]{0:T(128)S(1)} %get-tuple-element.591, ...), custom_call_target="tpu_custom_call" | custom-call | flops 1610612736 | bytes 524288 | tf_op jit(solution)/shard_map/pallas_call | solution.py:618
  20.1 0.1 collective-permute-start.15
  20.2 1.3 %collective-permute-done.15 = bf16[4,128,128]{2,1,0:T(8,128)(2,1)S(1)} collective-permute-done((bf16[4,128,128]{2,1,0:T(8,128)(2,1)S(1)}, bf16[4,128,128]{2,1,0:T(8,128)(2,1)S(1)}, u32[]{:S(2)}, u32[]{:S(2)}) %collective-permute-start.15) | collective-permute-done | bytes 131104 | tf_op jit(solution)/shard_map/ppermute | solution.py:537
  21.5 0.8 %collective-permute-start.16 = (bf16[4,128,128]{2,1,0:T(8,128)(2,1)S(1)}, bf16[4,128,128]{2,1,0:T(8,128)(2,1)S(1)}, u32[]{:S(2)}, u32[]{:S(2)}) collective-permute-start(bf16[4,128,128]{2,1,0:T(8,128)(2,1)S(1)} %pad_maximum_fusion.refs_2_), channel_id=1, source_target_pairs={{0,8},{4,20},{8,0},{12,28},{16,24},{20,4},{24,16},{28,12},{1,9},{5... | collective-permute-start | bytes 393224 | tf_op jit(solution)/shard_map/ppermute | solution.py:546
  22.4 3.1 %collective-permute-start.17 = (bf16[2,128,128]{2,1,0:T(8,128)(2,1)S(1)}, bf16[2,128,128]{2,1,0:T(8,128)(2,1)S(1)}, u32[]{:S(2)}, u32[]{:S(2)}) collective-permute-start(bf16[2,128,128]{2,1,0:T(8,128)(2,1)S(1)} %get-tuple-element.384), channel_id=1, source_target_pairs={{0,24},{4,28},{8,16},{12,20},{16,8},{20,12},{24,0},{28,4},{1,25},{... | collective-permute-start | bytes 196616 | tf_op jit(solution)/shard_map/ppermute | solution.py:537
  25.5 1.6 %collective-permute-done.16.order_ref = bf16[4,128,128]{2,1,0:T(8,128)(2,1)S(1)} collective-permute-done((bf16[4,128,128]{2,1,0:T(8,128)(2,1)S(1)}, bf16[4,128,128]{2,1,0:T(8,128)(2,1)S(1)}, u32[]{:S(2)}, u32[]{:S(2)}) %collective-permute-start.16) | collective-permute-done | bytes 131104 | tf_op jit(solution)/shard_map/ppermute | solution.py:546
  27.1 2.5 %shard_map.96 = (bf16[256,512]{1,0:T(8,128)(2,1)}, f32[256,512]{1,0:T(8,128)}, f32[256,128]{1,0:T(8,128)S(1)}, f32[256,128]{1,0:T(8,128)S(1)}, bf16[4,128,128]{2,1,0:T(8,128)(2,1)S(1)}) custom-call(s32[42]{0:T(128)S(1)} %get-tuple-element.591, bf16[256,512]{1,0:T(8,128)(2,1)S(1)} %copy-done, ...), custom_call_target="tpu_custom_call", output_to_operand_aliasing={{4}: (15, {})} | custom-call | flops 2147483648 | bytes 1048576 | tf_op jit(solution)/shard_map/pallas_call | solution.py:665
  29.6 3.0 %collective-permute-start.18 = (bf16[4,128,128]{2,1,0:T(8,128)(2,1)S(1)}, bf16[4,128,128]{2,1,0:T(8,128)(2,1)S(1)}, u32[]{:S(2)}, u32[]{:S(2)}) collective-permute-start(bf16[4,128,128]{2,1,0:T(8,128)(2,1)S(1)} %get-tuple-element.350.refs_3_), channel_id=1, source_target_pairs={{0,4},{4,0},{8,12},{12,8},{16,20},{20,16},{24,28},{28,24},{1,5},{5... | collective-permute-start | bytes 393224 | tf_op jit(solution)/shard_map/ppermute | solution.py:537
  32.6 0.1 collective-permute-start.19
  32.7 1.2 %collective-permute-done.19.refs_6_ = bf16[2,128,128]{2,1,0:T(8,128)(2,1)S(1)} collective-permute-done((bf16[2,128,128]{2,1,0:T(8,128)(2,1)S(1)}, bf16[2,128,128]{2,1,0:T(8,128)(2,1)S(1)}, u32[]{:S(2)}, u32[]{:S(2)}) %collective-permute-start.19) | collective-permute-done | bytes 65568 | tf_op jit(solution)/shard_map/ppermute | solution.py:537
  33.9 0.6 %shard_map.97 = (f32[256,128]{1,0:T(8,128)S(1)}, f32[256,128]{1,0:T(8,128)S(1)}) custom-call(s32[42]{0:T(128)S(1)} %get-tuple-element.591, f32[256,128]{1,0:T(8,128)S(1)} %get-tuple-element.348.refs_0_, f32[256,128]{1,0:T(8,128)S(1)} %get-tuple-element.349.refs_1_, bf16[4,128,128]{2,1,0:T(8,128)(2,1)S(1)} %pad_maximum_fusion.refs_2_, ...), custom_call_target="tpu_custom_call" | custom-call | bytes 655360 | tf_op jit(solution)/shard_map/pallas_call | solution.py:692
  34.5 0.0 copy-start.2
  34.5 0.0 copy-start.3
  34.5 0.6 %copy-done.2 = f32[256,128]{1,0:T(8,128)} copy-done((f32[256,128]{1,0:T(8,128)}, f32[256,128]{1,0:T(8,128)S(1)}, u32[]{:S(2)}) %copy-start.2) | copy-done | bytes 131096
  35.1 0.0 copy-done.3
  (14 shorter events, 0.1 us)
Async XLA Ops:
  0.6 0.7 %copy-start.6 = (s32[16]{0:T(128)S(1)}, s32[16]{0:T(128)}, u32[]{:S(2)}) copy-start(s32[16]{0:T(128)} %param.14) | copy-start | bytes 196
  0.6 1.6 %collective-permute-start.10 = (bf16[256,128]{1,0:T(8,128)(2,1)}, bf16[256,128]{1,0:T(8,128)(2,1)S(1)}, u32[]{:S(2)}, u32[]{:S(2)}) collective-permute-start(bf16[256,128]{1,0:T(8,128)(2,1)} %value_ref.5), channel_id=1, source_target_pairs={{0,4},{4,0},{8,12},{12,8},{16,20},{20,16},{24,28},{28,24},{1,5},{5... | collective-permute-start | bytes 196616 | tf_op jit(solution)/shard_map/ppermute | solution.py:537
  1.2 1.5 %collective-permute-start.9 = (bf16[256,128]{1,0:T(8,128)(2,1)}, bf16[256,128]{1,0:T(8,128)(2,1)S(1)}, u32[]{:S(2)}, u32[]{:S(2)}) collective-permute-start(bf16[256,128]{1,0:T(8,128)(2,1)} %key_ref.5), channel_id=1, source_target_pairs={{0,4},{4,0},{8,12},{12,8},{16,20},{20,16},{24,28},{28,24},{1,5},{5... | collective-permute-start | bytes 196616 | tf_op jit(solution)/shard_map/ppermute | solution.py:537
  2.0 13.8 %copy-start.4 = (bf16[256,128]{1,0:T(8,128)(2,1)S(1)}, bf16[256,128]{1,0:T(8,128)(2,1)}, u32[]{:S(2)}) copy-start(bf16[256,128]{1,0:T(8,128)(2,1)} %key_ref.5) | copy-start | bytes 196612
  2.0 13.8 %copy-start.5 = (bf16[256,128]{1,0:T(8,128)(2,1)S(1)}, bf16[256,128]{1,0:T(8,128)(2,1)}, u32[]{:S(2)}) copy-start(bf16[256,128]{1,0:T(8,128)(2,1)} %value_ref.5) | copy-start | bytes 196612
  4.9 10.4 %collective-permute-start.11 = (bf16[4,128,128]{2,1,0:T(8,128)(2,1)S(1)}, bf16[4,128,128]{2,1,0:T(8,128)(2,1)S(1)}, u32[]{:S(2)}, u32[]{:S(2)}) collective-permute-start(bf16[4,128,128]{2,1,0:T(8,128)(2,1)S(1)} %get-tuple-element.333), channel_id=1, source_target_pairs={{0,8},{4,20},{8,0},{12,28},{16,24},{20,4},{24,16},{28,12},{1,9},{5... | collective-permute-start | bytes 393224 | tf_op jit(solution)/shard_map/ppermute | solution.py:546
  7.7 7.6 %collective-permute-start.12 = (bf16[2,128,128]{2,1,0:T(8,128)(2,1)S(1)}, bf16[2,128,128]{2,1,0:T(8,128)(2,1)S(1)}, u32[]{:S(2)}, u32[]{:S(2)}) collective-permute-start(bf16[2,128,128]{2,1,0:T(8,128)(2,1)S(1)} %get-tuple-element.334), channel_id=1, source_target_pairs={{0,24},{4,28},{8,16},{12,20},{16,8},{20,12},{24,0},{28,4},{1,25},{... | collective-permute-start | bytes 196616 | tf_op jit(solution)/shard_map/ppermute | solution.py:537
  15.3 2.7 %collective-permute-start.14 = (bf16[2,128,128]{2,1,0:T(8,128)(2,1)S(1)}, bf16[2,128,128]{2,1,0:T(8,128)(2,1)S(1)}, u32[]{:S(2)}, u32[]{:S(2)}) collective-permute-start(bf16[2,128,128]{2,1,0:T(8,128)(2,1)S(1)} %collective-permute-done.12.refs_1_), channel_id=1, source_target_pairs={{0,4},{4,0},{8,12},{12,8},{16,20},{20,16},{24,28},{28,24},{1,5},{5... | collective-permute-start | bytes 196616 | tf_op jit(solution)/shard_map/ppermute | solution.py:537
  15.3 2.7 %collective-permute-start.13 = (bf16[4,128,128]{2,1,0:T(8,128)(2,1)S(1)}, bf16[4,128,128]{2,1,0:T(8,128)(2,1)S(1)}, u32[]{:S(2)}, u32[]{:S(2)}) collective-permute-start(bf16[4,128,128]{2,1,0:T(8,128)(2,1)S(1)} %collective-permute-done.11.refs_0_), channel_id=1, source_target_pairs={{0,4},{4,0},{8,12},{12,8},{16,20},{20,16},{24,28},{28,24},{1,5},{5... | collective-permute-start | bytes 393224 | tf_op jit(solution)/shard_map/ppermute | solution.py:537
  15.8 1.0 %copy-start = (bf16[256,512]{1,0:T(8,128)(2,1)S(1)}, bf16[256,512]{1,0:T(8,128)(2,1)}, u32[]{:S(2)}) copy-start(bf16[256,512]{1,0:T(8,128)(2,1)} %query_ref.5) | copy-start | bytes 786436
  15.8 1.0 %copy-start.1 = (bf16[256,512]{1,0:T(8,128)(2,1)S(1)}, bf16[256,512]{1,0:T(8,128)(2,1)}, u32[]{:S(2)}) copy-start(bf16[256,512]{1,0:T(8,128)(2,1)} %grad_ref.5) | copy-start | bytes 786436
  20.1 1.4 %collective-permute-start.15 = (bf16[4,128,128]{2,1,0:T(8,128)(2,1)S(1)}, bf16[4,128,128]{2,1,0:T(8,128)(2,1)S(1)}, u32[]{:S(2)}, u32[]{:S(2)}) collective-permute-start(bf16[4,128,128]{2,1,0:T(8,128)(2,1)S(1)} %get-tuple-element.345), channel_id=1, source_target_pairs={{0,4},{4,0},{8,12},{12,8},{16,20},{20,16},{24,28},{28,24},{1,5},{5... | collective-permute-start | bytes 393224 | tf_op jit(solution)/shard_map/ppermute | solution.py:537
  21.5 5.6 %collective-permute-start.16 = (bf16[4,128,128]{2,1,0:T(8,128)(2,1)S(1)}, bf16[4,128,128]{2,1,0:T(8,128)(2,1)S(1)}, u32[]{:S(2)}, u32[]{:S(2)}) collective-permute-start(bf16[4,128,128]{2,1,0:T(8,128)(2,1)S(1)} %pad_maximum_fusion.refs_2_), channel_id=1, source_target_pairs={{0,8},{4,20},{8,0},{12,28},{16,24},{20,4},{24,16},{28,12},{1,9},{5... | collective-permute-start | bytes 393224 | tf_op jit(solution)/shard_map/ppermute | solution.py:546
  22.4 10.2 %collective-permute-start.17 = (bf16[2,128,128]{2,1,0:T(8,128)(2,1)S(1)}, bf16[2,128,128]{2,1,0:T(8,128)(2,1)S(1)}, u32[]{:S(2)}, u32[]{:S(2)}) collective-permute-start(bf16[2,128,128]{2,1,0:T(8,128)(2,1)S(1)} %get-tuple-element.384), channel_id=1, source_target_pairs={{0,24},{4,28},{8,16},{12,20},{16,8},{20,12},{24,0},{28,4},{1,25},{... | collective-permute-start | bytes 196616 | tf_op jit(solution)/shard_map/ppermute | solution.py:537
  29.6 4.3 %collective-permute-start.18 = (bf16[4,128,128]{2,1,0:T(8,128)(2,1)S(1)}, bf16[4,128,128]{2,1,0:T(8,128)(2,1)S(1)}, u32[]{:S(2)}, u32[]{:S(2)}) collective-permute-start(bf16[4,128,128]{2,1,0:T(8,128)(2,1)S(1)} %get-tuple-element.350.refs_3_), channel_id=1, source_target_pairs={{0,4},{4,0},{8,12},{12,8},{16,20},{20,16},{24,28},{28,24},{1,5},{5... | collective-permute-start | bytes 393224 | tf_op jit(solution)/shard_map/ppermute | solution.py:537
  32.6 1.3 %collective-permute-start.19 = (bf16[2,128,128]{2,1,0:T(8,128)(2,1)S(1)}, bf16[2,128,128]{2,1,0:T(8,128)(2,1)S(1)}, u32[]{:S(2)}, u32[]{:S(2)}) collective-permute-start(bf16[2,128,128]{2,1,0:T(8,128)(2,1)S(1)} %collective-permute-done.17.refs_4_), channel_id=1, source_target_pairs={{0,4},{4,0},{8,12},{12,8},{16,20},{20,16},{24,28},{28,24},{1,5},{5... | collective-permute-start | bytes 196616 | tf_op jit(solution)/shard_map/ppermute | solution.py:537
  34.5 0.7 %copy-start.2 = (f32[256,128]{1,0:T(8,128)}, f32[256,128]{1,0:T(8,128)S(1)}, u32[]{:S(2)}) copy-start(f32[256,128]{1,0:T(8,128)S(1)} %get-tuple-element.324) | copy-start | bytes 393220
  34.5 0.7 %copy-start.3 = (f32[256,128]{1,0:T(8,128)}, f32[256,128]{1,0:T(8,128)S(1)}, u32[]{:S(2)}) copy-start(f32[256,128]{1,0:T(8,128)S(1)} %get-tuple-element.325) | copy-start | bytes 393220
where the time goes:
time: 35.4 us; the launch traced here: 35.2 us
  starting transfers between devices  13.5 us (38%)
  waiting for transfers between devices  9.79 us (28%)
  Pallas kernels  8.52 us (24%)
  local copies, waits for them, and re-layouts  1.75 us (5%)
  between operations  0.82 us (2%)
  other arithmetic  0.76 us (2%)
    ppermute x9, starting transfers between devices, swap(): lax.ppermute(values, 'seq', [(source, source ^ step) for source in range(...  9.88 us
    ppermute x9, waiting for transfers between devices, swap(): lax.ppermute(values, 'seq', [(source, source ^ step) for source in range(...  8.15 us
    ppermute x2, starting transfers between devices, trade(): got.append(lax.ppermute(full, 'seq', routes))  3.64 us
    pallas_call x1, Pallas kernels, per_device(): call(functools.partial(rest_kernel, tiles, slots, heads, tile_total), [SM...  2.45 us
    pallas_call x1, Pallas kernels, per_device(): call(functools.partial(list_kernel, tile_total, tiles, slots), [SMEM_SPEC...  2.3 us
    pallas_call x1, Pallas kernels, per_device(): call(functools.partial(gathered_kernel, chips, tiles, slots, heads, tile_...  2.03 us
    unnamed x14, local copies, waits for them, and re-layouts  1.75 us
    ppermute x2, waiting for transfers between devices, trade(): got.append(lax.ppermute(full, 'seq', routes))  1.64 us
  transfers between devices with their start and end apart: 11, of which 6 were waited for; matrix products, arithmetic and copies ran while one was open for 2% of the time, Pallas kernels for 10%

commit v1 on v0

--- a/solution.py
+++ b/solution.py
@@ -221,14 +221,12 @@
     grad_ref,
     key_ref,
     value_ref,
-    order_ref,
     max_ref,
     total_ref,
     weighted_ref,
     grad_t_ref,
     bias_ref,
 ):
-    del order_ref
     query = stacked(query_ref, heads)
     scores = own_scores(tiles, slots, heads, tile_total, info_ref, bias_ref, key_ref[...], query)
     row_max = jnp.max(scores, axis=0, keepdims=True)
@@ -601,13 +599,13 @@
     work = 2 * columns * row_count * HD
     max_own, total_own, weighted, grad_t = call(
         functools.partial(own_kernel, tiles, slots, heads, tile_total),
-        [SMEM_SPEC] + [VMEM_SPEC] * 4 + [ANY_SPEC],
+        [SMEM_SPEC] + [VMEM_SPEC] * 4,
         (line, line, shape((HD, columns), f32), shape((HD, columns), bf16)),
         (VMEM_SPEC,) * 4,
         scratch=(pltpu.VMEM((row_count, row_count), f32),),
         flops=24 * work,
         moved=4 * row_count * heads * HD,
-    )(info, queries, out_grad, key_rows, value_rows, more)
+    )(info, queries, out_grad, key_rows, value_rows)
 
     full = (
         shape(queries.shape, bf16),
@@ -661,11 +659,10 @@
     partner = swap(parts, 1)
     half_sum = add(parts[:slots], partner[slots:])
     chip_sum = jnp.concatenate([half_sum, add(parts[slots:], partner[:slots])])
-    back = trade(chip_sum, half_sum)
-    attended, query_grad, key_own, value_own, back[0] = call(
+    attended, query_grad, key_own, value_own, half_sum = call(
         functools.partial(rest_kernel, tiles, slots, heads, tile_total),
         [SMEM_SPEC] + [VMEM_SPEC] * 10 + [ANY_SPEC] * 5,
-        full + (shape(back[0].shape, bf16),),
+        full + (shape(slot_shape, bf16),),
         (VMEM_SPEC,) * 4 + (ANY_SPEC,),
         scratch=(pltpu.VMEM((row_count, row_count), f32), pltpu.SemaphoreType.DMA),
         flops=32 * work,
@@ -684,8 +681,9 @@
         dscores,
         slot_keys,
         *full_values,
-        back[0],
+        half_sum,
     )
+    back = trade(chip_sum, half_sum)
     sums = [chip_sum] + back + [swap(values, 1) for values in back]
 
     def close(kernel, lead, grads, sums):

time: 35.4 us -> 33.1 us (0.935)
  starting transfers between devices: 13.5 us -> 11.3 us
  Pallas kernels: 8.52 us -> 8.93 us
  waiting for transfers between devices: 9.79 us -> 9.42 us
    ppermute x9, starting transfers between devices: 9.88 us -> 7.43 us  [swap(): lax.ppermute(values, 'seq', [(source, source ^ step) for source in range(...]
    ppermute x2, waiting for transfers between devices: 1.64 us -> 0.01 us  [trade(): got.append(lax.ppermute(full, 'seq', routes))]
    ppermute x9, waiting for transfers between devices: 8.15 us -> 9.42 us  [swap(): lax.ppermute(values, 'seq', [(source, source ^ step) for source in range(...]
    pallas_call x1, Pallas kernels: 1.18 us -> 1.56 us  [per_device(): call(functools.partial(own_kernel, tiles, slots, heads, tile_total), [SME...]
  transfers between devices with their start and end apart: 11 -> 11, of which waited for: 6 -> 8; matrix products, arithmetic and copies ran while one was open for 2% -> 2% of each run, Pallas kernels for 10% -> 12%
where the time goes in v1:
time: 33.1 us; the launch traced here: 32.9 us
  starting transfers between devices  11.3 us (34%)
  waiting for transfers between devices  9.42 us (28%)
  Pallas kernels  8.93 us (27%)
  local copies, waits for them, and re-layouts  1.65 us (5%)
  between operations  0.8 us (2%)
  other arithmetic  0.77 us (2%)
    ppermute x9, waiting for transfers between devices, swap(): lax.ppermute(values, 'seq', [(source, source ^ step) for source in range(...  9.42 us
    ppermute x9, starting transfers between devices, swap(): lax.ppermute(values, 'seq', [(source, source ^ step) for source in range(...  7.43 us
    ppermute x2, starting transfers between devices, trade(): got.append(lax.ppermute(full, 'seq', routes))  3.85 us
    pallas_call x1, Pallas kernels, per_device(): call(functools.partial(rest_kernel, tiles, slots, heads, tile_total), [SM...  2.48 us
    pallas_call x1, Pallas kernels, per_device(): call(functools.partial(list_kernel, tile_total, tiles, slots), [SMEM_SPEC...  2.3 us
    pallas_call x1, Pallas kernels, per_device(): call(functools.partial(gathered_kernel, chips, tiles, slots, heads, tile_...  2.02 us
    unnamed x14, local copies, waits for them, and re-layouts  1.65 us
    pallas_call x1, Pallas kernels, per_device(): call(functools.partial(own_kernel, tiles, slots, heads, tile_total), [SME...  1.56 us
  transfers between devices with their start and end apart: 11, of which 8 were waited for; matrix products, arithmetic and copies ran while one was open for 2% of the time, Pallas kernels for 12%

profile of v1, /device:TPU:0, one launch (start us, length us, event | category | flops | bytes accessed | tf_op | source)
XLA Modules:
  0.0 32.9 jit_solution(14009750216249490489)
XLA Ops:
  0.6 0.5 %collective-permute-start.10 = (bf16[256,128]{1,0:T(8,128)(2,1)}, bf16[256,128]{1,0:T(8,128)(2,1)S(1)}, u32[]{:S(2)}, u32[]{:S(2)}) collective-permute-start(bf16[256,128]{1,0:T(8,128)(2,1)} %value_ref.5), channel_id=1, source_target_pairs={{0,4},{4,0},{8,12},{12,8},{16,20},{20,16},{24,28},{28,24},{1,5},{5... | collective-permute-start | bytes 196616 | tf_op jit(solution)/shard_map/ppermute | solution.py:535
  1.2 0.1 collective-permute-start.9
  1.2 0.7 %pad_add_fusion.table_ref.table_any = s32[17,16]{1,0:T(8,128)S(1)} fusion(s32[1,16]{1,0:T(1,128)} %bitcast.35, s32[16,16]{1,0:T(8,128)} %param.15), kind=kLoop, calls=%fused_computation.11 | loop fusion | flops 272 | bytes 2176 | tf_op jit(solution)/shard_map/add | solution.py:554
  2.0 0.3 collective-permute-done.10.refs_3_.value_other
  2.3 0.4 %collective-permute-done.9.refs_2_.key_other = bf16[256,128]{1,0:T(8,128)(2,1)S(1)} collective-permute-done((bf16[256,128]{1,0:T(8,128)(2,1)}, bf16[256,128]{1,0:T(8,128)(2,1)S(1)}, u32[]{:S(2)}, u32[]{:S(2)}) %collective-permute-start.9) | collective-permute-done | bytes 65568 | tf_op jit(solution)/shard_map/ppermute | solution.py:535
  2.6 2.3 %shard_map.93 = (s32[42]{0:T(128)S(1)}, bf16[4,128,128]{2,1,0:T(8,128)(2,1)S(1)}, bf16[2,128,128]{2,1,0:T(8,128)(2,1)S(1)}, bf16[7,2,2,128,128]{4,3,2,1,0:T(8,128)(2,1)}) custom-call(s32[17,16]{1,0:T(8,128)S(1)} %pad_add_fusion.table_ref.table_any, bf16[256,128]{1,0:T(8,128)(2,1)} %key_ref.5, bf16[256,128]{1,0:T(8,128)(2,1)} %value_ref.5, ...), custom_call_target="tpu_custom_call" | custom-call | bytes 4194304 | tf_op jit(solution)/shard_map/pallas_call | solution.py:557
  4.9 2.8 %collective-permute-start.11 = (bf16[4,128,128]{2,1,0:T(8,128)(2,1)S(1)}, bf16[4,128,128]{2,1,0:T(8,128)(2,1)S(1)}, u32[]{:S(2)}, u32[]{:S(2)}) collective-permute-start(bf16[4,128,128]{2,1,0:T(8,128)(2,1)S(1)} %get-tuple-element.333), channel_id=1, source_target_pairs={{0,8},{4,20},{8,0},{12,28},{16,24},{20,4},{24,16},{28,12},{1,9},{5... | collective-permute-start | bytes 393224 | tf_op jit(solution)/shard_map/ppermute | solution.py:544
  7.7 2.5 %collective-permute-start.12 = (bf16[2,128,128]{2,1,0:T(8,128)(2,1)S(1)}, bf16[2,128,128]{2,1,0:T(8,128)(2,1)S(1)}, u32[]{:S(2)}, u32[]{:S(2)}) collective-permute-start(bf16[2,128,128]{2,1,0:T(8,128)(2,1)S(1)} %get-tuple-element.334), channel_id=1, source_target_pairs={{0,24},{4,28},{8,16},{12,20},{16,8},{20,12},{24,0},{28,4},{1,25},{... | collective-permute-start | bytes 196616 | tf_op jit(solution)/shard_map/ppermute | solution.py:535
  10.2 0.9 %copy-done.1 = bf16[256,512]{1,0:T(8,128)(2,1)S(1)} copy-done((bf16[256,512]{1,0:T(8,128)(2,1)S(1)}, bf16[256,512]{1,0:T(8,128)(2,1)}, u32[]{:S(2)}) %copy-start.1) | copy-done | bytes 262168
  11.2 1.6 %shard_map.94 = (f32[1,1024]{1,0:T(1,128)S(1)}, f32[1,1024]{1,0:T(1,128)S(1)}, f32[128,1024]{1,0:T(8,128)S(1)}, bf16[128,1024]{1,0:T(8,128)(2,1)S(1)}) custom-call(s32[42]{0:T(128)S(1)} %get-tuple-element.519.info_ref, bf16[256,512]{1,0:T(8,128)(2,1)S(1)} %copy-done, bf16[256,512]{1,0:T(8,128)(2,1)S(1)} %copy-done.1, bf16[256,128]{1,0:T(8,128)(2,1)} %key_ref.5, ...), custom_call_target="tpu_custom_call" | custom-call | flops 1610612736 | bytes 524288 | tf_op jit(solution)/shard_map/pallas_call | solution.py:600
  12.8 2.5 %collective-permute-done.12.refs_1_ = bf16[2,128,128]{2,1,0:T(8,128)(2,1)S(1)} collective-permute-done((bf16[2,128,128]{2,1,0:T(8,128)(2,1)S(1)}, bf16[2,128,128]{2,1,0:T(8,128)(2,1)S(1)}, u32[]{:S(2)}, u32[]{:S(2)}) %collective-permute-start.12) | collective-permute-done | bytes 65568 | tf_op jit(solution)/shard_map/ppermute | solution.py:535
  15.3 0.0 collective-permute-done.11.refs_0_
  15.3 0.5 %collective-permute-start.13 = (bf16[4,128,128]{2,1,0:T(8,128)(2,1)S(1)}, bf16[4,128,128]{2,1,0:T(8,128)(2,1)S(1)}, u32[]{:S(2)}, u32[]{:S(2)}) collective-permute-start(bf16[4,128,128]{2,1,0:T(8,128)(2,1)S(1)} %collective-permute-done.11.refs_0_), channel_id=1, source_target_pairs={{0,4},{4,0},{8,12},{12,8},{16,20},{20,16},{24,28},{28,24},{1,5},{5... | collective-permute-start | bytes 393224 | tf_op jit(solution)/shard_map/ppermute | solution.py:535
  15.8 0.7 %collective-permute-done.14.refs_3_ = bf16[2,128,128]{2,1,0:T(8,128)(2,1)S(1)} collective-permute-done((bf16[2,128,128]{2,1,0:T(8,128)(2,1)S(1)}, bf16[2,128,128]{2,1,0:T(8,128)(2,1)S(1)}, u32[]{:S(2)}, u32[]{:S(2)}) %collective-permute-start.14) | collective-permute-done | bytes 65568 | tf_op jit(solution)/shard_map/ppermute | solution.py:535
  16.5 0.2 collective-permute-done.13.refs_2_
  16.8 2.0 %shard_map.95 = (bf16[4,128,128]{2,1,0:T(8,128)(2,1)S(1)}, f32[1,1024]{1,0:T(1,128)S(1)}, f32[1,1024]{1,0:T(1,128)S(1)}, f32[1,1024]{1,0:T(1,128)S(1)}, bf16[128...) custom-call(s32[42]{0:T(128)S(1)} %get-tuple-element.591, ...), custom_call_target="tpu_custom_call" | custom-call | flops 1610612736 | bytes 524288 | tf_op jit(solution)/shard_map/pallas_call | solution.py:616
  18.8 0.0 copy-start.2
  18.8 0.4 %collective-permute-start.15 = (bf16[4,128,128]{2,1,0:T(8,128)(2,1)S(1)}, bf16[4,128,128]{2,1,0:T(8,128)(2,1)S(1)}, u32[]{:S(2)}, u32[]{:S(2)}) collective-permute-start(bf16[4,128,128]{2,1,0:T(8,128)(2,1)S(1)} %get-tuple-element.345), channel_id=1, source_target_pairs={{0,4},{4,0},{8,12},{12,8},{16,20},{20,16},{24,28},{28,24},{1,5},{5... | collective-permute-start | bytes 393224 | tf_op jit(solution)/shard_map/ppermute | solution.py:535
  19.3 1.0 %collective-permute-done.15 = bf16[4,128,128]{2,1,0:T(8,128)(2,1)S(1)} collective-permute-done((bf16[4,128,128]{2,1,0:T(8,128)(2,1)S(1)}, bf16[4,128,128]{2,1,0:T(8,128)(2,1)S(1)}, u32[]{:S(2)}, u32[]{:S(2)}) %collective-permute-start.15) | collective-permute-done | bytes 131104 | tf_op jit(solution)/shard_map/ppermute | solution.py:535
  20.3 1.1 %collective-permute-start.16 = (bf16[4,128,128]{2,1,0:T(8,128)(2,1)S(1)}, bf16[4,128,128]{2,1,0:T(8,128)(2,1)S(1)}, u32[]{:S(2)}, u32[]{:S(2)}) collective-permute-start(bf16[4,128,128]{2,1,0:T(8,128)(2,1)S(1)} %pad_maximum_fusion.refs_2_), channel_id=1, source_target_pairs={{0,8},{4,20},{8,0},{12,28},{16,24},{20,4},{24,16},{28,12},{1,9},{5... | collective-permute-start | bytes 393224 | tf_op jit(solution)/shard_map/ppermute | solution.py:544
  21.4 2.5 %shard_map.96 = (bf16[256,512]{1,0:T(8,128)(2,1)}, f32[256,512]{1,0:T(8,128)}, f32[256,128]{1,0:T(8,128)S(1)}, f32[256,128]{1,0:T(8,128)S(1)}, bf16[2,128,128]{2,1,0:T(8,128)(2,1)S(1)}) custom-call(s32[42]{0:T(128)S(1)} %get-tuple-element.591, bf16[256,512]{1,0:T(8,128)(2,1)S(1)} %copy-done, ...), custom_call_target="tpu_custom_call", output_to_operand_aliasing={{4}: (15, {})} | custom-call | flops 2147483648 | bytes 1048576 | tf_op jit(solution)/shard_map/pallas_call | solution.py:662
  23.9 3.1 %collective-permute-start.17 = (bf16[2,128,128]{2,1,0:T(8,128)(2,1)S(1)}, bf16[2,128,128]{2,1,0:T(8,128)(2,1)S(1)}, u32[]{:S(2)}, u32[]{:S(2)}) collective-permute-start(bf16[2,128,128]{2,1,0:T(8,128)(2,1)S(1)} %get-tuple-element.350), channel_id=1, source_target_pairs={{0,24},{4,28},{8,16},{12,20},{16,8},{20,12},{24,0},{28,4},{1,25},{... | collective-permute-start | bytes 196616 | tf_op jit(solution)/shard_map/ppermute | solution.py:535
  27.0 0.0 collective-permute-done.16.refs_3_
  27.0 0.0 collective-permute-start.18
  27.0 3.3 %collective-permute-done.17.refs_4_ = bf16[2,128,128]{2,1,0:T(8,128)(2,1)S(1)} collective-permute-done((bf16[2,128,128]{2,1,0:T(8,128)(2,1)S(1)}, bf16[2,128,128]{2,1,0:T(8,128)(2,1)S(1)}, u32[]{:S(2)}, u32[]{:S(2)}) %collective-permute-start.17) | collective-permute-done | bytes 65568 | tf_op jit(solution)/shard_map/ppermute | solution.py:535
  30.3 0.3 collective-permute-start.19
  30.6 1.0 %collective-permute-done.19.refs_6_ = bf16[2,128,128]{2,1,0:T(8,128)(2,1)S(1)} collective-permute-done((bf16[2,128,128]{2,1,0:T(8,128)(2,1)S(1)}, bf16[2,128,128]{2,1,0:T(8,128)(2,1)S(1)}, u32[]{:S(2)}, u32[]{:S(2)}) %collective-permute-start.19) | collective-permute-done | bytes 65568 | tf_op jit(solution)/shard_map/ppermute | solution.py:535
  31.6 0.6 %shard_map.97 = (f32[256,128]{1,0:T(8,128)S(1)}, f32[256,128]{1,0:T(8,128)S(1)}) custom-call(s32[42]{0:T(128)S(1)} %get-tuple-element.591, f32[256,128]{1,0:T(8,128)S(1)} %get-tuple-element.348.refs_0_, f32[256,128]{1,0:T(8,128)S(1)} %get-tuple-element.349.refs_1_, bf16[4,128,128]{2,1,0:T(8,128)(2,1)S(1)} %pad_maximum_fusion.refs_2_, ...), custom_call_target="tpu_custom_call" | custom-call | bytes 655360 | tf_op jit(solution)/shard_map/pallas_call | solution.py:690
  32.2 0.0 copy-start.3
  32.2 0.0 copy-start.4
  32.2 0.6 %copy-done.3 = f32[256,128]{1,0:T(8,128)} copy-done((f32[256,128]{1,0:T(8,128)}, f32[256,128]{1,0:T(8,128)S(1)}, u32[]{:S(2)}) %copy-start.3) | copy-done | bytes 131096
  32.8 0.0 copy-done.4
  (14 shorter events, 0.1 us)
Async XLA Ops:
  0.6 9.6 %copy-start = (bf16[256,512]{1,0:T(8,128)(2,1)S(1)}, bf16[256,512]{1,0:T(8,128)(2,1)}, u32[]{:S(2)}) copy-start(bf16[256,512]{1,0:T(8,128)(2,1)} %query_ref.5) | copy-start | bytes 786436
  0.6 1.6 %collective-permute-start.10 = (bf16[256,128]{1,0:T(8,128)(2,1)}, bf16[256,128]{1,0:T(8,128)(2,1)S(1)}, u32[]{:S(2)}, u32[]{:S(2)}) collective-permute-start(bf16[256,128]{1,0:T(8,128)(2,1)} %value_ref.5), channel_id=1, source_target_pairs={{0,4},{4,0},{8,12},{12,8},{16,20},{20,16},{24,28},{28,24},{1,5},{5... | collective-permute-start | bytes 196616 | tf_op jit(solution)/shard_map/ppermute | solution.py:535
  1.2 1.5 %collective-permute-start.9 = (bf16[256,128]{1,0:T(8,128)(2,1)}, bf16[256,128]{1,0:T(8,128)(2,1)S(1)}, u32[]{:S(2)}, u32[]{:S(2)}) collective-permute-start(bf16[256,128]{1,0:T(8,128)(2,1)} %key_ref.5), channel_id=1, source_target_pairs={{0,4},{4,0},{8,12},{12,8},{16,20},{20,16},{24,28},{28,24},{1,5},{5... | collective-permute-start | bytes 196616 | tf_op jit(solution)/shard_map/ppermute | solution.py:535
  4.9 10.4 %collective-permute-start.11 = (bf16[4,128,128]{2,1,0:T(8,128)(2,1)S(1)}, bf16[4,128,128]{2,1,0:T(8,128)(2,1)S(1)}, u32[]{:S(2)}, u32[]{:S(2)}) collective-permute-start(bf16[4,128,128]{2,1,0:T(8,128)(2,1)S(1)} %get-tuple-element.333), channel_id=1, source_target_pairs={{0,8},{4,20},{8,0},{12,28},{16,24},{20,4},{24,16},{28,12},{1,9},{5... | collective-permute-start | bytes 393224 | tf_op jit(solution)/shard_map/ppermute | solution.py:544
  7.7 7.6 %collective-permute-start.12 = (bf16[2,128,128]{2,1,0:T(8,128)(2,1)S(1)}, bf16[2,128,128]{2,1,0:T(8,128)(2,1)S(1)}, u32[]{:S(2)}, u32[]{:S(2)}) collective-permute-start(bf16[2,128,128]{2,1,0:T(8,128)(2,1)S(1)} %get-tuple-element.334), channel_id=1, source_target_pairs={{0,24},{4,28},{8,16},{12,20},{16,8},{20,12},{24,0},{28,4},{1,25},{... | collective-permute-start | bytes 196616 | tf_op jit(solution)/shard_map/ppermute | solution.py:535
  10.2 1.0 %copy-start.1 = (bf16[256,512]{1,0:T(8,128)(2,1)S(1)}, bf16[256,512]{1,0:T(8,128)(2,1)}, u32[]{:S(2)}) copy-start(bf16[256,512]{1,0:T(8,128)(2,1)} %grad_ref.5) | copy-start | bytes 786436
  11.2 4.6 %copy-start.5 = (bf16[256,128]{1,0:T(8,128)(2,1)S(1)}, bf16[256,128]{1,0:T(8,128)(2,1)}, u32[]{:S(2)}) copy-start(bf16[256,128]{1,0:T(8,128)(2,1)} %key_ref.5) | copy-start | bytes 196612
  11.2 4.6 %copy-start.6 = (bf16[256,128]{1,0:T(8,128)(2,1)S(1)}, bf16[256,128]{1,0:T(8,128)(2,1)}, u32[]{:S(2)}) copy-start(bf16[256,128]{1,0:T(8,128)(2,1)} %value_ref.5) | copy-start | bytes 196612
  15.3 1.3 %collective-permute-start.14 = (bf16[2,128,128]{2,1,0:T(8,128)(2,1)S(1)}, bf16[2,128,128]{2,1,0:T(8,128)(2,1)S(1)}, u32[]{:S(2)}, u32[]{:S(2)}) collective-permute-start(bf16[2,128,128]{2,1,0:T(8,128)(2,1)S(1)} %collective-permute-done.12.refs_1_), channel_id=1, source_target_pairs={{0,4},{4,0},{8,12},{12,8},{16,20},{20,16},{24,28},{28,24},{1,5},{5... | collective-permute-start | bytes 196616 | tf_op jit(solution)/shard_map/ppermute | solution.py:535
  15.3 1.5 %collective-permute-start.13 = (bf16[4,128,128]{2,1,0:T(8,128)(2,1)S(1)}, bf16[4,128,128]{2,1,0:T(8,128)(2,1)S(1)}, u32[]{:S(2)}, u32[]{:S(2)}) collective-permute-start(bf16[4,128,128]{2,1,0:T(8,128)(2,1)S(1)} %collective-permute-done.11.refs_0_), channel_id=1, source_target_pairs={{0,4},{4,0},{8,12},{12,8},{16,20},{20,16},{24,28},{28,24},{1,5},{5... | collective-permute-start | bytes 393224 | tf_op jit(solution)/shard_map/ppermute | solution.py:535
  18.8 2.5 %copy-start.2 = (bf16[256,512]{1,0:T(8,128)(2,1)S(1)}, bf16[256,512]{1,0:T(8,128)(2,1)}, u32[]{:S(2)}) copy-start(bf16[256,512]{1,0:T(8,128)(2,1)} %grad_ref.5) | copy-start | bytes 786436
  18.8 1.4 %collective-permute-start.15 = (bf16[4,128,128]{2,1,0:T(8,128)(2,1)S(1)}, bf16[4,128,128]{2,1,0:T(8,128)(2,1)S(1)}, u32[]{:S(2)}, u32[]{:S(2)}) collective-permute-start(bf16[4,128,128]{2,1,0:T(8,128)(2,1)S(1)} %get-tuple-element.345), channel_id=1, source_target_pairs={{0,4},{4,0},{8,12},{12,8},{16,20},{20,16},{24,28},{28,24},{1,5},{5... | collective-permute-start | bytes 393224 | tf_op jit(solution)/shard_map/ppermute | solution.py:535
  20.3 6.7 %collective-permute-start.16 = (bf16[4,128,128]{2,1,0:T(8,128)(2,1)S(1)}, bf16[4,128,128]{2,1,0:T(8,128)(2,1)S(1)}, u32[]{:S(2)}, u32[]{:S(2)}) collective-permute-start(bf16[4,128,128]{2,1,0:T(8,128)(2,1)S(1)} %pad_maximum_fusion.refs_2_), channel_id=1, source_target_pairs={{0,8},{4,20},{8,0},{12,28},{16,24},{20,4},{24,16},{28,12},{1,9},{5... | collective-permute-start | bytes 393224 | tf_op jit(solution)/shard_map/ppermute | solution.py:544
  23.9 6.5 %collective-permute-start.17 = (bf16[2,128,128]{2,1,0:T(8,128)(2,1)S(1)}, bf16[2,128,128]{2,1,0:T(8,128)(2,1)S(1)}, u32[]{:S(2)}, u32[]{:S(2)}) collective-permute-start(bf16[2,128,128]{2,1,0:T(8,128)(2,1)S(1)} %get-tuple-element.350), channel_id=1, source_target_pairs={{0,24},{4,28},{8,16},{12,20},{16,8},{20,12},{24,0},{28,4},{1,25},{... | collective-permute-start | bytes 196616 | tf_op jit(solution)/shard_map/ppermute | solution.py:535
  27.0 4.6 %collective-permute-start.18 = (bf16[4,128,128]{2,1,0:T(8,128)(2,1)S(1)}, bf16[4,128,128]{2,1,0:T(8,128)(2,1)S(1)}, u32[]{:S(2)}, u32[]{:S(2)}) collective-permute-start(bf16[4,128,128]{2,1,0:T(8,128)(2,1)S(1)} %collective-permute-done.16.refs_3_), channel_id=1, source_target_pairs={{0,4},{4,0},{8,12},{12,8},{16,20},{20,16},{24,28},{28,24},{1,5},{5... | collective-permute-start | bytes 393224 | tf_op jit(solution)/shard_map/ppermute | solution.py:535
  30.3 1.3 %collective-permute-start.19 = (bf16[2,128,128]{2,1,0:T(8,128)(2,1)S(1)}, bf16[2,128,128]{2,1,0:T(8,128)(2,1)S(1)}, u32[]{:S(2)}, u32[]{:S(2)}) collective-permute-start(bf16[2,128,128]{2,1,0:T(8,128)(2,1)S(1)} %collective-permute-done.17.refs_4_), channel_id=1, source_target_pairs={{0,4},{4,0},{8,12},{12,8},{16,20},{20,16},{24,28},{28,24},{1,5},{5... | collective-permute-start | bytes 196616 | tf_op jit(solution)/shard_map/ppermute | solution.py:535
  32.2 0.7 %copy-start.3 = (f32[256,128]{1,0:T(8,128)}, f32[256,128]{1,0:T(8,128)S(1)}, u32[]{:S(2)}) copy-start(f32[256,128]{1,0:T(8,128)S(1)} %get-tuple-element.324) | copy-start | bytes 393220
  32.2 0.7 %copy-start.4 = (f32[256,128]{1,0:T(8,128)}, f32[256,128]{1,0:T(8,128)S(1)}, u32[]{:S(2)}) copy-start(f32[256,128]{1,0:T(8,128)S(1)} %get-tuple-element.325) | copy-start | bytes 393220

commit v2 on v1

--- a/solution.py
+++ b/solution.py
@@ -453,7 +453,14 @@
         repack(parts_ref.at[pl.ds(part * slots, slots)], part, 0)
 
 
-def rest_kernel(
+def fetch_full(copy_sem, *pairs):
+    for source, target in pairs:
+        copy = pltpu.make_async_copy(source, target, copy_sem)
+        copy.start()
+        copy.wait()
+
+
+def own_grads_kernel(
     tiles,
     slots,
     heads,
@@ -466,16 +473,10 @@
     max_ref,
     inverse_ref,
     delta_ref,
-    out_t_ref,
-    dscores_ref,
-    slot_keys,
-    attended_full,
-    query_full,
     key_full,
     value_full,
     order_ref,
-    attended_ref,
-    query_out,
+    dscores_ref,
     key_out,
     value_out,
     order_out,
@@ -483,21 +484,49 @@
     copy_sem,
 ):
     del order_ref, order_out
-    factor = HD**-0.5
-    rows = tiles * TILE
 
     @pl.when(info_ref[0] <= slots)
     def _():
-        keys = key_ref[...]
         query = stacked(query_ref, heads)
         grad = stacked(grad_ref, heads)
-        scores = own_scores(tiles, slots, heads, tile_total, info_ref, bias_ref, keys, query)
+        scores = own_scores(
+            tiles, slots, heads, tile_total, info_ref, bias_ref, key_ref[...], query
+        )
         probs = jnp.exp2(scores - max_ref[...]) * inverse_ref[...]
         dprobs = dot_t(value_ref[...], grad)
         dscores = (probs * (dprobs - delta_ref[...])).astype(jnp.bfloat16)
+        dscores_ref[...] = dscores
         value_out[...] = dot(probs.astype(jnp.bfloat16), grad)
-        key_out[...] = dot(dscores, query) * factor
-        query_t = (dot(keys.T, dscores) + dot(slot_keys[...].T, dscores_ref[...])) * factor
+        key_out[...] = dot(dscores, query) * HD**-0.5
+
+    @pl.when(info_ref[0] > slots)
+    def _():
+        fetch_full(copy_sem, (key_full, key_out), (value_full, value_out))
+
+
+def queries_kernel(
+    slots,
+    heads,
+    info_ref,
+    key_ref,
+    own_dscores,
+    slot_dscores,
+    slot_keys,
+    out_t_ref,
+    attended_full,
+    query_full,
+    order_ref,
+    attended_ref,
+    query_out,
+    copy_sem,
+):
+    del order_ref
+    rows = query_out.shape[0]
+
+    @pl.when(info_ref[0] <= slots)
+    def _():
+        query_t = dot(key_ref[...].T, own_dscores[...])
+        query_t = (query_t + dot(slot_keys[...].T, slot_dscores[...])) * HD**-0.5
         for h in range(heads):
             columns = pl.ds(h * HD, HD)
             attended_ref[:, columns] = out_t_ref[:, pl.ds(h * rows, rows)].T
@@ -505,15 +534,7 @@
 
     @pl.when(info_ref[0] > slots)
     def _():
-        for source, target in (
-            (attended_full, attended_ref),
-            (query_full, query_out),
-            (key_full, key_out),
-            (value_full, value_out),
-        ):
-            copy = pltpu.make_async_copy(source, target, copy_sem)
-            copy.start()
-            copy.wait()
+        fetch_full(copy_sem, (attended_full, attended_ref), (query_full, query_out))
 
 
 def per_device(queries, key_rows, value_rows, out_grad, tile_ids, tile_mask):
@@ -659,15 +680,15 @@
     partner = swap(parts, 1)
     half_sum = add(parts[:slots], partner[slots:])
     chip_sum = jnp.concatenate([half_sum, add(parts[slots:], partner[:slots])])
-    attended, query_grad, key_own, value_own, half_sum = call(
-        functools.partial(rest_kernel, tiles, slots, heads, tile_total),
-        [SMEM_SPEC] + [VMEM_SPEC] * 10 + [ANY_SPEC] * 5,
-        full + (shape(slot_shape, bf16),),
-        (VMEM_SPEC,) * 4 + (ANY_SPEC,),
+    own_dscores, key_own, value_own, half_sum = call(
+        functools.partial(own_grads_kernel, tiles, slots, heads, tile_total),
+        [SMEM_SPEC] + [VMEM_SPEC] * 7 + [ANY_SPEC] * 3,
+        (shape((row_count, columns), bf16), *full[2:], shape(slot_shape, bf16)),
+        (VMEM_SPEC,) * 3 + (ANY_SPEC,),
         scratch=(pltpu.VMEM((row_count, row_count), f32), pltpu.SemaphoreType.DMA),
-        flops=32 * work,
-        moved=8 * row_count * heads * HD,
-        aliases={15: 4},
+        flops=18 * work,
+        moved=4 * row_count * heads * HD,
+        aliases={10: 3},
     )(
         info,
         queries,
@@ -677,13 +698,19 @@
         row_max,
         inverse,
         delta,
-        out_t,
-        dscores,
-        slot_keys,
-        *full_values,
+        *full_values[2:],
         half_sum,
     )
     back = trade(chip_sum, half_sum)
+    attended, query_grad = call(
+        functools.partial(queries_kernel, slots, heads),
+        [SMEM_SPEC] + [VMEM_SPEC] * 5 + [ANY_SPEC] * 3,
+        full[:2],
+        (VMEM_SPEC,) * 2,
+        scratch=(pltpu.SemaphoreType.DMA,),
+        flops=16 * work,
+        moved=8 * row_count * heads * HD,
+    )(info, key_rows, own_dscores, dscores, slot_keys, out_t, *full_values[:2], back[0])
     sums = [chip_sum] + back + [swap(values, 1) for values in back]
 
     def close(kernel, lead, grads, sums):

time: 33.1 us -> 33.4 us (level)
  waiting for transfers between devices: 9.42 us -> 7.24 us
  starting transfers between devices: 11.3 us -> 12.5 us
  Pallas kernels: 8.93 us -> 10.1 us
    ppermute x9, waiting for transfers between devices: 9.42 us -> 7.24 us  [swap(): lax.ppermute(values, 'seq', [(source, source ^ step) for source in range(...]
    ppermute x9, starting transfers between devices: 7.43 us -> 8.65 us  [swap(): lax.ppermute(values, 'seq', [(source, source ^ step) for source in range(...]
    pallas_call x1 -> x2, Pallas kernels: 2.48 us -> 3.22 us  [the longest x1 1.9 us: per_device(): call(functools.partial(queries_kernel, slots, heads), [SMEM_SPEC] + [VMEM...]
    pallas_call x1, Pallas kernels: 2.02 us -> 2.38 us  [per_device(): call(functools.partial(gathered_kernel, chips, tiles, slots, heads, tile_...]
    unnamed x14 -> x20, local copies, waits for them, and re-layouts: 1.65 us -> 1.67 us
  transfers between devices with their start and end apart: 11 -> 11, of which waited for: 8 -> 7; matrix products, arithmetic and copies ran while one was open for 2% -> 2% of each run, Pallas kernels for 12% -> 14%
where the time goes in v2:
time: 33.4 us; the launch traced here: 33.1 us
  starting transfers between devices  12.5 us (37%)
  Pallas kernels  10.1 us (30%)
  waiting for transfers between devices  7.24 us (22%)
  local copies, waits for them, and re-layouts  1.67 us (5%)
  between operations  0.84 us (3%)
  other arithmetic  0.77 us (2%)
    ppermute x9, starting transfers between devices, swap(): lax.ppermute(values, 'seq', [(source, source ^ step) for source in range(...  8.65 us
    ppermute x9, waiting for transfers between devices, swap(): lax.ppermute(values, 'seq', [(source, source ^ step) for source in range(...  7.24 us
    ppermute x2, starting transfers between devices, trade(): got.append(lax.ppermute(full, 'seq', routes))  3.84 us
    pallas_call x1, Pallas kernels, per_device(): call(functools.partial(gathered_kernel, chips, tiles, slots, heads, tile_...  2.38 us
    pallas_call x1, Pallas kernels, per_device(): call(functools.partial(list_kernel, tile_total, tiles, slots), [SMEM_SPEC...  2.3 us
    pallas_call x1, Pallas kernels, per_device(): call(functools.partial(queries_kernel, slots, heads), [SMEM_SPEC] + [VMEM...  1.9 us
    unnamed x20, local copies, waits for them, and re-layouts  1.67 us
    pallas_call x1, Pallas kernels, per_device(): call(functools.partial(own_kernel, tiles, slots, heads, tile_total), [SME...  1.55 us
  transfers between devices with their start and end apart: 11, of which 7 were waited for; matrix products, arithmetic and copies ran while one was open for 2% of the time, Pallas kernels for 14%

profile of v2, /device:TPU:0, one launch (start us, length us, event | category | flops | bytes accessed | tf_op | source)
XLA Modules:
  0.0 33.1 jit_solution(15081567527899809204)
XLA Ops:
  0.6 0.5 %collective-permute-start.10 = (bf16[256,128]{1,0:T(8,128)(2,1)}, bf16[256,128]{1,0:T(8,128)(2,1)S(1)}, u32[]{:S(2)}, u32[]{:S(2)}) collective-permute-start(bf16[256,128]{1,0:T(8,128)(2,1)} %value_ref.5), channel_id=1, source_target_pairs={{0,4},{4,0},{8,12},{12,8},{16,20},{20,16},{24,28},{28,24},{1,5},{5... | collective-permute-start | bytes 196616 | tf_op jit(solution)/shard_map/ppermute | solution.py:556
  1.2 0.1 collective-permute-start.9
  1.2 0.7 %pad_add_fusion.table_ref.table_any = s32[17,16]{1,0:T(8,128)S(1)} fusion(s32[1,16]{1,0:T(1,128)} %bitcast.35, s32[16,16]{1,0:T(8,128)} %param.15), kind=kLoop, calls=%fused_computation.11 | loop fusion | flops 272 | bytes 2176 | tf_op jit(solution)/shard_map/add | solution.py:575
  2.0 0.3 collective-permute-done.10.refs_3_.value_other
  2.3 0.4 %collective-permute-done.9.refs_2_.key_other = bf16[256,128]{1,0:T(8,128)(2,1)S(1)} collective-permute-done((bf16[256,128]{1,0:T(8,128)(2,1)}, bf16[256,128]{1,0:T(8,128)(2,1)S(1)}, u32[]{:S(2)}, u32[]{:S(2)}) %collective-permute-start.9) | collective-permute-done | bytes 65568 | tf_op jit(solution)/shard_map/ppermute | solution.py:556
  2.6 2.3 %shard_map.93 = (s32[42]{0:T(128)S(1)}, bf16[4,128,128]{2,1,0:T(8,128)(2,1)S(1)}, bf16[2,128,128]{2,1,0:T(8,128)(2,1)S(1)}, bf16[7,2,2,128,128]{4,3,2,1,0:T(8,128)(2,1)}) custom-call(s32[17,16]{1,0:T(8,128)S(1)} %pad_add_fusion.table_ref.table_any, bf16[256,128]{1,0:T(8,128)(2,1)} %key_ref.7, bf16[256,128]{1,0:T(8,128)(2,1)} %value_ref.5, ...), custom_call_target="tpu_custom_call" | custom-call | bytes 4194304 | tf_op jit(solution)/shard_map/pallas_call | solution.py:578
  4.9 2.8 %collective-permute-start.11 = (bf16[4,128,128]{2,1,0:T(8,128)(2,1)S(1)}, bf16[4,128,128]{2,1,0:T(8,128)(2,1)S(1)}, u32[]{:S(2)}, u32[]{:S(2)}) collective-permute-start(bf16[4,128,128]{2,1,0:T(8,128)(2,1)S(1)} %get-tuple-element.334), channel_id=1, source_target_pairs={{0,8},{4,20},{8,0},{12,28},{16,24},{20,4},{24,16},{28,12},{1,9},{5... | collective-permute-start | bytes 393224 | tf_op jit(solution)/shard_map/ppermute | solution.py:565
  7.7 2.5 %collective-permute-start.12 = (bf16[2,128,128]{2,1,0:T(8,128)(2,1)S(1)}, bf16[2,128,128]{2,1,0:T(8,128)(2,1)S(1)}, u32[]{:S(2)}, u32[]{:S(2)}) collective-permute-start(bf16[2,128,128]{2,1,0:T(8,128)(2,1)S(1)} %get-tuple-element.335), channel_id=1, source_target_pairs={{0,24},{4,28},{8,16},{12,20},{16,8},{20,12},{24,0},{28,4},{1,25},{... | collective-permute-start | bytes 196616 | tf_op jit(solution)/shard_map/ppermute | solution.py:556
  10.2 0.9 %copy-done.1 = bf16[256,512]{1,0:T(8,128)(2,1)S(1)} copy-done((bf16[256,512]{1,0:T(8,128)(2,1)S(1)}, bf16[256,512]{1,0:T(8,128)(2,1)}, u32[]{:S(2)}) %copy-start.1) | copy-done | bytes 262168
  11.2 1.6 %shard_map.94 = (f32[1,1024]{1,0:T(1,128)S(1)}, f32[1,1024]{1,0:T(1,128)S(1)}, f32[128,1024]{1,0:T(8,128)S(1)}, bf16[128,1024]{1,0:T(8,128)(2,1)S(1)}) custom-call(s32[42]{0:T(128)S(1)} %get-tuple-element.521.info_ref, bf16[256,512]{1,0:T(8,128)(2,1)S(1)} %copy-done, bf16[256,512]{1,0:T(8,128)(2,1)S(1)} %copy-done.1, bf16[256,128]{1,0:T(8,128)(2,1)} %key_ref.7, ...), custom_call_target="tpu_custom_call" | custom-call | flops 1610612736 | bytes 524288 | tf_op jit(solution)/shard_map/pallas_call | solution.py:621
  12.8 2.5 %collective-permute-done.12.refs_1_ = bf16[2,128,128]{2,1,0:T(8,128)(2,1)S(1)} collective-permute-done((bf16[2,128,128]{2,1,0:T(8,128)(2,1)S(1)}, bf16[2,128,128]{2,1,0:T(8,128)(2,1)S(1)}, u32[]{:S(2)}, u32[]{:S(2)}) %collective-permute-start.12) | collective-permute-done | bytes 65568 | tf_op jit(solution)/shard_map/ppermute | solution.py:556
  15.3 0.5 %collective-permute-start.13 = (bf16[4,128,128]{2,1,0:T(8,128)(2,1)S(1)}, bf16[4,128,128]{2,1,0:T(8,128)(2,1)S(1)}, u32[]{:S(2)}, u32[]{:S(2)}) collective-permute-start(bf16[4,128,128]{2,1,0:T(8,128)(2,1)S(1)} %collective-permute-done.11.refs_0_), channel_id=1, source_target_pairs={{0,4},{4,0},{8,12},{12,8},{16,20},{20,16},{24,28},{28,24},{1,5},{5... | collective-permute-start | bytes 393224 | tf_op jit(solution)/shard_map/ppermute | solution.py:556
  15.8 0.0 copy-start.9
  15.8 0.7 %collective-permute-done.14.refs_3_ = bf16[2,128,128]{2,1,0:T(8,128)(2,1)S(1)} collective-permute-done((bf16[2,128,128]{2,1,0:T(8,128)(2,1)S(1)}, bf16[2,128,128]{2,1,0:T(8,128)(2,1)S(1)}, u32[]{:S(2)}, u32[]{:S(2)}) %collective-permute-start.14) | collective-permute-done | bytes 65568 | tf_op jit(solution)/shard_map/ppermute | solution.py:556
  16.5 0.2 collective-permute-done.13.refs_2_
  16.8 2.4 %shard_map.95 = (bf16[4,128,128]{2,1,0:T(8,128)(2,1)S(1)}, f32[1,1024]{1,0:T(1,128)S(1)}, f32[1,1024]{1,0:T(1,128)S(1)}, f32[1,1024]{1,0:T(1,128)S(1)}, bf16[128...) custom-call(s32[42]{0:T(128)S(1)} %get-tuple-element.593, ...), custom_call_target="tpu_custom_call" | custom-call | flops 1610612736 | bytes 524288 | tf_op jit(solution)/shard_map/pallas_call | solution.py:637
  19.2 0.4 %collective-permute-start.15 = (bf16[4,128,128]{2,1,0:T(8,128)(2,1)S(1)}, bf16[4,128,128]{2,1,0:T(8,128)(2,1)S(1)}, u32[]{:S(2)}, u32[]{:S(2)}) collective-permute-start(bf16[4,128,128]{2,1,0:T(8,128)(2,1)S(1)} %get-tuple-element.341), channel_id=1, source_target_pairs={{0,4},{4,0},{8,12},{12,8},{16,20},{20,16},{24,28},{28,24},{1,5},{5... | collective-permute-start | bytes 393224 | tf_op jit(solution)/shard_map/ppermute | solution.py:556
  19.6 1.0 %collective-permute-done.15 = bf16[4,128,128]{2,1,0:T(8,128)(2,1)S(1)} collective-permute-done((bf16[4,128,128]{2,1,0:T(8,128)(2,1)S(1)}, bf16[4,128,128]{2,1,0:T(8,128)(2,1)S(1)}, u32[]{:S(2)}, u32[]{:S(2)}) %collective-permute-start.15) | collective-permute-done | bytes 131104 | tf_op jit(solution)/shard_map/ppermute | solution.py:556
  20.6 0.0 copy-start.6
  20.6 0.0 copy-start.8
  20.7 1.0 %collective-permute-start.16 = (bf16[4,128,128]{2,1,0:T(8,128)(2,1)S(1)}, bf16[4,128,128]{2,1,0:T(8,128)(2,1)S(1)}, u32[]{:S(2)}, u32[]{:S(2)}) collective-permute-start(bf16[4,128,128]{2,1,0:T(8,128)(2,1)S(1)} %pad_maximum_fusion.refs_2_), channel_id=1, source_target_pairs={{0,8},{4,20},{8,0},{12,28},{16,24},{20,4},{24,16},{28,12},{1,9},{5... | collective-permute-start | bytes 393224 | tf_op jit(solution)/shard_map/ppermute | solution.py:565
  21.7 1.3 %shard_map.96 = (bf16[256,1024]{1,0:T(8,128)(2,1)S(1)}, f32[256,128]{1,0:T(8,128)S(1)}, f32[256,128]{1,0:T(8,128)S(1)}, bf16[2,128,128]{2,1,0:T(8,128)(2,1)S(1)}) custom-call(s32[42]{0:T(128)S(1)} %get-tuple-element.593, bf16[256,512]{1,0:T(8,128)(2,1)S(1)} %copy-done, bf16[256,512]{1,0:T(8,128)(2,1)S(1)} %copy-done.2, ...), custom_call_target="tpu_custom_call", output_to_operand_aliasing={{3}: (10, {})} | custom-call | flops 1207959552 | bytes 524288 | tf_op jit(solution)/shard_map/pallas_call | solution.py:683
  23.1 3.2 %collective-permute-start.17 = (bf16[2,128,128]{2,1,0:T(8,128)(2,1)S(1)}, bf16[2,128,128]{2,1,0:T(8,128)(2,1)S(1)}, u32[]{:S(2)}, u32[]{:S(2)}) collective-permute-start(bf16[2,128,128]{2,1,0:T(8,128)(2,1)S(1)} %get-tuple-element.352), channel_id=1, source_target_pairs={{0,24},{4,28},{8,16},{12,20},{16,8},{20,12},{24,0},{28,4},{1,25},{... | collective-permute-start | bytes 196616 | tf_op jit(solution)/shard_map/ppermute | solution.py:556
  26.2 1.2 %collective-permute-start.18 = (bf16[4,128,128]{2,1,0:T(8,128)(2,1)S(1)}, bf16[4,128,128]{2,1,0:T(8,128)(2,1)S(1)}, u32[]{:S(2)}, u32[]{:S(2)}) collective-permute-start(bf16[4,128,128]{2,1,0:T(8,128)(2,1)S(1)} %collective-permute-done.16.order_ref.refs_3_), channel_id=1, source_target_pairs={{0,4},{4,0},{8,12},{12,8},{16,20},{20,16},{24,28},{28,24},{1,5},{5... | collective-permute-start | bytes 393224 | tf_op jit(solution)/shard_map/ppermute | solution.py:556
  27.4 2.1 %collective-permute-done.17.refs_4_ = bf16[2,128,128]{2,1,0:T(8,128)(2,1)S(1)} collective-permute-done((bf16[2,128,128]{2,1,0:T(8,128)(2,1)S(1)}, bf16[2,128,128]{2,1,0:T(8,128)(2,1)S(1)}, u32[]{:S(2)}, u32[]{:S(2)}) %collective-permute-start.17) | collective-permute-done | bytes 65568 | tf_op jit(solution)/shard_map/ppermute | solution.py:556
  29.5 0.3 collective-permute-start.19
  29.8 1.9 %shard_map.97 = (bf16[256,512]{1,0:T(8,128)(2,1)}, f32[256,512]{1,0:T(8,128)}) custom-call(s32[42]{0:T(128)S(1)} %get-tuple-element.593, bf16[256,128]{1,0:T(8,128)(2,1)S(1)} %copy-done.8, bf16[256,1024]{1,0:T(8,128)(2,1)S(1)} %get-tuple-element.342.own_dscores, bf16[256,1024]{1,0:T(8,128)(2,1)S(1)} %get-tuple-element.343.slot_dscores, ...), custom_call_target="tpu_custom_call" | custom-call | flops 1073741824 | bytes 1048576 | tf_op jit(solution)/shard_map/pallas_call | solution.py:705
  31.7 0.6 %shard_map.98 = (f32[256,128]{1,0:T(8,128)S(1)}, f32[256,128]{1,0:T(8,128)S(1)}) custom-call(s32[42]{0:T(128)S(1)} %get-tuple-element.593, f32[256,128]{1,0:T(8,128)S(1)} %get-tuple-element.350.refs_0_, f32[256,128]{1,0:T(8,128)S(1)} %get-tuple-element.351.refs_1_, bf16[4,128,128]{2,1,0:T(8,128)(2,1)S(1)} %pad_maximum_fusion.refs_2_, ...), custom_call_target="tpu_custom_call" | custom-call | bytes 655360 | tf_op jit(solution)/shard_map/pallas_call | solution.py:717
  32.4 0.0 copy-start.3
  32.4 0.0 copy-start.4
  32.4 0.6 %copy-done.3 = f32[256,128]{1,0:T(8,128)} copy-done((f32[256,128]{1,0:T(8,128)}, f32[256,128]{1,0:T(8,128)S(1)}, u32[]{:S(2)}) %copy-start.3) | copy-done | bytes 131096
  33.0 0.0 copy-done.4
  (21 shorter events, 0.1 us)
Async XLA Ops:
  0.6 9.6 %copy-start = (bf16[256,512]{1,0:T(8,128)(2,1)S(1)}, bf16[256,512]{1,0:T(8,128)(2,1)}, u32[]{:S(2)}) copy-start(bf16[256,512]{1,0:T(8,128)(2,1)} %query_ref.5) | copy-start | bytes 786436
  0.6 1.6 %collective-permute-start.10 = (bf16[256,128]{1,0:T(8,128)(2,1)}, bf16[256,128]{1,0:T(8,128)(2,1)S(1)}, u32[]{:S(2)}, u32[]{:S(2)}) collective-permute-start(bf16[256,128]{1,0:T(8,128)(2,1)} %value_ref.5), channel_id=1, source_target_pairs={{0,4},{4,0},{8,12},{12,8},{16,20},{20,16},{24,28},{28,24},{1,5},{5... | collective-permute-start | bytes 196616 | tf_op jit(solution)/shard_map/ppermute | solution.py:556
  1.2 1.5 %collective-permute-start.9 = (bf16[256,128]{1,0:T(8,128)(2,1)}, bf16[256,128]{1,0:T(8,128)(2,1)S(1)}, u32[]{:S(2)}, u32[]{:S(2)}) collective-permute-start(bf16[256,128]{1,0:T(8,128)(2,1)} %key_ref.7), channel_id=1, source_target_pairs={{0,4},{4,0},{8,12},{12,8},{16,20},{20,16},{24,28},{28,24},{1,5},{5... | collective-permute-start | bytes 196616 | tf_op jit(solution)/shard_map/ppermute | solution.py:556
  4.9 10.3 %collective-permute-start.11 = (bf16[4,128,128]{2,1,0:T(8,128)(2,1)S(1)}, bf16[4,128,128]{2,1,0:T(8,128)(2,1)S(1)}, u32[]{:S(2)}, u32[]{:S(2)}) collective-permute-start(bf16[4,128,128]{2,1,0:T(8,128)(2,1)S(1)} %get-tuple-element.334), channel_id=1, source_target_pairs={{0,8},{4,20},{8,0},{12,28},{16,24},{20,4},{24,16},{28,12},{1,9},{5... | collective-permute-start | bytes 393224 | tf_op jit(solution)/shard_map/ppermute | solution.py:565
  7.7 7.5 %collective-permute-start.12 = (bf16[2,128,128]{2,1,0:T(8,128)(2,1)S(1)}, bf16[2,128,128]{2,1,0:T(8,128)(2,1)S(1)}, u32[]{:S(2)}, u32[]{:S(2)}) collective-permute-start(bf16[2,128,128]{2,1,0:T(8,128)(2,1)S(1)} %get-tuple-element.335), channel_id=1, source_target_pairs={{0,24},{4,28},{8,16},{12,20},{16,8},{20,12},{24,0},{28,4},{1,25},{... | collective-permute-start | bytes 196616 | tf_op jit(solution)/shard_map/ppermute | solution.py:556
  10.2 1.0 %copy-start.1 = (bf16[256,512]{1,0:T(8,128)(2,1)S(1)}, bf16[256,512]{1,0:T(8,128)(2,1)}, u32[]{:S(2)}) copy-start(bf16[256,512]{1,0:T(8,128)(2,1)} %grad_ref.5) | copy-start | bytes 786436
  11.2 4.6 %copy-start.5 = (bf16[256,128]{1,0:T(8,128)(2,1)S(1)}, bf16[256,128]{1,0:T(8,128)(2,1)}, u32[]{:S(2)}) copy-start(bf16[256,128]{1,0:T(8,128)(2,1)} %value_ref.5) | copy-start | bytes 196612
  11.2 4.6 %copy-start.7 = (bf16[256,128]{1,0:T(8,128)(2,1)S(1)}, bf16[256,128]{1,0:T(8,128)(2,1)}, u32[]{:S(2)}) copy-start(bf16[256,128]{1,0:T(8,128)(2,1)} %key_ref.7) | copy-start | bytes 196612
  15.3 1.3 %collective-permute-start.14 = (bf16[2,128,128]{2,1,0:T(8,128)(2,1)S(1)}, bf16[2,128,128]{2,1,0:T(8,128)(2,1)S(1)}, u32[]{:S(2)}, u32[]{:S(2)}) collective-permute-start(bf16[2,128,128]{2,1,0:T(8,128)(2,1)S(1)} %collective-permute-done.12.refs_1_), channel_id=1, source_target_pairs={{0,4},{4,0},{8,12},{12,8},{16,20},{20,16},{24,28},{28,24},{1,5},{5... | collective-permute-start | bytes 196616 | tf_op jit(solution)/shard_map/ppermute | solution.py:556
  15.3 1.5 %collective-permute-start.13 = (bf16[4,128,128]{2,1,0:T(8,128)(2,1)S(1)}, bf16[4,128,128]{2,1,0:T(8,128)(2,1)S(1)}, u32[]{:S(2)}, u32[]{:S(2)}) collective-permute-start(bf16[4,128,128]{2,1,0:T(8,128)(2,1)S(1)} %collective-permute-done.11.refs_0_), channel_id=1, source_target_pairs={{0,4},{4,0},{8,12},{12,8},{16,20},{20,16},{24,28},{28,24},{1,5},{5... | collective-permute-start | bytes 393224 | tf_op jit(solution)/shard_map/ppermute | solution.py:556
  15.8 1.0 %copy-start.2 = (bf16[256,512]{1,0:T(8,128)(2,1)S(1)}, bf16[256,512]{1,0:T(8,128)(2,1)}, u32[]{:S(2)}) copy-start(bf16[256,512]{1,0:T(8,128)(2,1)} %grad_ref.5) | copy-start | bytes 786436
  15.8 1.0 %copy-start.9 = (bf16[256,128]{1,0:T(8,128)(2,1)}, bf16[256,128]{1,0:T(8,128)(2,1)S(1)}, u32[]{:S(2)}) copy-start(bf16[256,128]{1,0:T(8,128)(2,1)S(1)} %get-tuple-element.582) | copy-start | bytes 196612
  19.2 1.4 %collective-permute-start.15 = (bf16[4,128,128]{2,1,0:T(8,128)(2,1)S(1)}, bf16[4,128,128]{2,1,0:T(8,128)(2,1)S(1)}, u32[]{:S(2)}, u32[]{:S(2)}) collective-permute-start(bf16[4,128,128]{2,1,0:T(8,128)(2,1)S(1)} %get-tuple-element.341), channel_id=1, source_target_pairs={{0,4},{4,0},{8,12},{12,8},{16,20},{20,16},{24,28},{28,24},{1,5},{5... | collective-permute-start | bytes 393224 | tf_op jit(solution)/shard_map/ppermute | solution.py:556
  20.6 1.1 %copy-start.6 = (bf16[256,128]{1,0:T(8,128)(2,1)S(1)}, bf16[256,128]{1,0:T(8,128)(2,1)}, u32[]{:S(2)}) copy-start(bf16[256,128]{1,0:T(8,128)(2,1)} %value_ref.5) | copy-start | bytes 196612
  20.6 1.1 %copy-start.8 = (bf16[256,128]{1,0:T(8,128)(2,1)S(1)}, bf16[256,128]{1,0:T(8,128)(2,1)}, u32[]{:S(2)}) copy-start(bf16[256,128]{1,0:T(8,128)(2,1)} %key_ref.7) | copy-start | bytes 196612
  20.7 5.5 %collective-permute-start.16 = (bf16[4,128,128]{2,1,0:T(8,128)(2,1)S(1)}, bf16[4,128,128]{2,1,0:T(8,128)(2,1)S(1)}, u32[]{:S(2)}, u32[]{:S(2)}) collective-permute-start(bf16[4,128,128]{2,1,0:T(8,128)(2,1)S(1)} %pad_maximum_fusion.refs_2_), channel_id=1, source_target_pairs={{0,8},{4,20},{8,0},{12,28},{16,24},{20,4},{24,16},{28,12},{1,9},{5... | collective-permute-start | bytes 393224 | tf_op jit(solution)/shard_map/ppermute | solution.py:565
  23.1 6.5 %collective-permute-start.17 = (bf16[2,128,128]{2,1,0:T(8,128)(2,1)S(1)}, bf16[2,128,128]{2,1,0:T(8,128)(2,1)S(1)}, u32[]{:S(2)}, u32[]{:S(2)}) collective-permute-start(bf16[2,128,128]{2,1,0:T(8,128)(2,1)S(1)} %get-tuple-element.352), channel_id=1, source_target_pairs={{0,24},{4,28},{8,16},{12,20},{16,8},{20,12},{24,0},{28,4},{1,25},{... | collective-permute-start | bytes 196616 | tf_op jit(solution)/shard_map/ppermute | solution.py:556
  26.2 5.5 %collective-permute-start.18 = (bf16[4,128,128]{2,1,0:T(8,128)(2,1)S(1)}, bf16[4,128,128]{2,1,0:T(8,128)(2,1)S(1)}, u32[]{:S(2)}, u32[]{:S(2)}) collective-permute-start(bf16[4,128,128]{2,1,0:T(8,128)(2,1)S(1)} %collective-permute-done.16.order_ref.refs_3_), channel_id=1, source_target_pairs={{0,4},{4,0},{8,12},{12,8},{16,20},{20,16},{24,28},{28,24},{1,5},{5... | collective-permute-start | bytes 393224 | tf_op jit(solution)/shard_map/ppermute | solution.py:556
  29.5 2.2 %collective-permute-start.19 = (bf16[2,128,128]{2,1,0:T(8,128)(2,1)S(1)}, bf16[2,128,128]{2,1,0:T(8,128)(2,1)S(1)}, u32[]{:S(2)}, u32[]{:S(2)}) collective-permute-start(bf16[2,128,128]{2,1,0:T(8,128)(2,1)S(1)} %collective-permute-done.17.refs_4_), channel_id=1, source_target_pairs={{0,4},{4,0},{8,12},{12,8},{16,20},{20,16},{24,28},{28,24},{1,5},{5... | collective-permute-start | bytes 196616 | tf_op jit(solution)/shard_map/ppermute | solution.py:556
  32.4 0.7 %copy-start.3 = (f32[256,128]{1,0:T(8,128)}, f32[256,128]{1,0:T(8,128)S(1)}, u32[]{:S(2)}) copy-start(f32[256,128]{1,0:T(8,128)S(1)} %get-tuple-element.325) | copy-start | bytes 393220
  32.4 0.7 %copy-start.4 = (f32[256,128]{1,0:T(8,128)}, f32[256,128]{1,0:T(8,128)S(1)}, u32[]{:S(2)}) copy-start(f32[256,128]{1,0:T(8,128)S(1)} %get-tuple-element.326) | copy-start | bytes 393220

commit v3 on v2

--- a/solution.py
+++ b/solution.py
@@ -247,8 +247,8 @@
     table_any,
     query_ref,
     grad_ref,
-    key_ref,
-    value_ref,
+    key_any,
+    value_any,
     key_other,
     value_other,
     max_own,
@@ -361,8 +361,10 @@
             return table_ref[ids(rank * tiles + b), ids(rank * tiles + a)]
 
         own_bias(tiles, bias_ref.at[own_rows, :], allowed)
-        keys_ref[own_rows, :] = key_ref[...]
-        values_ref[own_rows, :] = value_ref[...]
+        for source, target in ((key_any, keys_ref), (value_any, values_ref)):
+            copy = pltpu.make_async_copy(source, target.at[own_rows, :], copy_sem)
+            copy.start()
+            copy.wait()
 
         def fetch(index, carry):
             copy = pltpu.make_async_copy(more_ref.at[index - 1], staged_ref, copy_sem)
@@ -518,9 +520,10 @@
     order_ref,
     attended_ref,
     query_out,
+    order_out,
     copy_sem,
 ):
-    del order_ref
+    del order_ref, order_out
     rows = query_out.shape[0]
 
     @pl.when(info_ref[0] <= slots)
@@ -636,7 +639,12 @@
     )
     parts, row_max, inverse, delta, out_t, dscores, slot_keys, more_terms, *full_values = call(
         functools.partial(gathered_kernel, chips, tiles, slots, heads, tile_total),
-        [SMEM_SPEC, ANY_SPEC] + [VMEM_SPEC] * 10 + [ANY_SPEC] + [VMEM_SPEC] * (2 * len(arrived)),
+        [SMEM_SPEC, ANY_SPEC]
+        + [VMEM_SPEC] * 2
+        + [ANY_SPEC] * 2
+        + [VMEM_SPEC] * 6
+        + [ANY_SPEC]
+        + [VMEM_SPEC] * (2 * len(arrived)),
         (
             shape((2 * slots, TILE, HD), bf16),
             line,
@@ -702,14 +710,15 @@
         half_sum,
     )
     back = trade(chip_sum, half_sum)
-    attended, query_grad = call(
+    attended, query_grad, back[0] = call(
         functools.partial(queries_kernel, slots, heads),
         [SMEM_SPEC] + [VMEM_SPEC] * 5 + [ANY_SPEC] * 3,
-        full[:2],
-        (VMEM_SPEC,) * 2,
+        (*full[:2], shape(back[0].shape, bf16)),
+        (VMEM_SPEC,) * 2 + (ANY_SPEC,),
         scratch=(pltpu.SemaphoreType.DMA,),
         flops=16 * work,
         moved=8 * row_count * heads * HD,
+        aliases={8: 2},
     )(info, key_rows, own_dscores, dscores, slot_keys, out_t, *full_values[:2], back[0])
     sums = [chip_sum] + back + [swap(values, 1) for values in back]
 

time: 33.4 us -> 32 us (0.958)
  waiting for transfers between devices: 7.24 us -> 6.23 us
  Pallas kernels: 10.1 us -> 9.68 us
    ppermute x9, waiting for transfers between devices: 7.24 us -> 6.23 us  [swap(): lax.ppermute(values, 'seq', [(source, source ^ step) for source in range(...]
    pallas_call x1, Pallas kernels: 2.38 us -> 2.02 us  [per_device(): call(functools.partial(gathered_kernel, chips, tiles, slots, heads, tile_...]
    unnamed x20 -> x14, local copies, waits for them, and re-layouts: 1.67 us -> 1.65 us
  transfers between devices with their start and end apart: 11 -> 11, of which waited for: 7 -> 8; matrix products, arithmetic and copies ran while one was open for 2% -> 2% of each run, Pallas kernels for 14% -> 15%
where the time goes in v3:
time: 32 us; the launch traced here: 31.7 us
  starting transfers between devices  12.5 us (39%)
  Pallas kernels  9.68 us (30%)
  waiting for transfers between devices  6.23 us (19%)
  local copies, waits for them, and re-layouts  1.65 us (5%)
  between operations  0.81 us (3%)
  other arithmetic  0.77 us (2%)
    ppermute x9, starting transfers between devices, swap(): lax.ppermute(values, 'seq', [(source, source ^ step) for source in range(...  8.7 us
    ppermute x9, waiting for transfers between devices, swap(): lax.ppermute(values, 'seq', [(source, source ^ step) for source in range(...  6.23 us
    ppermute x2, starting transfers between devices, trade(): got.append(lax.ppermute(full, 'seq', routes))  3.85 us
    pallas_call x1, Pallas kernels, per_device(): call(functools.partial(list_kernel, tile_total, tiles, slots), [SMEM_SPEC...  2.3 us
    pallas_call x1, Pallas kernels, per_device(): call(functools.partial(gathered_kernel, chips, tiles, slots, heads, tile_...  2.02 us
    pallas_call x1, Pallas kernels, per_device(): call(functools.partial(queries_kernel, slots, heads), [SMEM_SPEC] + [VMEM...  1.91 us
    unnamed x14, local copies, waits for them, and re-layouts  1.65 us
    pallas_call x1, Pallas kernels, per_device(): call(functools.partial(own_kernel, tiles, slots, heads, tile_total), [SME...  1.56 us
  transfers between devices with their start and end apart: 11, of which 8 were waited for; matrix products, arithmetic and copies ran while one was open for 2% of the time, Pallas kernels for 15%

profile of v3, /device:TPU:0, one launch (start us, length us, event | category | flops | bytes accessed | tf_op | source)
XLA Modules:
  0.0 31.7 jit_solution(17234379752753766993)
XLA Ops:
  0.6 0.5 %collective-permute-start.10 = (bf16[256,128]{1,0:T(8,128)(2,1)}, bf16[256,128]{1,0:T(8,128)(2,1)S(1)}, u32[]{:S(2)}, u32[]{:S(2)}) collective-permute-start(bf16[256,128]{1,0:T(8,128)(2,1)} %value_ref.3), channel_id=1, source_target_pairs={{0,4},{4,0},{8,12},{12,8},{16,20},{20,16},{24,28},{28,24},{1,5},{5... | collective-permute-start | bytes 196616 | tf_op jit(solution)/shard_map/ppermute | solution.py:559
  1.2 0.1 collective-permute-start.9
  1.2 0.7 %pad_add_fusion.table_ref.table_any = s32[17,16]{1,0:T(8,128)S(1)} fusion(s32[1,16]{1,0:T(1,128)} %bitcast.35, s32[16,16]{1,0:T(8,128)} %param.15), kind=kLoop, calls=%fused_computation.11 | loop fusion | flops 272 | bytes 2176 | tf_op jit(solution)/shard_map/add | solution.py:578
  2.0 0.3 collective-permute-done.10.refs_3_.value_other
  2.3 0.4 %collective-permute-done.9.refs_2_.key_other = bf16[256,128]{1,0:T(8,128)(2,1)S(1)} collective-permute-done((bf16[256,128]{1,0:T(8,128)(2,1)}, bf16[256,128]{1,0:T(8,128)(2,1)S(1)}, u32[]{:S(2)}, u32[]{:S(2)}) %collective-permute-start.9) | collective-permute-done | bytes 65568 | tf_op jit(solution)/shard_map/ppermute | solution.py:559
  2.6 2.3 %shard_map.93 = (s32[42]{0:T(128)S(1)}, bf16[4,128,128]{2,1,0:T(8,128)(2,1)S(1)}, bf16[2,128,128]{2,1,0:T(8,128)(2,1)S(1)}, bf16[7,2,2,128,128]{4,3,2,1,0:T(8,128)(2,1)}) custom-call(s32[17,16]{1,0:T(8,128)S(1)} %pad_add_fusion.table_ref.table_any, bf16[256,128]{1,0:T(8,128)(2,1)} %key_ref.5, bf16[256,128]{1,0:T(8,128)(2,1)} %value_ref.3, ...), custom_call_target="tpu_custom_call" | custom-call | bytes 4194304 | tf_op jit(solution)/shard_map/pallas_call | solution.py:581
  4.9 2.8 %collective-permute-start.11 = (bf16[4,128,128]{2,1,0:T(8,128)(2,1)S(1)}, bf16[4,128,128]{2,1,0:T(8,128)(2,1)S(1)}, u32[]{:S(2)}, u32[]{:S(2)}) collective-permute-start(bf16[4,128,128]{2,1,0:T(8,128)(2,1)S(1)} %get-tuple-element.335), channel_id=1, source_target_pairs={{0,8},{4,20},{8,0},{12,28},{16,24},{20,4},{24,16},{28,12},{1,9},{5... | collective-permute-start | bytes 393224 | tf_op jit(solution)/shard_map/ppermute | solution.py:568
  7.7 2.5 %collective-permute-start.12 = (bf16[2,128,128]{2,1,0:T(8,128)(2,1)S(1)}, bf16[2,128,128]{2,1,0:T(8,128)(2,1)S(1)}, u32[]{:S(2)}, u32[]{:S(2)}) collective-permute-start(bf16[2,128,128]{2,1,0:T(8,128)(2,1)S(1)} %get-tuple-element.336), channel_id=1, source_target_pairs={{0,24},{4,28},{8,16},{12,20},{16,8},{20,12},{24,0},{28,4},{1,25},{... | collective-permute-start | bytes 196616 | tf_op jit(solution)/shard_map/ppermute | solution.py:559
  10.2 0.9 %copy-done.1 = bf16[256,512]{1,0:T(8,128)(2,1)S(1)} copy-done((bf16[256,512]{1,0:T(8,128)(2,1)S(1)}, bf16[256,512]{1,0:T(8,128)(2,1)}, u32[]{:S(2)}) %copy-start.1) | copy-done | bytes 262168
  11.2 1.6 %shard_map.94 = (f32[1,1024]{1,0:T(1,128)S(1)}, f32[1,1024]{1,0:T(1,128)S(1)}, f32[128,1024]{1,0:T(8,128)S(1)}, bf16[128,1024]{1,0:T(8,128)(2,1)S(1)}) custom-call(s32[42]{0:T(128)S(1)} %get-tuple-element.523.info_ref, bf16[256,512]{1,0:T(8,128)(2,1)S(1)} %copy-done, bf16[256,512]{1,0:T(8,128)(2,1)S(1)} %copy-done.1, bf16[256,128]{1,0:T(8,128)(2,1)} %key_ref.5, ...), custom_call_target="tpu_custom_call" | custom-call | flops 1610612736 | bytes 524288 | tf_op jit(solution)/shard_map/pallas_call | solution.py:624
  12.8 2.5 %collective-permute-done.12.refs_1_ = bf16[2,128,128]{2,1,0:T(8,128)(2,1)S(1)} collective-permute-done((bf16[2,128,128]{2,1,0:T(8,128)(2,1)S(1)}, bf16[2,128,128]{2,1,0:T(8,128)(2,1)S(1)}, u32[]{:S(2)}, u32[]{:S(2)}) %collective-permute-start.12) | collective-permute-done | bytes 65568 | tf_op jit(solution)/shard_map/ppermute | solution.py:559
  15.3 0.0 collective-permute-start.14
  15.3 0.5 %collective-permute-start.13 = (bf16[4,128,128]{2,1,0:T(8,128)(2,1)S(1)}, bf16[4,128,128]{2,1,0:T(8,128)(2,1)S(1)}, u32[]{:S(2)}, u32[]{:S(2)}) collective-permute-start(bf16[4,128,128]{2,1,0:T(8,128)(2,1)S(1)} %collective-permute-done.11.refs_0_), channel_id=1, source_target_pairs={{0,4},{4,0},{8,12},{12,8},{16,20},{20,16},{24,28},{28,24},{1,5},{5... | collective-permute-start | bytes 393224 | tf_op jit(solution)/shard_map/ppermute | solution.py:559
  15.8 0.7 %collective-permute-done.14.refs_3_ = bf16[2,128,128]{2,1,0:T(8,128)(2,1)S(1)} collective-permute-done((bf16[2,128,128]{2,1,0:T(8,128)(2,1)S(1)}, bf16[2,128,128]{2,1,0:T(8,128)(2,1)S(1)}, u32[]{:S(2)}, u32[]{:S(2)}) %collective-permute-start.14) | collective-permute-done | bytes 65568 | tf_op jit(solution)/shard_map/ppermute | solution.py:559
  16.5 0.2 collective-permute-done.13.refs_2_
  16.8 2.0 %shard_map.95 = (bf16[4,128,128]{2,1,0:T(8,128)(2,1)S(1)}, f32[1,1024]{1,0:T(1,128)S(1)}, f32[1,1024]{1,0:T(1,128)S(1)}, f32[1,1024]{1,0:T(1,128)S(1)}, bf16[128...) custom-call(s32[42]{0:T(128)S(1)} %get-tuple-element.595, ...), custom_call_target="tpu_custom_call" | custom-call | flops 1610612736 | bytes 524288 | tf_op jit(solution)/shard_map/pallas_call | solution.py:640
  18.8 0.0 copy-start.2
  18.8 0.4 %collective-permute-start.15 = (bf16[4,128,128]{2,1,0:T(8,128)(2,1)S(1)}, bf16[4,128,128]{2,1,0:T(8,128)(2,1)S(1)}, u32[]{:S(2)}, u32[]{:S(2)}) collective-permute-start(bf16[4,128,128]{2,1,0:T(8,128)(2,1)S(1)} %get-tuple-element.342), channel_id=1, source_target_pairs={{0,4},{4,0},{8,12},{12,8},{16,20},{20,16},{24,28},{28,24},{1,5},{5... | collective-permute-start | bytes 393224 | tf_op jit(solution)/shard_map/ppermute | solution.py:559
  19.2 1.0 %collective-permute-done.15 = bf16[4,128,128]{2,1,0:T(8,128)(2,1)S(1)} collective-permute-done((bf16[4,128,128]{2,1,0:T(8,128)(2,1)S(1)}, bf16[4,128,128]{2,1,0:T(8,128)(2,1)S(1)}, u32[]{:S(2)}, u32[]{:S(2)}) %collective-permute-start.15) | collective-permute-done | bytes 131104 | tf_op jit(solution)/shard_map/ppermute | solution.py:559
  20.3 1.1 %collective-permute-start.16 = (bf16[4,128,128]{2,1,0:T(8,128)(2,1)S(1)}, bf16[4,128,128]{2,1,0:T(8,128)(2,1)S(1)}, u32[]{:S(2)}, u32[]{:S(2)}) collective-permute-start(bf16[4,128,128]{2,1,0:T(8,128)(2,1)S(1)} %pad_maximum_fusion.refs_2_), channel_id=1, source_target_pairs={{0,8},{4,20},{8,0},{12,28},{16,24},{20,4},{24,16},{28,12},{1,9},{5... | collective-permute-start | bytes 393224 | tf_op jit(solution)/shard_map/ppermute | solution.py:568
  21.4 1.3 %shard_map.96 = (bf16[256,1024]{1,0:T(8,128)(2,1)S(1)}, f32[256,128]{1,0:T(8,128)S(1)}, f32[256,128]{1,0:T(8,128)S(1)}, bf16[2,128,128]{2,1,0:T(8,128)(2,1)S(1)}) custom-call(s32[42]{0:T(128)S(1)} %get-tuple-element.595, bf16[256,512]{1,0:T(8,128)(2,1)S(1)} %copy-done, bf16[256,512]{1,0:T(8,128)(2,1)S(1)} %copy-done.2, ...), custom_call_target="tpu_custom_call", output_to_operand_aliasing={{3}: (10, {})} | custom-call | flops 1207959552 | bytes 524288 | tf_op jit(solution)/shard_map/pallas_call | solution.py:691
  22.7 3.2 %collective-permute-start.17 = (bf16[2,128,128]{2,1,0:T(8,128)(2,1)S(1)}, bf16[2,128,128]{2,1,0:T(8,128)(2,1)S(1)}, u32[]{:S(2)}, u32[]{:S(2)}) collective-permute-start(bf16[2,128,128]{2,1,0:T(8,128)(2,1)S(1)} %get-tuple-element.354), channel_id=1, source_target_pairs={{0,24},{4,28},{8,16},{12,20},{16,8},{20,12},{24,0},{28,4},{1,25},{... | collective-permute-start | bytes 196616 | tf_op jit(solution)/shard_map/ppermute | solution.py:559
  25.9 1.9 %shard_map.97 = (bf16[256,512]{1,0:T(8,128)(2,1)}, f32[256,512]{1,0:T(8,128)}, bf16[4,128,128]{2,1,0:T(8,128)(2,1)S(1)}) custom-call(s32[42]{0:T(128)S(1)} %get-tuple-element.595, bf16[256,128]{1,0:T(8,128)(2,1)S(1)} %get-tuple-element.580, bf16[256,1024]{1,0:T(8,128)(2,1)S(1)} %get-tuple-element.343.own_dscores, ...), custom_call_target="tpu_custom_call", output_to_operand_aliasing={{2}: (8, {})} | custom-call | flops 1073741824 | bytes 1048576 | tf_op jit(solution)/shard_map/pallas_call | solution.py:713
  27.8 1.2 %collective-permute-start.18 = (bf16[4,128,128]{2,1,0:T(8,128)(2,1)S(1)}, bf16[4,128,128]{2,1,0:T(8,128)(2,1)S(1)}, u32[]{:S(2)}, u32[]{:S(2)}) collective-permute-start(bf16[4,128,128]{2,1,0:T(8,128)(2,1)S(1)} %get-tuple-element.353.refs_3_), channel_id=1, source_target_pairs={{0,4},{4,0},{8,12},{12,8},{16,20},{20,16},{24,28},{28,24},{1,5},{5... | collective-permute-start | bytes 393224 | tf_op jit(solution)/shard_map/ppermute | solution.py:559
  29.0 0.1 collective-permute-done.17.refs_4_
  29.1 0.3 collective-permute-start.19
  29.4 1.0 %collective-permute-done.19.refs_6_ = bf16[2,128,128]{2,1,0:T(8,128)(2,1)S(1)} collective-permute-done((bf16[2,128,128]{2,1,0:T(8,128)(2,1)S(1)}, bf16[2,128,128]{2,1,0:T(8,128)(2,1)S(1)}, u32[]{:S(2)}, u32[]{:S(2)}) %collective-permute-start.19) | collective-permute-done | bytes 65568 | tf_op jit(solution)/shard_map/ppermute | solution.py:559
  30.4 0.6 %shard_map.98 = (f32[256,128]{1,0:T(8,128)S(1)}, f32[256,128]{1,0:T(8,128)S(1)}) custom-call(s32[42]{0:T(128)S(1)} %get-tuple-element.595, f32[256,128]{1,0:T(8,128)S(1)} %get-tuple-element.351.refs_0_, f32[256,128]{1,0:T(8,128)S(1)} %get-tuple-element.352.refs_1_, bf16[4,128,128]{2,1,0:T(8,128)(2,1)S(1)} %pad_maximum_fusion.refs_2_, ...), custom_call_target="tpu_custom_call" | custom-call | bytes 655360 | tf_op jit(solution)/shard_map/pallas_call | solution.py:726
  31.0 0.0 copy-start.3
  31.0 0.0 copy-start.4
  31.0 0.6 %copy-done.3 = f32[256,128]{1,0:T(8,128)} copy-done((f32[256,128]{1,0:T(8,128)}, f32[256,128]{1,0:T(8,128)S(1)}, u32[]{:S(2)}) %copy-start.3) | copy-done | bytes 131096
  31.7 0.0 copy-done.4
  (15 shorter events, 0.1 us)
Async XLA Ops:
  0.6 9.6 %copy-start = (bf16[256,512]{1,0:T(8,128)(2,1)S(1)}, bf16[256,512]{1,0:T(8,128)(2,1)}, u32[]{:S(2)}) copy-start(bf16[256,512]{1,0:T(8,128)(2,1)} %query_ref.5) | copy-start | bytes 786436
  0.6 1.6 %collective-permute-start.10 = (bf16[256,128]{1,0:T(8,128)(2,1)}, bf16[256,128]{1,0:T(8,128)(2,1)S(1)}, u32[]{:S(2)}, u32[]{:S(2)}) collective-permute-start(bf16[256,128]{1,0:T(8,128)(2,1)} %value_ref.3), channel_id=1, source_target_pairs={{0,4},{4,0},{8,12},{12,8},{16,20},{20,16},{24,28},{28,24},{1,5},{5... | collective-permute-start | bytes 196616 | tf_op jit(solution)/shard_map/ppermute | solution.py:559
  1.2 1.5 %collective-permute-start.9 = (bf16[256,128]{1,0:T(8,128)(2,1)}, bf16[256,128]{1,0:T(8,128)(2,1)S(1)}, u32[]{:S(2)}, u32[]{:S(2)}) collective-permute-start(bf16[256,128]{1,0:T(8,128)(2,1)} %key_ref.5), channel_id=1, source_target_pairs={{0,4},{4,0},{8,12},{12,8},{16,20},{20,16},{24,28},{28,24},{1,5},{5... | collective-permute-start | bytes 196616 | tf_op jit(solution)/shard_map/ppermute | solution.py:559
  4.9 10.3 %collective-permute-start.11 = (bf16[4,128,128]{2,1,0:T(8,128)(2,1)S(1)}, bf16[4,128,128]{2,1,0:T(8,128)(2,1)S(1)}, u32[]{:S(2)}, u32[]{:S(2)}) collective-permute-start(bf16[4,128,128]{2,1,0:T(8,128)(2,1)S(1)} %get-tuple-element.335), channel_id=1, source_target_pairs={{0,8},{4,20},{8,0},{12,28},{16,24},{20,4},{24,16},{28,12},{1,9},{5... | collective-permute-start | bytes 393224 | tf_op jit(solution)/shard_map/ppermute | solution.py:568
  7.7 7.5 %collective-permute-start.12 = (bf16[2,128,128]{2,1,0:T(8,128)(2,1)S(1)}, bf16[2,128,128]{2,1,0:T(8,128)(2,1)S(1)}, u32[]{:S(2)}, u32[]{:S(2)}) collective-permute-start(bf16[2,128,128]{2,1,0:T(8,128)(2,1)S(1)} %get-tuple-element.336), channel_id=1, source_target_pairs={{0,24},{4,28},{8,16},{12,20},{16,8},{20,12},{24,0},{28,4},{1,25},{... | collective-permute-start | bytes 196616 | tf_op jit(solution)/shard_map/ppermute | solution.py:559
  10.2 1.0 %copy-start.1 = (bf16[256,512]{1,0:T(8,128)(2,1)S(1)}, bf16[256,512]{1,0:T(8,128)(2,1)}, u32[]{:S(2)}) copy-start(bf16[256,512]{1,0:T(8,128)(2,1)} %grad_ref.5) | copy-start | bytes 786436
  11.2 4.6 %copy-start.5 = (bf16[256,128]{1,0:T(8,128)(2,1)S(1)}, bf16[256,128]{1,0:T(8,128)(2,1)}, u32[]{:S(2)}) copy-start(bf16[256,128]{1,0:T(8,128)(2,1)} %value_ref.3) | copy-start | bytes 196612
  11.2 4.6 %copy-start.6 = (bf16[256,128]{1,0:T(8,128)(2,1)S(1)}, bf16[256,128]{1,0:T(8,128)(2,1)}, u32[]{:S(2)}) copy-start(bf16[256,128]{1,0:T(8,128)(2,1)} %key_ref.5) | copy-start | bytes 196612
  15.3 1.3 %collective-permute-start.14 = (bf16[2,128,128]{2,1,0:T(8,128)(2,1)S(1)}, bf16[2,128,128]{2,1,0:T(8,128)(2,1)S(1)}, u32[]{:S(2)}, u32[]{:S(2)}) collective-permute-start(bf16[2,128,128]{2,1,0:T(8,128)(2,1)S(1)} %collective-permute-done.12.refs_1_), channel_id=1, source_target_pairs={{0,4},{4,0},{8,12},{12,8},{16,20},{20,16},{24,28},{28,24},{1,5},{5... | collective-permute-start | bytes 196616 | tf_op jit(solution)/shard_map/ppermute | solution.py:559
  15.3 1.5 %collective-permute-start.13 = (bf16[4,128,128]{2,1,0:T(8,128)(2,1)S(1)}, bf16[4,128,128]{2,1,0:T(8,128)(2,1)S(1)}, u32[]{:S(2)}, u32[]{:S(2)}) collective-permute-start(bf16[4,128,128]{2,1,0:T(8,128)(2,1)S(1)} %collective-permute-done.11.refs_0_), channel_id=1, source_target_pairs={{0,4},{4,0},{8,12},{12,8},{16,20},{20,16},{24,28},{28,24},{1,5},{5... | collective-permute-start | bytes 393224 | tf_op jit(solution)/shard_map/ppermute | solution.py:559
  18.8 2.5 %copy-start.2 = (bf16[256,512]{1,0:T(8,128)(2,1)S(1)}, bf16[256,512]{1,0:T(8,128)(2,1)}, u32[]{:S(2)}) copy-start(bf16[256,512]{1,0:T(8,128)(2,1)} %grad_ref.5) | copy-start | bytes 786436
  18.8 1.4 %collective-permute-start.15 = (bf16[4,128,128]{2,1,0:T(8,128)(2,1)S(1)}, bf16[4,128,128]{2,1,0:T(8,128)(2,1)S(1)}, u32[]{:S(2)}, u32[]{:S(2)}) collective-permute-start(bf16[4,128,128]{2,1,0:T(8,128)(2,1)S(1)} %get-tuple-element.342), channel_id=1, source_target_pairs={{0,4},{4,0},{8,12},{12,8},{16,20},{20,16},{24,28},{28,24},{1,5},{5... | collective-permute-start | bytes 393224 | tf_op jit(solution)/shard_map/ppermute | solution.py:559
  20.3 5.6 %collective-permute-start.16 = (bf16[4,128,128]{2,1,0:T(8,128)(2,1)S(1)}, bf16[4,128,128]{2,1,0:T(8,128)(2,1)S(1)}, u32[]{:S(2)}, u32[]{:S(2)}) collective-permute-start(bf16[4,128,128]{2,1,0:T(8,128)(2,1)S(1)} %pad_maximum_fusion.refs_2_), channel_id=1, source_target_pairs={{0,8},{4,20},{8,0},{12,28},{16,24},{20,4},{24,16},{28,12},{1,9},{5... | collective-permute-start | bytes 393224 | tf_op jit(solution)/shard_map/ppermute | solution.py:568
  22.7 6.5 %collective-permute-start.17 = (bf16[2,128,128]{2,1,0:T(8,128)(2,1)S(1)}, bf16[2,128,128]{2,1,0:T(8,128)(2,1)S(1)}, u32[]{:S(2)}, u32[]{:S(2)}) collective-permute-start(bf16[2,128,128]{2,1,0:T(8,128)(2,1)S(1)} %get-tuple-element.354), channel_id=1, source_target_pairs={{0,24},{4,28},{8,16},{12,20},{16,8},{20,12},{24,0},{28,4},{1,25},{... | collective-permute-start | bytes 196616 | tf_op jit(solution)/shard_map/ppermute | solution.py:559
  27.8 2.6 %collective-permute-start.18 = (bf16[4,128,128]{2,1,0:T(8,128)(2,1)S(1)}, bf16[4,128,128]{2,1,0:T(8,128)(2,1)S(1)}, u32[]{:S(2)}, u32[]{:S(2)}) collective-permute-start(bf16[4,128,128]{2,1,0:T(8,128)(2,1)S(1)} %get-tuple-element.353.refs_3_), channel_id=1, source_target_pairs={{0,4},{4,0},{8,12},{12,8},{16,20},{20,16},{24,28},{28,24},{1,5},{5... | collective-permute-start | bytes 393224 | tf_op jit(solution)/shard_map/ppermute | solution.py:559
  29.1 1.3 %collective-permute-start.19 = (bf16[2,128,128]{2,1,0:T(8,128)(2,1)S(1)}, bf16[2,128,128]{2,1,0:T(8,128)(2,1)S(1)}, u32[]{:S(2)}, u32[]{:S(2)}) collective-permute-start(bf16[2,128,128]{2,1,0:T(8,128)(2,1)S(1)} %collective-permute-done.17.refs_4_), channel_id=1, source_target_pairs={{0,4},{4,0},{8,12},{12,8},{16,20},{20,16},{24,28},{28,24},{1,5},{5... | collective-permute-start | bytes 196616 | tf_op jit(solution)/shard_map/ppermute | solution.py:559
  31.0 0.7 %copy-start.3 = (f32[256,128]{1,0:T(8,128)}, f32[256,128]{1,0:T(8,128)S(1)}, u32[]{:S(2)}) copy-start(f32[256,128]{1,0:T(8,128)S(1)} %get-tuple-element.326) | copy-start | bytes 393220
  31.0 0.7 %copy-start.4 = (f32[256,128]{1,0:T(8,128)}, f32[256,128]{1,0:T(8,128)S(1)}, u32[]{:S(2)}) copy-start(f32[256,128]{1,0:T(8,128)S(1)} %get-tuple-element.327) | copy-start | bytes 393220

commit v4 on v3

--- a/solution.py
+++ b/solution.py
@@ -45,17 +45,9 @@
     return [(step, step + 1) for step in range(1, chips - 1, 2)]
 
 
-def list_kernel(tile_total, tiles, slots, table_ref, *refs):
-    sources, (info_ref, full_ref, half_ref, spare_ref, *refs) = refs[:4], refs[4:]
-    any_ref, loaded, sems = refs[0], refs[1:5], refs[5:]
+def list_kernel(tile_total, tiles, slots, table_ref, info_ref, spare_ref, any_ref):
     del spare_ref
     rank = lax.axis_index("seq")
-    copies = [
-        pltpu.make_async_copy(source, target, sem)
-        for source, target, sem in zip(sources, loaded, sems)
-    ]
-    for copy in copies:
-        copy.start()
 
     def ids(position):
         return table_ref[tile_total, position]
@@ -92,13 +84,14 @@
         for b in range(tiles):
             info_ref[place] = mask(my_tiles[b], my_tiles[a])
             place += 1
-    for copy in copies:
-        copy.wait()
-    odd = rank % 2
+
+def first_kernel(tiles, slots, info_ref, *refs):
+    sources, (full_ref, half_ref) = refs[:4], refs[4:]
+    odd = lax.axis_index("seq") % 2
     for kind in range(2):
         part = odd ^ kind
         target = full_ref.at[pl.ds(part * slots, slots)]
-        pick(tiles, slots, 0, info_ref, loaded[kind], loaded[2 + kind], target)
+        pick(tiles, slots, 0, info_ref, sources[kind], sources[2 + kind], target)
     half_ref[...] = full_ref[:slots]
 
 
@@ -321,29 +314,50 @@
         keys = keys_ref[first, :]
         values = values_ref[first, :]
         slot_keys[...] = keys
-        query = stacked(query_ref, heads)
-        grad = stacked(grad_ref, heads)
-        bias = jnp.concatenate([bias_ref[first, :]] * heads, axis=1)
-        scores = dot_t(keys, query) * scale + bias
-        dprobs = dot_t(values, grad)
-        row_max = jnp.maximum(max_own[...], jnp.max(scores, axis=0, keepdims=True))
-        shrink = jnp.exp2(max_own[...] - row_max)
-        terms = jnp.exp2(scores - row_max)
-        inverse = 1.0 / (total_own[...] * shrink + jnp.sum(terms, axis=0, keepdims=True))
-        weighted = weighted_own[...] * shrink + dot(values.T, terms.astype(jnp.bfloat16))
-        out = (weighted * inverse).astype(jnp.bfloat16)
-        delta = jnp.sum(
-            grad_t_ref[...].astype(jnp.float32) * out.astype(jnp.float32), axis=0, keepdims=True
-        )
-        probs = terms * inverse
-        dscores = (probs * (dprobs - delta)).astype(jnp.bfloat16)
-        value_sum[first, :] = dot(probs.astype(jnp.bfloat16), grad)
-        key_sum[first, :] = dot(dscores, query)
-        out_t_ref[...] = out
-        max_ref[...] = row_max
-        inverse_ref[...] = inverse
-        delta_ref[...] = delta
-        dscores_ref[...] = dscores
+        values_t = values.T
+        per_block = heads // 2 if heads % 2 == 0 else heads
+        width = per_block * rows
+        blocks = range(heads // per_block)
+        bias = jnp.concatenate([bias_ref[first, :]] * per_block, axis=1)
+        spans = [pl.ds(block * width, width) for block in blocks]
+        query_all = stacked(query_ref, heads)
+        grad_all = stacked(grad_ref, heads)
+        query = [query_all[block * width : (block + 1) * width] for block in blocks]
+        grad = [grad_all[block * width : (block + 1) * width] for block in blocks]
+        scores = [dot_t(keys, query[block]) * scale + bias for block in blocks]
+        dprobs, probs, outs = [], [], []
+        for block, span in zip(blocks, spans):
+            dprobs.append(dot_t(values, grad[block]))
+            old_max = max_own[:, span]
+            row_max = jnp.maximum(old_max, jnp.max(scores[block], axis=0, keepdims=True))
+            shrink = jnp.exp2(old_max - row_max)
+            terms = jnp.exp2(scores[block] - row_max)
+            total = total_own[:, span] * shrink + jnp.sum(terms, axis=0, keepdims=True)
+            inverse = 1.0 / total
+            weighted = dot(values_t, terms.astype(jnp.bfloat16))
+            outs.append((shrink * inverse, inverse, weighted))
+            probs.append(terms * inverse)
+            max_ref[:, span] = row_max
+            inverse_ref[:, span] = inverse
+        key_total, value_total = None, None
+        for block, span in zip(blocks, spans):
+            part = dot(probs[block].astype(jnp.bfloat16), grad[block])
+            value_total = part if value_total is None else value_total + part
+            shrunk, inverse, weighted = outs[block]
+            out = (weighted_own[:, span] * shrunk + weighted * inverse).astype(jnp.bfloat16)
+            out_t_ref[:, span] = out
+            delta = jnp.sum(
+                grad_t_ref[:, span].astype(jnp.float32) * out.astype(jnp.float32),
+                axis=0,
+                keepdims=True,
+            )
+            delta_ref[:, span] = delta
+            dscores = (probs[block] * (dprobs[block] - delta)).astype(jnp.bfloat16)
+            dscores_ref[:, span] = dscores
+            part = dot(dscores, query[block])
+            key_total = part if key_total is None else key_total + part
+        key_sum[first, :] = key_total
+        value_sum[first, :] = value_total
 
     @pl.when(needed > slots)
     def _():
@@ -578,23 +592,21 @@
     table = table + jnp.pad(tile_ids[None], ((tile_total, 0), (0, 0)))
     key_other, value_other = swap(key_rows, 1), swap(value_rows, 1)
     chip_rows = (key_rows, value_rows, key_other, value_other)
-    info, chosen, chosen_half, spare = call(
+    info, spare = call(
         functools.partial(list_kernel, tile_total, tiles, slots),
-        [SMEM_SPEC] + [ANY_SPEC] * 4,
-        (
-            shape((info_size(tile_total, tiles, slots),), jnp.int32),
-            shape((2 * slots, TILE, HD), bf16),
-            shape(slot_shape, bf16),
-            shape(buffer, bf16),
-        ),
-        (SMEM_SPEC, VMEM_SPEC, VMEM_SPEC, ANY_SPEC),
-        scratch=(
-            pltpu.SMEM((tile_total,), jnp.int32),
-            *[pltpu.VMEM(key_rows.shape, bf16)] * 4,
-            *[pltpu.SemaphoreType.DMA] * 4,
-        ),
+        [SMEM_SPEC],
+        (shape((info_size(tile_total, tiles, slots),), jnp.int32), shape(buffer, bf16)),
+        (SMEM_SPEC, ANY_SPEC),
+        scratch=(pltpu.SMEM((tile_total,), jnp.int32),),
         moved=4 * 1024 * 1024,
-    )(table, *chip_rows)
+    )(table)
+    chosen, chosen_half = call(
+        functools.partial(first_kernel, tiles, slots),
+        [SMEM_SPEC] + [VMEM_SPEC] * 4,
+        (shape((2 * slots, TILE, HD), bf16), shape(slot_shape, bf16)),
+        (VMEM_SPEC,) * 2,
+        moved=5 * row_count * HD * 2,
+    )(info, *chip_rows)
     used = (info[0] + slots - 1) // slots
 
     def select(index):

time: 32 us -> 31.7 us (level)
  waiting for transfers between devices: 6.23 us -> 5.37 us
    pallas_call x0 -> x1, Pallas kernels: none -> 0.97 us  [per_device(): call(functools.partial(first_kernel, tiles, slots), [SMEM_SPEC] + [VMEM_S...]
    ppermute x9, waiting for transfers between devices: 6.23 us -> 5.37 us  [swap(): lax.ppermute(values, 'seq', [(source, source ^ step) for source in range(...]
    pallas_call x1, Pallas kernels: 2.3 us -> 1.61 us  [per_device(): call(functools.partial(list_kernel, tile_total, tiles, slots), [SMEM_SPEC...]
    unnamed x14 -> x16, local copies, waits for them, and re-layouts: 1.65 us -> 1.69 us
  transfers between devices with their start and end apart: 11 -> 11, of which waited for: 8 -> 6; matrix products, arithmetic and copies ran while one was open for 2% -> 2% of each run, Pallas kernels for 15% -> 20%
where the time goes in v4:
time: 31.7 us; the launch traced here: 31.4 us
  starting transfers between devices  12.8 us (40%)
  Pallas kernels  9.97 us (31%)
  waiting for transfers between devices  5.37 us (17%)
  local copies, waits for them, and re-layouts  1.69 us (5%)
  between operations  0.84 us (3%)
  other arithmetic  0.76 us (2%)
    ppermute x9, starting transfers between devices, swap(): lax.ppermute(values, 'seq', [(source, source ^ step) for source in range(...  8.65 us
    ppermute x9, waiting for transfers between devices, swap(): lax.ppermute(values, 'seq', [(source, source ^ step) for source in range(...  5.37 us
    ppermute x2, starting transfers between devices, trade(): got.append(lax.ppermute(full, 'seq', routes))  4.15 us
    pallas_call x1, Pallas kernels, per_device(): call(functools.partial(gathered_kernel, chips, tiles, slots, heads, tile_...  2.01 us
    pallas_call x1, Pallas kernels, per_device(): call(functools.partial(queries_kernel, slots, heads), [SMEM_SPEC] + [VMEM...  1.91 us
    unnamed x16, local copies, waits for them, and re-layouts  1.69 us
    pallas_call x1, Pallas kernels, per_device(): call(functools.partial(list_kernel, tile_total, tiles, slots), [SMEM_SPEC...  1.61 us
    pallas_call x1, Pallas kernels, per_device(): call(functools.partial(own_kernel, tiles, slots, heads, tile_total), [SME...  1.56 us
  transfers between devices with their start and end apart: 11, of which 6 were waited for; matrix products, arithmetic and copies ran while one was open for 2% of the time, Pallas kernels for 20%

profile of v4, /device:TPU:0, one launch (start us, length us, event | category | flops | bytes accessed | tf_op | source)
XLA Modules:
  0.0 31.4 jit_solution(5562719852999112178)
XLA Ops:
  0.7 0.5 %collective-permute-start.10 = (bf16[256,128]{1,0:T(8,128)(2,1)}, bf16[256,128]{1,0:T(8,128)(2,1)S(1)}, u32[]{:S(2)}, u32[]{:S(2)}) collective-permute-start(bf16[256,128]{1,0:T(8,128)(2,1)} %value_ref.3), channel_id=1, source_target_pairs={{0,4},{4,0},{8,12},{12,8},{16,20},{20,16},{24,28},{28,24},{1,5},{5... | collective-permute-start | bytes 196616 | tf_op jit(solution)/shard_map/ppermute | solution.py:573
  1.2 0.1 collective-permute-start.9
  1.2 0.0 copy-done.7
  1.3 0.7 %pad_add_fusion.table_ref.table_any = s32[17,16]{1,0:T(8,128)S(1)} fusion(s32[1,16]{1,0:T(1,128)S(1)} %bitcast.35, s32[16,16]{1,0:T(8,128)} %param.15), kind=kLoop, calls=%fused_computation.11 | loop fusion | flops 272 | bytes 2176 | tf_op jit(solution)/shard_map/add | solution.py:592
  2.0 1.6 %shard_map.93 = (s32[42]{0:T(128)S(1)}, bf16[7,2,2,128,128]{4,3,2,1,0:T(8,128)(2,1)}) custom-call(s32[17,16]{1,0:T(8,128)S(1)} %pad_add_fusion.table_ref.table_any), custom_call_target="tpu_custom_call" | custom-call | bytes 4194304 | tf_op jit(solution)/shard_map/pallas_call | solution.py:595
  3.6 0.0 collective-permute-done.10.refs_3_.value_other
  3.6 1.0 %shard_map.95 = (bf16[4,128,128]{2,1,0:T(8,128)(2,1)S(1)}, bf16[2,128,128]{2,1,0:T(8,128)(2,1)S(1)}) custom-call(s32[42]{0:T(128)S(1)} %get-tuple-element.523.info_ref, bf16[256,128]{1,0:T(8,128)(2,1)} %key_ref.5, bf16[256,128]{1,0:T(8,128)(2,1)} %value_ref.3, bf16[256,128]{1,0:T(8,128)(2,1)S(1)} %collective-permute-done.9.refs_2_.key_other, ...), custom_call_target="tpu_custom_call" | custom-call | bytes 327680 | tf_op jit(solution)/shard_map/pallas_call | solution.py:603
  4.6 3.1 %collective-permute-start.11 = (bf16[4,128,128]{2,1,0:T(8,128)(2,1)S(1)}, bf16[4,128,128]{2,1,0:T(8,128)(2,1)S(1)}, u32[]{:S(2)}, u32[]{:S(2)}) collective-permute-start(bf16[4,128,128]{2,1,0:T(8,128)(2,1)S(1)} %get-tuple-element.335), channel_id=1, source_target_pairs={{0,8},{4,20},{8,0},{12,28},{16,24},{20,4},{24,16},{28,12},{1,9},{5... | collective-permute-start | bytes 393224 | tf_op jit(solution)/shard_map/ppermute | solution.py:582
  7.7 2.5 %collective-permute-start.12 = (bf16[2,128,128]{2,1,0:T(8,128)(2,1)S(1)}, bf16[2,128,128]{2,1,0:T(8,128)(2,1)S(1)}, u32[]{:S(2)}, u32[]{:S(2)}) collective-permute-start(bf16[2,128,128]{2,1,0:T(8,128)(2,1)S(1)} %get-tuple-element.336), channel_id=1, source_target_pairs={{0,24},{4,28},{8,16},{12,20},{16,8},{20,12},{24,0},{28,4},{1,25},{... | collective-permute-start | bytes 196616 | tf_op jit(solution)/shard_map/ppermute | solution.py:573
  10.2 0.9 %copy-done.1 = bf16[256,512]{1,0:T(8,128)(2,1)S(1)} copy-done((bf16[256,512]{1,0:T(8,128)(2,1)S(1)}, bf16[256,512]{1,0:T(8,128)(2,1)}, u32[]{:S(2)}) %copy-start.1) | copy-done | bytes 262168
  11.1 1.6 %shard_map.94 = (f32[1,1024]{1,0:T(1,128)S(1)}, f32[1,1024]{1,0:T(1,128)S(1)}, f32[128,1024]{1,0:T(8,128)S(1)}, bf16[128,1024]{1,0:T(8,128)(2,1)S(1)}) custom-call(s32[42]{0:T(128)S(1)} %get-tuple-element.523.info_ref, bf16[256,512]{1,0:T(8,128)(2,1)S(1)} %copy-done, bf16[256,512]{1,0:T(8,128)(2,1)S(1)} %copy-done.1, bf16[256,128]{1,0:T(8,128)(2,1)} %key_ref.5, ...), custom_call_target="tpu_custom_call" | custom-call | flops 1610612736 | bytes 524288 | tf_op jit(solution)/shard_map/pallas_call | solution.py:636
  12.8 2.2 %collective-permute-done.12.refs_1_ = bf16[2,128,128]{2,1,0:T(8,128)(2,1)S(1)} collective-permute-done((bf16[2,128,128]{2,1,0:T(8,128)(2,1)S(1)}, bf16[2,128,128]{2,1,0:T(8,128)(2,1)S(1)}, u32[]{:S(2)}, u32[]{:S(2)}) %collective-permute-start.12) | collective-permute-done | bytes 65568 | tf_op jit(solution)/shard_map/ppermute | solution.py:573
  15.0 0.5 %collective-permute-start.13 = (bf16[4,128,128]{2,1,0:T(8,128)(2,1)S(1)}, bf16[4,128,128]{2,1,0:T(8,128)(2,1)S(1)}, u32[]{:S(2)}, u32[]{:S(2)}) collective-permute-start(bf16[4,128,128]{2,1,0:T(8,128)(2,1)S(1)} %collective-permute-done.11.refs_0_), channel_id=1, source_target_pairs={{0,4},{4,0},{8,12},{12,8},{16,20},{20,16},{24,28},{28,24},{1,5},{5... | collective-permute-start | bytes 393224 | tf_op jit(solution)/shard_map/ppermute | solution.py:573
  15.5 0.7 %collective-permute-done.14.refs_3_ = bf16[2,128,128]{2,1,0:T(8,128)(2,1)S(1)} collective-permute-done((bf16[2,128,128]{2,1,0:T(8,128)(2,1)S(1)}, bf16[2,128,128]{2,1,0:T(8,128)(2,1)S(1)}, u32[]{:S(2)}, u32[]{:S(2)}) %collective-permute-start.14) | collective-permute-done | bytes 65568 | tf_op jit(solution)/shard_map/ppermute | solution.py:573
  16.2 0.2 collective-permute-done.13.refs_2_
  16.5 2.0 %shard_map.96 = (bf16[4,128,128]{2,1,0:T(8,128)(2,1)S(1)}, f32[1,1024]{1,0:T(1,128)S(1)}, f32[1,1024]{1,0:T(1,128)S(1)}, f32[1,1024]{1,0:T(1,128)S(1)}, bf16[128...) custom-call(s32[42]{0:T(128)S(1)} %get-tuple-element.595, ...), custom_call_target="tpu_custom_call" | custom-call | flops 1610612736 | bytes 524288 | tf_op jit(solution)/shard_map/pallas_call | solution.py:652
  18.5 0.0 copy-start.2
  18.5 0.4 %collective-permute-start.15 = (bf16[4,128,128]{2,1,0:T(8,128)(2,1)S(1)}, bf16[4,128,128]{2,1,0:T(8,128)(2,1)S(1)}, u32[]{:S(2)}, u32[]{:S(2)}) collective-permute-start(bf16[4,128,128]{2,1,0:T(8,128)(2,1)S(1)} %get-tuple-element.342), channel_id=1, source_target_pairs={{0,4},{4,0},{8,12},{12,8},{16,20},{20,16},{24,28},{28,24},{1,5},{5... | collective-permute-start | bytes 393224 | tf_op jit(solution)/shard_map/ppermute | solution.py:573
  18.9 1.0 %collective-permute-done.15 = bf16[4,128,128]{2,1,0:T(8,128)(2,1)S(1)} collective-permute-done((bf16[4,128,128]{2,1,0:T(8,128)(2,1)S(1)}, bf16[4,128,128]{2,1,0:T(8,128)(2,1)S(1)}, u32[]{:S(2)}, u32[]{:S(2)}) %collective-permute-start.15) | collective-permute-done | bytes 131104 | tf_op jit(solution)/shard_map/ppermute | solution.py:573
  20.0 1.1 %collective-permute-start.16 = (bf16[4,128,128]{2,1,0:T(8,128)(2,1)S(1)}, bf16[4,128,128]{2,1,0:T(8,128)(2,1)S(1)}, u32[]{:S(2)}, u32[]{:S(2)}) collective-permute-start(bf16[4,128,128]{2,1,0:T(8,128)(2,1)S(1)} %pad_maximum_fusion.refs_2_), channel_id=1, source_target_pairs={{0,8},{4,20},{8,0},{12,28},{16,24},{20,4},{24,16},{28,12},{1,9},{5... | collective-permute-start | bytes 393224 | tf_op jit(solution)/shard_map/ppermute | solution.py:582
  21.0 1.3 %shard_map.97 = (bf16[256,1024]{1,0:T(8,128)(2,1)S(1)}, f32[256,128]{1,0:T(8,128)S(1)}, f32[256,128]{1,0:T(8,128)S(1)}, bf16[2,128,128]{2,1,0:T(8,128)(2,1)S(1)}) custom-call(s32[42]{0:T(128)S(1)} %get-tuple-element.595, bf16[256,512]{1,0:T(8,128)(2,1)S(1)} %copy-done, bf16[256,512]{1,0:T(8,128)(2,1)S(1)} %copy-done.2, ...), custom_call_target="tpu_custom_call", output_to_operand_aliasing={{3}: (10, {})} | custom-call | flops 1207959552 | bytes 524288 | tf_op jit(solution)/shard_map/pallas_call | solution.py:703
  22.4 3.1 %collective-permute-start.17 = (bf16[2,128,128]{2,1,0:T(8,128)(2,1)S(1)}, bf16[2,128,128]{2,1,0:T(8,128)(2,1)S(1)}, u32[]{:S(2)}, u32[]{:S(2)}) collective-permute-start(bf16[2,128,128]{2,1,0:T(8,128)(2,1)S(1)} %get-tuple-element.354), channel_id=1, source_target_pairs={{0,24},{4,28},{8,16},{12,20},{16,8},{20,12},{24,0},{28,4},{1,25},{... | collective-permute-start | bytes 196616 | tf_op jit(solution)/shard_map/ppermute | solution.py:573
  25.5 1.9 %shard_map.98 = (bf16[256,512]{1,0:T(8,128)(2,1)}, f32[256,512]{1,0:T(8,128)}, bf16[4,128,128]{2,1,0:T(8,128)(2,1)S(1)}) custom-call(s32[42]{0:T(128)S(1)} %get-tuple-element.595, bf16[256,128]{1,0:T(8,128)(2,1)S(1)} %get-tuple-element.580, bf16[256,1024]{1,0:T(8,128)(2,1)S(1)} %get-tuple-element.343.own_dscores, ...), custom_call_target="tpu_custom_call", output_to_operand_aliasing={{2}: (8, {})} | custom-call | flops 1073741824 | bytes 1048576 | tf_op jit(solution)/shard_map/pallas_call | solution.py:725
  27.4 1.2 %collective-permute-start.18 = (bf16[4,128,128]{2,1,0:T(8,128)(2,1)S(1)}, bf16[4,128,128]{2,1,0:T(8,128)(2,1)S(1)}, u32[]{:S(2)}, u32[]{:S(2)}) collective-permute-start(bf16[4,128,128]{2,1,0:T(8,128)(2,1)S(1)} %get-tuple-element.353.refs_3_), channel_id=1, source_target_pairs={{0,4},{4,0},{8,12},{12,8},{16,20},{20,16},{24,28},{28,24},{1,5},{5... | collective-permute-start | bytes 393224 | tf_op jit(solution)/shard_map/ppermute | solution.py:573
  28.7 0.2 collective-permute-done.17.refs_4_
  28.9 0.3 collective-permute-start.19
  29.1 1.0 %collective-permute-done.19.refs_6_ = bf16[2,128,128]{2,1,0:T(8,128)(2,1)S(1)} collective-permute-done((bf16[2,128,128]{2,1,0:T(8,128)(2,1)S(1)}, bf16[2,128,128]{2,1,0:T(8,128)(2,1)S(1)}, u32[]{:S(2)}, u32[]{:S(2)}) %collective-permute-start.19) | collective-permute-done | bytes 65568 | tf_op jit(solution)/shard_map/ppermute | solution.py:573
  30.1 0.6 %shard_map.99 = (f32[256,128]{1,0:T(8,128)S(1)}, f32[256,128]{1,0:T(8,128)S(1)}) custom-call(s32[42]{0:T(128)S(1)} %get-tuple-element.595, f32[256,128]{1,0:T(8,128)S(1)} %get-tuple-element.351.refs_0_, f32[256,128]{1,0:T(8,128)S(1)} %get-tuple-element.352.refs_1_, bf16[4,128,128]{2,1,0:T(8,128)(2,1)S(1)} %pad_maximum_fusion.refs_2_, ...), custom_call_target="tpu_custom_call" | custom-call | bytes 655360 | tf_op jit(solution)/shard_map/pallas_call | solution.py:738
  30.7 0.0 copy-start.3
  30.7 0.0 copy-start.4
  30.8 0.6 %copy-done.3 = f32[256,128]{1,0:T(8,128)} copy-done((f32[256,128]{1,0:T(8,128)}, f32[256,128]{1,0:T(8,128)S(1)}, u32[]{:S(2)}) %copy-start.3) | copy-done | bytes 131096
  31.4 0.0 copy-done.4
  (18 shorter events, 0.1 us)
Async XLA Ops:
  0.6 0.7 %copy-start.7 = (s32[16]{0:T(128)S(1)}, s32[16]{0:T(128)}, u32[]{:S(2)}) copy-start(s32[16]{0:T(128)} %param.14) | copy-start | bytes 196
  0.6 9.5 %copy-start = (bf16[256,512]{1,0:T(8,128)(2,1)S(1)}, bf16[256,512]{1,0:T(8,128)(2,1)}, u32[]{:S(2)}) copy-start(bf16[256,512]{1,0:T(8,128)(2,1)} %query_ref.5) | copy-start | bytes 786436
  0.7 3.0 %collective-permute-start.10 = (bf16[256,128]{1,0:T(8,128)(2,1)}, bf16[256,128]{1,0:T(8,128)(2,1)S(1)}, u32[]{:S(2)}, u32[]{:S(2)}) collective-permute-start(bf16[256,128]{1,0:T(8,128)(2,1)} %value_ref.3), channel_id=1, source_target_pairs={{0,4},{4,0},{8,12},{12,8},{16,20},{20,16},{24,28},{28,24},{1,5},{5... | collective-permute-start | bytes 196616 | tf_op jit(solution)/shard_map/ppermute | solution.py:573
  1.2 2.5 %collective-permute-start.9 = (bf16[256,128]{1,0:T(8,128)(2,1)}, bf16[256,128]{1,0:T(8,128)(2,1)S(1)}, u32[]{:S(2)}, u32[]{:S(2)}) collective-permute-start(bf16[256,128]{1,0:T(8,128)(2,1)} %key_ref.5), channel_id=1, source_target_pairs={{0,4},{4,0},{8,12},{12,8},{16,20},{20,16},{24,28},{28,24},{1,5},{5... | collective-permute-start | bytes 196616 | tf_op jit(solution)/shard_map/ppermute | solution.py:573
  4.6 10.4 %collective-permute-start.11 = (bf16[4,128,128]{2,1,0:T(8,128)(2,1)S(1)}, bf16[4,128,128]{2,1,0:T(8,128)(2,1)S(1)}, u32[]{:S(2)}, u32[]{:S(2)}) collective-permute-start(bf16[4,128,128]{2,1,0:T(8,128)(2,1)S(1)} %get-tuple-element.335), channel_id=1, source_target_pairs={{0,8},{4,20},{8,0},{12,28},{16,24},{20,4},{24,16},{28,12},{1,9},{5... | collective-permute-start | bytes 393224 | tf_op jit(solution)/shard_map/ppermute | solution.py:582
  7.7 7.3 %collective-permute-start.12 = (bf16[2,128,128]{2,1,0:T(8,128)(2,1)S(1)}, bf16[2,128,128]{2,1,0:T(8,128)(2,1)S(1)}, u32[]{:S(2)}, u32[]{:S(2)}) collective-permute-start(bf16[2,128,128]{2,1,0:T(8,128)(2,1)S(1)} %get-tuple-element.336), channel_id=1, source_target_pairs={{0,24},{4,28},{8,16},{12,20},{16,8},{20,12},{24,0},{28,4},{1,25},{... | collective-permute-start | bytes 196616 | tf_op jit(solution)/shard_map/ppermute | solution.py:573
  10.2 1.0 %copy-start.1 = (bf16[256,512]{1,0:T(8,128)(2,1)S(1)}, bf16[256,512]{1,0:T(8,128)(2,1)}, u32[]{:S(2)}) copy-start(bf16[256,512]{1,0:T(8,128)(2,1)} %grad_ref.5) | copy-start | bytes 786436
  11.1 4.4 %copy-start.5 = (bf16[256,128]{1,0:T(8,128)(2,1)S(1)}, bf16[256,128]{1,0:T(8,128)(2,1)}, u32[]{:S(2)}) copy-start(bf16[256,128]{1,0:T(8,128)(2,1)} %value_ref.3) | copy-start | bytes 196612
  11.1 4.4 %copy-start.6 = (bf16[256,128]{1,0:T(8,128)(2,1)S(1)}, bf16[256,128]{1,0:T(8,128)(2,1)}, u32[]{:S(2)}) copy-start(bf16[256,128]{1,0:T(8,128)(2,1)} %key_ref.5) | copy-start | bytes 196612
  15.0 1.3 %collective-permute-start.14 = (bf16[2,128,128]{2,1,0:T(8,128)(2,1)S(1)}, bf16[2,128,128]{2,1,0:T(8,128)(2,1)S(1)}, u32[]{:S(2)}, u32[]{:S(2)}) collective-permute-start(bf16[2,128,128]{2,1,0:T(8,128)(2,1)S(1)} %collective-permute-done.12.refs_1_), channel_id=1, source_target_pairs={{0,4},{4,0},{8,12},{12,8},{16,20},{20,16},{24,28},{28,24},{1,5},{5... | collective-permute-start | bytes 196616 | tf_op jit(solution)/shard_map/ppermute | solution.py:573
  15.0 1.5 %collective-permute-start.13 = (bf16[4,128,128]{2,1,0:T(8,128)(2,1)S(1)}, bf16[4,128,128]{2,1,0:T(8,128)(2,1)S(1)}, u32[]{:S(2)}, u32[]{:S(2)}) collective-permute-start(bf16[4,128,128]{2,1,0:T(8,128)(2,1)S(1)} %collective-permute-done.11.refs_0_), channel_id=1, source_target_pairs={{0,4},{4,0},{8,12},{12,8},{16,20},{20,16},{24,28},{28,24},{1,5},{5... | collective-permute-start | bytes 393224 | tf_op jit(solution)/shard_map/ppermute | solution.py:573
  18.5 2.6 %copy-start.2 = (bf16[256,512]{1,0:T(8,128)(2,1)S(1)}, bf16[256,512]{1,0:T(8,128)(2,1)}, u32[]{:S(2)}) copy-start(bf16[256,512]{1,0:T(8,128)(2,1)} %grad_ref.5) | copy-start | bytes 786436
  18.5 1.4 %collective-permute-start.15 = (bf16[4,128,128]{2,1,0:T(8,128)(2,1)S(1)}, bf16[4,128,128]{2,1,0:T(8,128)(2,1)S(1)}, u32[]{:S(2)}, u32[]{:S(2)}) collective-permute-start(bf16[4,128,128]{2,1,0:T(8,128)(2,1)S(1)} %get-tuple-element.342), channel_id=1, source_target_pairs={{0,4},{4,0},{8,12},{12,8},{16,20},{20,16},{24,28},{28,24},{1,5},{5... | collective-permute-start | bytes 393224 | tf_op jit(solution)/shard_map/ppermute | solution.py:573
  20.0 5.5 %collective-permute-start.16 = (bf16[4,128,128]{2,1,0:T(8,128)(2,1)S(1)}, bf16[4,128,128]{2,1,0:T(8,128)(2,1)S(1)}, u32[]{:S(2)}, u32[]{:S(2)}) collective-permute-start(bf16[4,128,128]{2,1,0:T(8,128)(2,1)S(1)} %pad_maximum_fusion.refs_2_), channel_id=1, source_target_pairs={{0,8},{4,20},{8,0},{12,28},{16,24},{20,4},{24,16},{28,12},{1,9},{5... | collective-permute-start | bytes 393224 | tf_op jit(solution)/shard_map/ppermute | solution.py:582
  22.4 6.5 %collective-permute-start.17 = (bf16[2,128,128]{2,1,0:T(8,128)(2,1)S(1)}, bf16[2,128,128]{2,1,0:T(8,128)(2,1)S(1)}, u32[]{:S(2)}, u32[]{:S(2)}) collective-permute-start(bf16[2,128,128]{2,1,0:T(8,128)(2,1)S(1)} %get-tuple-element.354), channel_id=1, source_target_pairs={{0,24},{4,28},{8,16},{12,20},{16,8},{20,12},{24,0},{28,4},{1,25},{... | collective-permute-start | bytes 196616 | tf_op jit(solution)/shard_map/ppermute | solution.py:573
  27.4 2.7 %collective-permute-start.18 = (bf16[4,128,128]{2,1,0:T(8,128)(2,1)S(1)}, bf16[4,128,128]{2,1,0:T(8,128)(2,1)S(1)}, u32[]{:S(2)}, u32[]{:S(2)}) collective-permute-start(bf16[4,128,128]{2,1,0:T(8,128)(2,1)S(1)} %get-tuple-element.353.refs_3_), channel_id=1, source_target_pairs={{0,4},{4,0},{8,12},{12,8},{16,20},{20,16},{24,28},{28,24},{1,5},{5... | collective-permute-start | bytes 393224 | tf_op jit(solution)/shard_map/ppermute | solution.py:573
  28.9 1.3 %collective-permute-start.19 = (bf16[2,128,128]{2,1,0:T(8,128)(2,1)S(1)}, bf16[2,128,128]{2,1,0:T(8,128)(2,1)S(1)}, u32[]{:S(2)}, u32[]{:S(2)}) collective-permute-start(bf16[2,128,128]{2,1,0:T(8,128)(2,1)S(1)} %collective-permute-done.17.refs_4_), channel_id=1, source_target_pairs={{0,4},{4,0},{8,12},{12,8},{16,20},{20,16},{24,28},{28,24},{1,5},{5... | collective-permute-start | bytes 196616 | tf_op jit(solution)/shard_map/ppermute | solution.py:573
  30.7 0.7 %copy-start.3 = (f32[256,128]{1,0:T(8,128)}, f32[256,128]{1,0:T(8,128)S(1)}, u32[]{:S(2)}) copy-start(f32[256,128]{1,0:T(8,128)S(1)} %get-tuple-element.326) | copy-start | bytes 393220
  30.7 0.7 %copy-start.4 = (f32[256,128]{1,0:T(8,128)}, f32[256,128]{1,0:T(8,128)S(1)}, u32[]{:S(2)}) copy-start(f32[256,128]{1,0:T(8,128)S(1)} %get-tuple-element.327) | copy-start | bytes 393220

commit v5 on v4

--- a/solution.py
+++ b/solution.py
@@ -45,45 +45,54 @@
     return [(step, step + 1) for step in range(1, chips - 1, 2)]
 
 
-def list_kernel(tile_total, tiles, slots, table_ref, info_ref, spare_ref, any_ref):
+def list_kernel(tile_total, tiles, slots, table_ref, key_any, value_any, *refs):
+    info_ref, spare_ref, key_out, value_out, key_sem, value_sem = refs
     del spare_ref
+    copies = [
+        pltpu.make_async_copy(key_any, key_out, key_sem),
+        pltpu.make_async_copy(value_any, value_out, value_sem),
+    ]
+    for copy in copies:
+        copy.start()
     rank = lax.axis_index("seq")
-
-    def ids(position):
-        return table_ref[tile_total, position]
-
-    def mask(query_tile, key_tile):
-        return table_ref[query_tile, key_tile]
-
     for place in range(1, tile_total + 2):
         info_ref[place] = 0
-    for tile in range(tile_total):
-        users = mask(0, tile)
-        for other in range(1, tile_total):
-            users = users + mask(other, tile)
-        any_ref[tile] = users
+    ids = [table_ref[1, position] for position in range(tile_total)]
+    rows = [table_ref[0, tile] for tile in ids]
+    wants = [
+        functools.reduce(jnp.bitwise_or, rows[first : first + tiles])
+        for first in range(0, tile_total, tiles)
+    ]
+    before, behind = [jnp.int32(0)], [jnp.int32(0)]
+    for want in wants:
+        before.append(before[-1] | want)
+    for want in wants[::-1]:
+        behind.append(behind[-1] | want)
+    behind = behind[::-1]
     count = jnp.int32(0)
     for position in range(tile_total):
-        key_tile = ids(position)
-        away = any_ref[key_tile]
-        for local in range(tiles):
-            away = away - mask(ids(position // tiles * tiles + local), key_tile)
+        home = position // tiles
+        wanted = ((before[home] | behind[home + 1]) >> ids[position]) & 1
         info_ref[1 + count] = position
-        info_ref[tile_total + 2 + position] = jnp.where(away > 0, count, -1)
-        count = count + jnp.where(away > 0, 1, 0)
+        info_ref[tile_total + 2 + position] = jnp.where(wanted == 1, count, -1)
+        count = count + wanted
     info_ref[0] = count
-    my_tiles = [ids(rank * tiles + b) for b in range(tiles)]
+    my_tiles = [table_ref[1, rank * tiles + b] for b in range(tiles)]
+    my_rows = [table_ref[0, tile] for tile in my_tiles]
     place = 2 * tile_total + 2
     for slot in range(slots):
         position = info_ref[1 + slot]
         usable = ((slot < count) & (position // tiles != rank)).astype(jnp.int32)
         for b in range(tiles):
-            info_ref[place] = usable * mask(my_tiles[b], ids(position))
+            info_ref[place] = usable & (my_rows[b] >> table_ref[1, position])
             place += 1
     for a in range(tiles):
         for b in range(tiles):
-            info_ref[place] = mask(my_tiles[b], my_tiles[a])
+            info_ref[place] = (my_rows[b] >> my_tiles[a]) & 1
             place += 1
+    for copy in copies:
+        copy.wait()
+
 
 def first_kernel(tiles, slots, info_ref, *refs):
     sources, (full_ref, half_ref) = refs[:4], refs[4:]
@@ -368,11 +377,11 @@
         copy.start()
         copy.wait()
 
-        def ids(position):
-            return table_ref[tile_total, position]
+        def seen(query_position, key_position):
+            return (table_ref[0, table_ref[1, query_position]] >> table_ref[1, key_position]) & 1
 
         def allowed(a, b):
-            return table_ref[ids(rank * tiles + b), ids(rank * tiles + a)]
+            return seen(rank * tiles + b, rank * tiles + a)
 
         own_bias(tiles, bias_ref.at[own_rows, :], allowed)
         for source, target in ((key_any, keys_ref), (value_any, values_ref)):
@@ -392,9 +401,8 @@
                 position = info_ref[1 + listed]
                 usable = (listed < needed) & (position // tiles != rank)
                 for b in range(tiles):
-                    seen = table_ref[ids(rank * tiles + b), ids(position)] == 1
                     bias_ref[tile_rows(first_row, slot), pl.ds(b * TILE, TILE)] = block_bias(
-                        usable & seen
+                        usable & (seen(rank * tiles + b, position) == 1)
                     )
             return carry
 
@@ -588,25 +596,31 @@
             total = total + value.astype(f32)
         return total.astype(bf16)
 
-    table = jnp.pad(tile_mask, ((0, 1), (0, 0)))
-    table = table + jnp.pad(tile_ids[None], ((tile_total, 0), (0, 0)))
+    assert tile_total <= 32
+    bits = jnp.where(tile_mask == 1, 1 << jnp.arange(tile_total, dtype=jnp.int32), 0)
+    table = jnp.stack([jnp.sum(bits, axis=1, dtype=jnp.int32), tile_ids])
     key_other, value_other = swap(key_rows, 1), swap(value_rows, 1)
     chip_rows = (key_rows, value_rows, key_other, value_other)
-    info, spare = call(
+    info, spare, key_here, value_here = call(
         functools.partial(list_kernel, tile_total, tiles, slots),
-        [SMEM_SPEC],
-        (shape((info_size(tile_total, tiles, slots),), jnp.int32), shape(buffer, bf16)),
-        (SMEM_SPEC, ANY_SPEC),
-        scratch=(pltpu.SMEM((tile_total,), jnp.int32),),
+        [SMEM_SPEC] + [ANY_SPEC] * 2,
+        (
+            shape((info_size(tile_total, tiles, slots),), jnp.int32),
+            shape(buffer, bf16),
+            shape(key_rows.shape, bf16),
+            shape(value_rows.shape, bf16),
+        ),
+        (SMEM_SPEC, ANY_SPEC, VMEM_SPEC, VMEM_SPEC),
+        scratch=(pltpu.SemaphoreType.DMA, pltpu.SemaphoreType.DMA),
         moved=4 * 1024 * 1024,
-    )(table)
+    )(table, key_rows, value_rows)
     chosen, chosen_half = call(
         functools.partial(first_kernel, tiles, slots),
         [SMEM_SPEC] + [VMEM_SPEC] * 4,
         (shape((2 * slots, TILE, HD), bf16), shape(slot_shape, bf16)),
         (VMEM_SPEC,) * 2,
         moved=5 * row_count * HD * 2,
-    )(info, *chip_rows)
+    )(info, key_here, value_here, key_other, value_other)
     used = (info[0] + slots - 1) // slots
 
     def select(index):

time: 31.7 us -> 32.5 us (1.025)
  other arithmetic: 0.76 us -> 1.53 us
  waiting for transfers between devices: 5.37 us -> 5.76 us
    reduce_sum x0 -> x1, other arithmetic: none -> 0.81 us  [per_device(): table = jnp.stack([jnp.sum(bits, axis=1, dtype=jnp.int32), tile_ids])]
    add x1 -> x0, other arithmetic: 0.7 us -> none  [per_device(): table = table + jnp.pad(tile_ids[None], ((tile_total, 0), (0, 0)))]
    another operation x0 -> x1, other arithmetic: none -> 0.67 us  [per_device(): table = jnp.stack([jnp.sum(bits, axis=1, dtype=jnp.int32), tile_ids])]
    pallas_call x1, Pallas kernels: 1.61 us -> 2.03 us  [per_device(): call(functools.partial(list_kernel, tile_total, tiles, slots), [SMEM_SPEC...]
    ppermute x9, waiting for transfers between devices: 5.37 us -> 5.75 us  [swap(): lax.ppermute(values, 'seq', [(source, source ^ step) for source in range(...]
    pallas_call x1, Pallas kernels: 1.56 us -> 1.18 us  [per_device(): call(functools.partial(own_kernel, tiles, slots, heads, tile_total), [SME...]
    pallas_call x1, Pallas kernels: 0.97 us -> 0.63 us  [per_device(): call(functools.partial(first_kernel, tiles, slots), [SMEM_SPEC] + [VMEM_S...]
    unnamed x16 -> x14, local copies, waits for them, and re-layouts: 1.69 us -> 1.65 us
  transfers between devices with their start and end apart: 11 -> 11, of which waited for: 6 -> 6; matrix products, arithmetic and copies ran while one was open for 2% -> 5% of each run, Pallas kernels for 20% -> 20%
where the time goes in v5:
time: 32.5 us; the launch traced here: 32.3 us
  starting transfers between devices  12.8 us (39%)
  Pallas kernels  9.68 us (30%)
  waiting for transfers between devices  5.76 us (18%)
  local copies, waits for them, and re-layouts  1.65 us (5%)
  other arithmetic  1.53 us (5%)
  between operations  0.85 us (3%)
    ppermute x9, starting transfers between devices, swap(): lax.ppermute(values, 'seq', [(source, source ^ step) for source in range(...  8.68 us
    ppermute x9, waiting for transfers between devices, swap(): lax.ppermute(values, 'seq', [(source, source ^ step) for source in range(...  5.75 us
    ppermute x2, starting transfers between devices, trade(): got.append(lax.ppermute(full, 'seq', routes))  4.11 us
    pallas_call x1, Pallas kernels, per_device(): call(functools.partial(gathered_kernel, chips, tiles, slots, heads, tile_...  2.03 us
    pallas_call x1, Pallas kernels, per_device(): call(functools.partial(list_kernel, tile_total, tiles, slots), [SMEM_SPEC...  2.03 us
    pallas_call x1, Pallas kernels, per_device(): call(functools.partial(queries_kernel, slots, heads), [SMEM_SPEC] + [VMEM...  1.91 us
    unnamed x14, local copies, waits for them, and re-layouts  1.65 us
    pallas_call x1, Pallas kernels, per_device(): call(functools.partial(own_grads_kernel, tiles, slots, heads, tile_total)...  1.32 us
  transfers between devices with their start and end apart: 11, of which 6 were waited for; matrix products, arithmetic and copies ran while one was open for 5% of the time, Pallas kernels for 20%

profile of v5, /device:TPU:0, one launch (start us, length us, event | category | flops | bytes accessed | tf_op | source)
XLA Modules:
  0.0 32.3 jit_solution(785235802314792152)
XLA Ops:
  0.6 0.5 %collective-permute-start.10 = (bf16[256,128]{1,0:T(8,128)(2,1)}, bf16[256,128]{1,0:T(8,128)(2,1)S(1)}, u32[]{:S(2)}, u32[]{:S(2)}) collective-permute-start(bf16[256,128]{1,0:T(8,128)(2,1)} %value_ref.3), channel_id=1, source_target_pairs={{0,4},{4,0},{8,12},{12,8},{16,20},{20,16},{24,28},{28,24},{1,5},{5... | collective-permute-start | bytes 196616 | tf_op jit(solution)/shard_map/ppermute | solution.py:581
  1.2 0.1 collective-permute-start.9
  1.2 0.8 %select_reduce_fusion = s32[16]{0:T(128)S(1)} fusion(s32[16,16]{1,0:T(8,128)} %param.15, s32[16]{0:T(128)S(1)} %iota_shift-left_fusion), kind=kLoop, calls=%fused_computation.11 | loop fusion | flops 752 | bytes 1152 | tf_op jit(solution)/shard_map/reduce_sum | solution.py:601
  2.1 0.7 %pad_add_fusion.table_ref.table_any = s32[2,16]{1,0:T(2,128)S(1)} fusion(s32[1,16]{1,0:T(1,128)} %bitcast.37, s32[1,16]{1,0:T(1,128)S(1)} %bitcast.36), kind=kLoop, calls=%fused_computation.12 | loop fusion | flops 32 | bytes 256 | tf_op jit(solution)/shard_map/stack | solution.py:601
  2.7 2.0 %shard_map.93 = (s32[42]{0:T(128)S(1)}, bf16[7,2,2,128,128]{4,3,2,1,0:T(8,128)(2,1)}, bf16[256,128]{1,0:T(8,128)(2,1)S(1)}, bf16[256,128]{1,0:T(8,128)(2,1)S(1)}) custom-call(s32[2,16]{1,0:T(2,128)S(1)} %pad_add_fusion.table_ref.table_any, bf16[256,128]{1,0:T(8,128)(2,1)} %key_ref.5, bf16[256,128]{1,0:T(8,128)(2,1)} %value_ref.3), custom_call_target="tpu_custom_call" | custom-call | bytes 4194304 | tf_op jit(solution)/shard_map/pallas_call | solution.py:604
  4.8 0.0 copy-start.5
  4.8 0.6 %shard_map.95 = (bf16[4,128,128]{2,1,0:T(8,128)(2,1)S(1)}, bf16[2,128,128]{2,1,0:T(8,128)(2,1)S(1)}) custom-call(s32[42]{0:T(128)S(1)} %get-tuple-element.527.info_ref, bf16[256,128]{1,0:T(8,128)(2,1)S(1)} %get-tuple-element.337.refs_0_, bf16[256,128]{1,0:T(8,128)(2,1)S(1)} %get-tuple-element.338.refs_1_, ...), custom_call_target="tpu_custom_call" | custom-call | bytes 327680 | tf_op jit(solution)/shard_map/pallas_call | solution.py:617
  5.4 3.1 %collective-permute-start.11 = (bf16[4,128,128]{2,1,0:T(8,128)(2,1)S(1)}, bf16[4,128,128]{2,1,0:T(8,128)(2,1)S(1)}, u32[]{:S(2)}, u32[]{:S(2)}) collective-permute-start(bf16[4,128,128]{2,1,0:T(8,128)(2,1)S(1)} %get-tuple-element.339), channel_id=1, source_target_pairs={{0,8},{4,20},{8,0},{12,28},{16,24},{20,4},{24,16},{28,12},{1,9},{5... | collective-permute-start | bytes 393224 | tf_op jit(solution)/shard_map/ppermute | solution.py:590
  8.5 2.5 %collective-permute-start.12 = (bf16[2,128,128]{2,1,0:T(8,128)(2,1)S(1)}, bf16[2,128,128]{2,1,0:T(8,128)(2,1)S(1)}, u32[]{:S(2)}, u32[]{:S(2)}) collective-permute-start(bf16[2,128,128]{2,1,0:T(8,128)(2,1)S(1)} %get-tuple-element.340), channel_id=1, source_target_pairs={{0,24},{4,28},{8,16},{12,20},{16,8},{20,12},{24,0},{28,4},{1,25},{... | collective-permute-start | bytes 196616 | tf_op jit(solution)/shard_map/ppermute | solution.py:581
  11.0 0.9 %copy-done.1 = bf16[256,512]{1,0:T(8,128)(2,1)S(1)} copy-done((bf16[256,512]{1,0:T(8,128)(2,1)S(1)}, bf16[256,512]{1,0:T(8,128)(2,1)}, u32[]{:S(2)}) %copy-start.1) | copy-done | bytes 262168
  11.9 1.2 %shard_map.94 = (f32[1,1024]{1,0:T(1,128)S(1)}, f32[1,1024]{1,0:T(1,128)S(1)}, f32[128,1024]{1,0:T(8,128)S(1)}, bf16[128,1024]{1,0:T(8,128)(2,1)S(1)}) custom-call(s32[42]{0:T(128)S(1)} %get-tuple-element.527.info_ref, bf16[256,512]{1,0:T(8,128)(2,1)S(1)} %copy-done, bf16[256,512]{1,0:T(8,128)(2,1)S(1)} %copy-done.1, bf16[256,128]{1,0:T(8,128)(2,1)S(1)} %copy-done.6, ...), custom_call_target="tpu_custom_call" | custom-call | flops 1610612736 | bytes 524288 | tf_op jit(solution)/shard_map/pallas_call | solution.py:650
  13.2 2.6 %collective-permute-done.12.refs_1_ = bf16[2,128,128]{2,1,0:T(8,128)(2,1)S(1)} collective-permute-done((bf16[2,128,128]{2,1,0:T(8,128)(2,1)S(1)}, bf16[2,128,128]{2,1,0:T(8,128)(2,1)S(1)}, u32[]{:S(2)}, u32[]{:S(2)}) %collective-permute-start.12) | collective-permute-done | bytes 65568 | tf_op jit(solution)/shard_map/ppermute | solution.py:581
  15.8 0.5 %collective-permute-start.13 = (bf16[4,128,128]{2,1,0:T(8,128)(2,1)S(1)}, bf16[4,128,128]{2,1,0:T(8,128)(2,1)S(1)}, u32[]{:S(2)}, u32[]{:S(2)}) collective-permute-start(bf16[4,128,128]{2,1,0:T(8,128)(2,1)S(1)} %collective-permute-done.11.refs_0_), channel_id=1, source_target_pairs={{0,4},{4,0},{8,12},{12,8},{16,20},{20,16},{24,28},{28,24},{1,5},{5... | collective-permute-start | bytes 393224 | tf_op jit(solution)/shard_map/ppermute | solution.py:581
  16.3 0.7 %collective-permute-done.14.refs_3_ = bf16[2,128,128]{2,1,0:T(8,128)(2,1)S(1)} collective-permute-done((bf16[2,128,128]{2,1,0:T(8,128)(2,1)S(1)}, bf16[2,128,128]{2,1,0:T(8,128)(2,1)S(1)}, u32[]{:S(2)}, u32[]{:S(2)}) %collective-permute-start.14) | collective-permute-done | bytes 65568 | tf_op jit(solution)/shard_map/ppermute | solution.py:581
  17.1 0.2 collective-permute-done.13.refs_2_
  17.3 2.0 %shard_map.96 = (bf16[4,128,128]{2,1,0:T(8,128)(2,1)S(1)}, f32[1,1024]{1,0:T(1,128)S(1)}, f32[1,1024]{1,0:T(1,128)S(1)}, f32[1,1024]{1,0:T(1,128)S(1)}, bf16[128...) custom-call(s32[42]{0:T(128)S(1)} %get-tuple-element.599, ...), custom_call_target="tpu_custom_call" | custom-call | flops 1610612736 | bytes 524288 | tf_op jit(solution)/shard_map/pallas_call | solution.py:666
  19.4 0.0 copy-start.2
  19.4 0.4 %collective-permute-start.15 = (bf16[4,128,128]{2,1,0:T(8,128)(2,1)S(1)}, bf16[4,128,128]{2,1,0:T(8,128)(2,1)S(1)}, u32[]{:S(2)}, u32[]{:S(2)}) collective-permute-start(bf16[4,128,128]{2,1,0:T(8,128)(2,1)S(1)} %get-tuple-element.346), channel_id=1, source_target_pairs={{0,4},{4,0},{8,12},{12,8},{16,20},{20,16},{24,28},{28,24},{1,5},{5... | collective-permute-start | bytes 393224 | tf_op jit(solution)/shard_map/ppermute | solution.py:581
  19.8 1.0 %collective-permute-done.15 = bf16[4,128,128]{2,1,0:T(8,128)(2,1)S(1)} collective-permute-done((bf16[4,128,128]{2,1,0:T(8,128)(2,1)S(1)}, bf16[4,128,128]{2,1,0:T(8,128)(2,1)S(1)}, u32[]{:S(2)}, u32[]{:S(2)}) %collective-permute-start.15) | collective-permute-done | bytes 131104 | tf_op jit(solution)/shard_map/ppermute | solution.py:581
  20.9 1.0 %collective-permute-start.16 = (bf16[4,128,128]{2,1,0:T(8,128)(2,1)S(1)}, bf16[4,128,128]{2,1,0:T(8,128)(2,1)S(1)}, u32[]{:S(2)}, u32[]{:S(2)}) collective-permute-start(bf16[4,128,128]{2,1,0:T(8,128)(2,1)S(1)} %pad_maximum_fusion.refs_2_), channel_id=1, source_target_pairs={{0,8},{4,20},{8,0},{12,28},{16,24},{20,4},{24,16},{28,12},{1,9},{5... | collective-permute-start | bytes 393224 | tf_op jit(solution)/shard_map/ppermute | solution.py:590
  21.9 1.3 %shard_map.97 = (bf16[256,1024]{1,0:T(8,128)(2,1)S(1)}, f32[256,128]{1,0:T(8,128)S(1)}, f32[256,128]{1,0:T(8,128)S(1)}, bf16[2,128,128]{2,1,0:T(8,128)(2,1)S(1)}) custom-call(s32[42]{0:T(128)S(1)} %get-tuple-element.599, bf16[256,512]{1,0:T(8,128)(2,1)S(1)} %copy-done, bf16[256,512]{1,0:T(8,128)(2,1)S(1)} %copy-done.2, ...), custom_call_target="tpu_custom_call", output_to_operand_aliasing={{3}: (10, {})} | custom-call | flops 1207959552 | bytes 524288 | tf_op jit(solution)/shard_map/pallas_call | solution.py:717
  23.2 3.2 %collective-permute-start.17 = (bf16[2,128,128]{2,1,0:T(8,128)(2,1)S(1)}, bf16[2,128,128]{2,1,0:T(8,128)(2,1)S(1)}, u32[]{:S(2)}, u32[]{:S(2)}) collective-permute-start(bf16[2,128,128]{2,1,0:T(8,128)(2,1)S(1)} %get-tuple-element.358), channel_id=1, source_target_pairs={{0,24},{4,28},{8,16},{12,20},{16,8},{20,12},{24,0},{28,4},{1,25},{... | collective-permute-start | bytes 196616 | tf_op jit(solution)/shard_map/ppermute | solution.py:581
  26.4 1.9 %shard_map.98 = (bf16[256,512]{1,0:T(8,128)(2,1)}, f32[256,512]{1,0:T(8,128)}, bf16[4,128,128]{2,1,0:T(8,128)(2,1)S(1)}) custom-call(s32[42]{0:T(128)S(1)} %get-tuple-element.599, bf16[256,128]{1,0:T(8,128)(2,1)S(1)} %get-tuple-element.584, bf16[256,1024]{1,0:T(8,128)(2,1)S(1)} %get-tuple-element.347.own_dscores, ...), custom_call_target="tpu_custom_call", output_to_operand_aliasing={{2}: (8, {})} | custom-call | flops 1073741824 | bytes 1048576 | tf_op jit(solution)/shard_map/pallas_call | solution.py:739
  28.3 1.2 %collective-permute-start.18 = (bf16[4,128,128]{2,1,0:T(8,128)(2,1)S(1)}, bf16[4,128,128]{2,1,0:T(8,128)(2,1)S(1)}, u32[]{:S(2)}, u32[]{:S(2)}) collective-permute-start(bf16[4,128,128]{2,1,0:T(8,128)(2,1)S(1)} %get-tuple-element.357.refs_3_), channel_id=1, source_target_pairs={{0,4},{4,0},{8,12},{12,8},{16,20},{20,16},{24,28},{28,24},{1,5},{5... | collective-permute-start | bytes 393224 | tf_op jit(solution)/shard_map/ppermute | solution.py:581
  29.6 0.2 collective-permute-done.17.refs_4_
  29.7 0.3 collective-permute-start.19
  30.0 1.0 %collective-permute-done.19.refs_6_ = bf16[2,128,128]{2,1,0:T(8,128)(2,1)S(1)} collective-permute-done((bf16[2,128,128]{2,1,0:T(8,128)(2,1)S(1)}, bf16[2,128,128]{2,1,0:T(8,128)(2,1)S(1)}, u32[]{:S(2)}, u32[]{:S(2)}) %collective-permute-start.19) | collective-permute-done | bytes 65568 | tf_op jit(solution)/shard_map/ppermute | solution.py:581
  31.0 0.6 %shard_map.99 = (f32[256,128]{1,0:T(8,128)S(1)}, f32[256,128]{1,0:T(8,128)S(1)}) custom-call(s32[42]{0:T(128)S(1)} %get-tuple-element.599, f32[256,128]{1,0:T(8,128)S(1)} %get-tuple-element.355.refs_0_, f32[256,128]{1,0:T(8,128)S(1)} %get-tuple-element.356.refs_1_, bf16[4,128,128]{2,1,0:T(8,128)(2,1)S(1)} %pad_maximum_fusion.refs_2_, ...), custom_call_target="tpu_custom_call" | custom-call | bytes 655360 | tf_op jit(solution)/shard_map/pallas_call | solution.py:752
  31.6 0.0 copy-start.3
  31.6 0.0 copy-start.4
  31.6 0.6 %copy-done.3 = f32[256,128]{1,0:T(8,128)} copy-done((f32[256,128]{1,0:T(8,128)}, f32[256,128]{1,0:T(8,128)S(1)}, u32[]{:S(2)}) %copy-start.3) | copy-done | bytes 131096
  32.2 0.0 copy-done.4
  (18 shorter events, 0.1 us)
Async XLA Ops:
  0.6 10.4 %copy-start = (bf16[256,512]{1,0:T(8,128)(2,1)S(1)}, bf16[256,512]{1,0:T(8,128)(2,1)}, u32[]{:S(2)}) copy-start(bf16[256,512]{1,0:T(8,128)(2,1)} %query_ref.5) | copy-start | bytes 786436
  0.6 4.1 %collective-permute-start.10 = (bf16[256,128]{1,0:T(8,128)(2,1)}, bf16[256,128]{1,0:T(8,128)(2,1)S(1)}, u32[]{:S(2)}, u32[]{:S(2)}) collective-permute-start(bf16[256,128]{1,0:T(8,128)(2,1)} %value_ref.3), channel_id=1, source_target_pairs={{0,4},{4,0},{8,12},{12,8},{16,20},{20,16},{24,28},{28,24},{1,5},{5... | collective-permute-start | bytes 196616 | tf_op jit(solution)/shard_map/ppermute | solution.py:581
  1.2 3.6 %collective-permute-start.9 = (bf16[256,128]{1,0:T(8,128)(2,1)}, bf16[256,128]{1,0:T(8,128)(2,1)S(1)}, u32[]{:S(2)}, u32[]{:S(2)}) collective-permute-start(bf16[256,128]{1,0:T(8,128)(2,1)} %key_ref.5), channel_id=1, source_target_pairs={{0,4},{4,0},{8,12},{12,8},{16,20},{20,16},{24,28},{28,24},{1,5},{5... | collective-permute-start | bytes 196616 | tf_op jit(solution)/shard_map/ppermute | solution.py:581
  4.8 6.2 %copy-start.5 = (bf16[256,128]{1,0:T(8,128)(2,1)S(1)}, bf16[256,128]{1,0:T(8,128)(2,1)}, u32[]{:S(2)}) copy-start(bf16[256,128]{1,0:T(8,128)(2,1)} %value_ref.3) | copy-start | bytes 196612
  4.8 6.2 %copy-start.6 = (bf16[256,128]{1,0:T(8,128)(2,1)S(1)}, bf16[256,128]{1,0:T(8,128)(2,1)}, u32[]{:S(2)}) copy-start(bf16[256,128]{1,0:T(8,128)(2,1)} %key_ref.5) | copy-start | bytes 196612
  5.4 10.4 %collective-permute-start.11 = (bf16[4,128,128]{2,1,0:T(8,128)(2,1)S(1)}, bf16[4,128,128]{2,1,0:T(8,128)(2,1)S(1)}, u32[]{:S(2)}, u32[]{:S(2)}) collective-permute-start(bf16[4,128,128]{2,1,0:T(8,128)(2,1)S(1)} %get-tuple-element.339), channel_id=1, source_target_pairs={{0,8},{4,20},{8,0},{12,28},{16,24},{20,4},{24,16},{28,12},{1,9},{5... | collective-permute-start | bytes 393224 | tf_op jit(solution)/shard_map/ppermute | solution.py:590
  8.5 7.3 %collective-permute-start.12 = (bf16[2,128,128]{2,1,0:T(8,128)(2,1)S(1)}, bf16[2,128,128]{2,1,0:T(8,128)(2,1)S(1)}, u32[]{:S(2)}, u32[]{:S(2)}) collective-permute-start(bf16[2,128,128]{2,1,0:T(8,128)(2,1)S(1)} %get-tuple-element.340), channel_id=1, source_target_pairs={{0,24},{4,28},{8,16},{12,20},{16,8},{20,12},{24,0},{28,4},{1,25},{... | collective-permute-start | bytes 196616 | tf_op jit(solution)/shard_map/ppermute | solution.py:581
  11.0 1.0 %copy-start.1 = (bf16[256,512]{1,0:T(8,128)(2,1)S(1)}, bf16[256,512]{1,0:T(8,128)(2,1)}, u32[]{:S(2)}) copy-start(bf16[256,512]{1,0:T(8,128)(2,1)} %grad_ref.5) | copy-start | bytes 786436
  15.8 1.3 %collective-permute-start.14 = (bf16[2,128,128]{2,1,0:T(8,128)(2,1)S(1)}, bf16[2,128,128]{2,1,0:T(8,128)(2,1)S(1)}, u32[]{:S(2)}, u32[]{:S(2)}) collective-permute-start(bf16[2,128,128]{2,1,0:T(8,128)(2,1)S(1)} %collective-permute-done.12.refs_1_), channel_id=1, source_target_pairs={{0,4},{4,0},{8,12},{12,8},{16,20},{20,16},{24,28},{28,24},{1,5},{5... | collective-permute-start | bytes 196616 | tf_op jit(solution)/shard_map/ppermute | solution.py:581
  15.8 1.5 %collective-permute-start.13 = (bf16[4,128,128]{2,1,0:T(8,128)(2,1)S(1)}, bf16[4,128,128]{2,1,0:T(8,128)(2,1)S(1)}, u32[]{:S(2)}, u32[]{:S(2)}) collective-permute-start(bf16[4,128,128]{2,1,0:T(8,128)(2,1)S(1)} %collective-permute-done.11.refs_0_), channel_id=1, source_target_pairs={{0,4},{4,0},{8,12},{12,8},{16,20},{20,16},{24,28},{28,24},{1,5},{5... | collective-permute-start | bytes 393224 | tf_op jit(solution)/shard_map/ppermute | solution.py:581
  19.4 2.5 %copy-start.2 = (bf16[256,512]{1,0:T(8,128)(2,1)S(1)}, bf16[256,512]{1,0:T(8,128)(2,1)}, u32[]{:S(2)}) copy-start(bf16[256,512]{1,0:T(8,128)(2,1)} %grad_ref.5) | copy-start | bytes 786436
  19.4 1.4 %collective-permute-start.15 = (bf16[4,128,128]{2,1,0:T(8,128)(2,1)S(1)}, bf16[4,128,128]{2,1,0:T(8,128)(2,1)S(1)}, u32[]{:S(2)}, u32[]{:S(2)}) collective-permute-start(bf16[4,128,128]{2,1,0:T(8,128)(2,1)S(1)} %get-tuple-element.346), channel_id=1, source_target_pairs={{0,4},{4,0},{8,12},{12,8},{16,20},{20,16},{24,28},{28,24},{1,5},{5... | collective-permute-start | bytes 393224 | tf_op jit(solution)/shard_map/ppermute | solution.py:581
  20.9 5.5 %collective-permute-start.16 = (bf16[4,128,128]{2,1,0:T(8,128)(2,1)S(1)}, bf16[4,128,128]{2,1,0:T(8,128)(2,1)S(1)}, u32[]{:S(2)}, u32[]{:S(2)}) collective-permute-start(bf16[4,128,128]{2,1,0:T(8,128)(2,1)S(1)} %pad_maximum_fusion.refs_2_), channel_id=1, source_target_pairs={{0,8},{4,20},{8,0},{12,28},{16,24},{20,4},{24,16},{28,12},{1,9},{5... | collective-permute-start | bytes 393224 | tf_op jit(solution)/shard_map/ppermute | solution.py:590
  23.2 6.5 %collective-permute-start.17 = (bf16[2,128,128]{2,1,0:T(8,128)(2,1)S(1)}, bf16[2,128,128]{2,1,0:T(8,128)(2,1)S(1)}, u32[]{:S(2)}, u32[]{:S(2)}) collective-permute-start(bf16[2,128,128]{2,1,0:T(8,128)(2,1)S(1)} %get-tuple-element.358), channel_id=1, source_target_pairs={{0,24},{4,28},{8,16},{12,20},{16,8},{20,12},{24,0},{28,4},{1,25},{... | collective-permute-start | bytes 196616 | tf_op jit(solution)/shard_map/ppermute | solution.py:581
  28.3 2.7 %collective-permute-start.18 = (bf16[4,128,128]{2,1,0:T(8,128)(2,1)S(1)}, bf16[4,128,128]{2,1,0:T(8,128)(2,1)S(1)}, u32[]{:S(2)}, u32[]{:S(2)}) collective-permute-start(bf16[4,128,128]{2,1,0:T(8,128)(2,1)S(1)} %get-tuple-element.357.refs_3_), channel_id=1, source_target_pairs={{0,4},{4,0},{8,12},{12,8},{16,20},{20,16},{24,28},{28,24},{1,5},{5... | collective-permute-start | bytes 393224 | tf_op jit(solution)/shard_map/ppermute | solution.py:581
  29.7 1.3 %collective-permute-start.19 = (bf16[2,128,128]{2,1,0:T(8,128)(2,1)S(1)}, bf16[2,128,128]{2,1,0:T(8,128)(2,1)S(1)}, u32[]{:S(2)}, u32[]{:S(2)}) collective-permute-start(bf16[2,128,128]{2,1,0:T(8,128)(2,1)S(1)} %collective-permute-done.17.refs_4_), channel_id=1, source_target_pairs={{0,4},{4,0},{8,12},{12,8},{16,20},{20,16},{24,28},{28,24},{1,5},{5... | collective-permute-start | bytes 196616 | tf_op jit(solution)/shard_map/ppermute | solution.py:581
  31.6 0.7 %copy-start.3 = (f32[256,128]{1,0:T(8,128)}, f32[256,128]{1,0:T(8,128)S(1)}, u32[]{:S(2)}) copy-start(f32[256,128]{1,0:T(8,128)S(1)} %get-tuple-element.328) | copy-start | bytes 393220
  31.6 0.7 %copy-start.4 = (f32[256,128]{1,0:T(8,128)}, f32[256,128]{1,0:T(8,128)S(1)}, u32[]{:S(2)}) copy-start(f32[256,128]{1,0:T(8,128)S(1)} %get-tuple-element.329) | copy-start | bytes 393220

commit v6 on v4

--- a/solution.py
+++ b/solution.py
@@ -45,8 +45,8 @@
     return [(step, step + 1) for step in range(1, chips - 1, 2)]
 
 
-def list_kernel(tile_total, tiles, slots, table_ref, info_ref, spare_ref, any_ref):
-    del spare_ref
+def list_kernel(tile_total, tiles, slots, table_ref, info_ref, spare_ref, spare_sums_ref, any_ref):
+    del spare_ref, spare_sums_ref
     rank = lax.axis_index("seq")
 
     def ids(position):
@@ -122,51 +122,50 @@
             pick(tiles, slots, round_ref[0] * slots, info_ref, own, other, out_ref)
 
 
-def add_sums(tiles, slots, tile_total, base, info_ref, grads, outs, sums_of):
+def close_kernel(tiles, slots, chips, tile_total, info_ref, extra_ref, *refs):
+    grads, (chip_ref, *sums) = refs[:2], refs[2:-8]
+    outs, staged_ref, late_ref, sems = refs[-6:-4], refs[-4], refs[-3], refs[-2:]
+    half = len(sums) // 2
+    arrived, handed = sums[:half], sums[half:]
     rank = lax.axis_index("seq")
     odd = rank % 2
-    for grad, out in zip(grads, outs):
-        out[...] = grad[...]
+
+    def total_of(part, slot):
+        total = chip_ref[part * slots + slot].astype(jnp.float32)
+        for own, other in zip(arrived[:-1], handed[:-1]):
+            total = total + own[part * slots + slot].astype(jnp.float32)
+            total = total + other[(1 - part) * slots + slot].astype(jnp.float32)
+        return total + (handed if part else arrived)[-1][slot].astype(jnp.float32)
+
     for tile in range(tiles):
-        slot = info_ref[tile_total + 2 + rank * tiles + tile] - base
-        rows = tile_rows(0, tile)
+        slot = info_ref[tile_total + 2 + rank * tiles + tile]
+        rows = pl.ds(tile * TILE, TILE)
+
+        def place(totals):
+            copies = []
+            for kind in range(2):
+                total = jnp.where(odd == kind, totals[0], totals[1])
+                staged_ref[kind] = grads[kind][rows, :] + total
+                copies.append(
+                    pltpu.make_async_copy(staged_ref.at[kind], outs[kind].at[rows, :], sems[kind])
+                )
+            for copy in copies:
+                copy.start()
+            for copy in copies:
+                copy.wait()
 
         @pl.when((slot >= 0) & (slot < slots))
         def _():
-            totals = []
+            place([total_of(part, slot) for part in range(2)])
+
+        @pl.when(slot >= slots)
+        def _():
             for part in range(2):
-                total = None
-                for source in sums_of(part, slot):
-                    source = source.astype(jnp.float32)
-                    total = source if total is None else total + source
-                totals.append(total)
-            for kind, out in enumerate(outs):
-                out[rows, :] += jnp.where(odd == kind, totals[0], totals[1])
-
-
-def close_kernel(tiles, slots, chips, tile_total, info_ref, *refs):
-    grads, (chip_ref, *sums), outs = refs[:2], refs[2:-2], refs[-2:]
-    half = len(sums) // 2
-    arrived, handed = sums[:half], sums[half:]
-
-    def sums_of(part, slot):
-        yield chip_ref[part * slots + slot]
-        for own, other in zip(arrived[:-1], handed[:-1]):
-            yield own[part * slots + slot]
-            yield other[(1 - part) * slots + slot]
-        yield (handed if part else arrived)[-1][slot]
-
-    add_sums(tiles, slots, tile_total, 0, info_ref, grads, outs, sums_of)
-
-
-def later_kernel(tiles, slots, tile_total, info_ref, round_ref, *refs):
-    grads, sums, outs = refs[:2], refs[2:-2], refs[-2:]
-
-    def sums_of(part, slot):
-        yield sums[part][slot]
-
-    base = round_ref[0] * slots
-    add_sums(tiles, slots, tile_total, base, info_ref, grads, outs, sums_of)
+                source = extra_ref.at[slot // slots - 1, part, slot % slots]
+                copy = pltpu.make_async_copy(source, late_ref.at[part], sems[part])
+                copy.start()
+                copy.wait()
+            place([late_ref[part].astype(jnp.float32) for part in range(2)])
 
 
 def causal_bias():
@@ -531,13 +530,10 @@
     out_t_ref,
     attended_full,
     query_full,
-    order_ref,
     attended_ref,
     query_out,
-    order_out,
     copy_sem,
 ):
-    del order_ref, order_out
     rows = query_out.shape[0]
 
     @pl.when(info_ref[0] <= slots)
@@ -552,6 +548,17 @@
     @pl.when(info_ref[0] > slots)
     def _():
         fetch_full(copy_sem, (attended_full, attended_ref), (query_full, query_out))
+
+
+def place_kernel(key_own, value_own, key_placed, value_placed, key_sem, value_sem):
+    copies = [
+        pltpu.make_async_copy(key_own, key_placed, key_sem),
+        pltpu.make_async_copy(value_own, value_placed, value_sem),
+    ]
+    for copy in copies:
+        copy.start()
+    for copy in copies:
+        copy.wait()
 
 
 def per_device(queries, key_rows, value_rows, out_grad, tile_ids, tile_mask):
@@ -592,11 +599,15 @@
     table = table + jnp.pad(tile_ids[None], ((tile_total, 0), (0, 0)))
     key_other, value_other = swap(key_rows, 1), swap(value_rows, 1)
     chip_rows = (key_rows, value_rows, key_other, value_other)
-    info, spare = call(
+    info, spare, spare_sums = call(
         functools.partial(list_kernel, tile_total, tiles, slots),
         [SMEM_SPEC],
-        (shape((info_size(tile_total, tiles, slots),), jnp.int32), shape(buffer, bf16)),
-        (SMEM_SPEC, ANY_SPEC),
+        (
+            shape((info_size(tile_total, tiles, slots),), jnp.int32),
+            shape(buffer, bf16),
+            shape(buffer, bf16),
+        ),
+        (SMEM_SPEC, ANY_SPEC, ANY_SPEC),
         scratch=(pltpu.SMEM((tile_total,), jnp.int32),),
         moved=4 * 1024 * 1024,
     )(table)
@@ -722,37 +733,55 @@
         half_sum,
     )
     back = trade(chip_sum, half_sum)
-    attended, query_grad, back[0] = call(
+    key_placed, value_placed = call(
+        place_kernel,
+        [VMEM_SPEC] * 2,
+        tuple(full[2:]),
+        (ANY_SPEC,) * 2,
+        scratch=(pltpu.SemaphoreType.DMA,) * 2,
+        moved=2 * 1024 * 1024,
+    )(key_own, value_own)
+    attended, query_grad = call(
         functools.partial(queries_kernel, slots, heads),
-        [SMEM_SPEC] + [VMEM_SPEC] * 5 + [ANY_SPEC] * 3,
-        (*full[:2], shape(back[0].shape, bf16)),
-        (VMEM_SPEC,) * 2 + (ANY_SPEC,),
+        [SMEM_SPEC] + [VMEM_SPEC] * 5 + [ANY_SPEC] * 2,
+        full[:2],
+        (VMEM_SPEC,) * 2,
         scratch=(pltpu.SemaphoreType.DMA,),
         flops=16 * work,
         moved=8 * row_count * heads * HD,
-        aliases={8: 2},
-    )(info, key_rows, own_dscores, dscores, slot_keys, out_t, *full_values[:2], back[0])
+    )(
+        info,
+        key_rows,
+        own_dscores,
+        dscores,
+        slot_keys,
+        out_t,
+        *full_values[:2],
+    )
     sums = [chip_sum] + back + [swap(values, 1) for values in back]
 
-    def close(kernel, lead, grads, sums):
-        return call(
-            kernel,
-            [SMEM_SPEC] * len(lead) + [VMEM_SPEC] * (2 + len(sums)),
-            (shape(key_rows.shape, f32), shape(value_rows.shape, f32)),
-            (VMEM_SPEC,) * 2,
-            moved=5 * row_count * HD * 4,
-        )(*lead, *grads, *sums)
-
-    def reduce_more(index, grads):
+    def reduce_more(index, totals):
         terms = lax.dynamic_index_in_dim(more_terms, index - 1, 0, keepdims=False)
         part = add(terms[0], swap(terms[1], 1))
         total = add(part, *across(part))
-        kernel = functools.partial(later_kernel, tiles, slots, tile_total)
-        return tuple(close(kernel, (info, index.reshape(1)), grads, (total, swap(total, 1))))
-
-    kernel = functools.partial(close_kernel, tiles, slots, chips, tile_total)
-    grads = tuple(close(kernel, (info,), (key_own, value_own), sums))
-    key_grad, value_grad = lax.fori_loop(1, used, reduce_more, grads)
+        pair = jnp.stack([total, swap(total, 1)])
+        return lax.dynamic_update_index_in_dim(totals, pair, index - 1, 0)
+
+    extra = lax.fori_loop(1, used, reduce_more, spare_sums)
+    key_grad, value_grad = call(
+        functools.partial(close_kernel, tiles, slots, chips, tile_total),
+        [SMEM_SPEC, ANY_SPEC] + [VMEM_SPEC] * (2 + len(sums)) + [ANY_SPEC] * 2,
+        tuple(full[2:]),
+        (ANY_SPEC,) * 2,
+        scratch=(
+            pltpu.VMEM((2, TILE, HD), f32),
+            pltpu.VMEM((2, TILE, HD), bf16),
+            pltpu.SemaphoreType.DMA,
+            pltpu.SemaphoreType.DMA,
+        ),
+        moved=5 * row_count * HD * 4,
+        aliases={4 + len(sums): 0, 5 + len(sums): 1},
+    )(info, extra, key_own, value_own, *sums, key_placed, value_placed)
     return attended, query_grad, key_grad, value_grad
 
 

time: 31.7 us -> 33.1 us (1.044)
  Pallas kernels: 9.97 us -> 11.1 us
  starting transfers between devices: 12.8 us -> 11.7 us
  local copies, waits for them, and re-layouts: 1.69 us -> 2.33 us
  waiting for transfers between devices: 5.37 us -> 6 us
    ppermute x9, starting transfers between devices: 8.65 us -> 7.6 us  [swap(): lax.ppermute(values, 'seq', [(source, source ^ step) for source in range(...]
    pallas_call x1 -> x2, Pallas kernels: 0.57 us -> 1.31 us  [the longest x1 0.71 us: per_device(): call(place_kernel, [VMEM_SPEC] * 2, tuple(full[2:]), (ANY_SPEC,) * 2, scr...]
    unnamed x16 -> x24, local copies, waits for them, and re-layouts: 1.69 us -> 2.33 us
    ppermute x9, waiting for transfers between devices: 5.37 us -> 5.99 us  [swap(): lax.ppermute(values, 'seq', [(source, source ^ step) for source in range(...]
    pallas_call x1, Pallas kernels: 2.01 us -> 2.37 us  [per_device(): call(functools.partial(gathered_kernel, chips, tiles, slots, heads, tile_...]
  transfers between devices with their start and end apart: 11 -> 11, of which waited for: 6 -> 7; matrix products, arithmetic and copies ran while one was open for 2% -> 2% of each run, Pallas kernels for 20% -> 22%
where the time goes in v6:
time: 33.1 us; the launch traced here: 32.8 us
  starting transfers between devices  11.7 us (35%)
  Pallas kernels  11.1 us (34%)
  waiting for transfers between devices  6 us (18%)
  local copies, waits for them, and re-layouts  2.33 us (7%)
  between operations  0.84 us (3%)
  other arithmetic  0.75 us (2%)
    ppermute x9, starting transfers between devices, swap(): lax.ppermute(values, 'seq', [(source, source ^ step) for source in range(...  7.6 us
    ppermute x9, waiting for transfers between devices, swap(): lax.ppermute(values, 'seq', [(source, source ^ step) for source in range(...  5.99 us
    ppermute x2, starting transfers between devices, trade(): got.append(lax.ppermute(full, 'seq', routes))  4.14 us
    pallas_call x1, Pallas kernels, per_device(): call(functools.partial(gathered_kernel, chips, tiles, slots, heads, tile_...  2.37 us
    unnamed x24, local copies, waits for them, and re-layouts  2.33 us
    pallas_call x1, Pallas kernels, per_device(): call(functools.partial(queries_kernel, slots, heads), [SMEM_SPEC] + [VMEM...  1.91 us
    pallas_call x1, Pallas kernels, per_device(): call(functools.partial(list_kernel, tile_total, tiles, slots), [SMEM_SPEC...  1.61 us
    pallas_call x1, Pallas kernels, per_device(): call(functools.partial(own_kernel, tiles, slots, heads, tile_total), [SME...  1.56 us
  transfers between devices with their start and end apart: 11, of which 7 were waited for; matrix products, arithmetic and copies ran while one was open for 2% of the time, Pallas kernels for 22%

profile of v6, /device:TPU:0, one launch (start us, length us, event | category | flops | bytes accessed | tf_op | source)
XLA Modules:
  0.0 32.8 jit_solution(6627087522320577434)
XLA Ops:
  0.7 0.5 %collective-permute-start.10 = (bf16[256,128]{1,0:T(8,128)(2,1)}, bf16[256,128]{1,0:T(8,128)(2,1)}, u32[]{:S(2)}, u32[]{:S(2)}) collective-permute-start(bf16[256,128]{1,0:T(8,128)(2,1)} %value_ref.3), channel_id=1, source_target_pairs={{0,4},{4,0},{8,12},{12,8},{16,20},{20,16},{24,28},{28,24},{1,5},{5... | collective-permute-start | bytes 196616 | tf_op jit(solution)/shard_map/ppermute | solution.py:580
  1.2 0.1 collective-permute-start.9
  1.3 0.0 copy-done.11
  1.3 0.7 %pad_add_fusion.table_ref.table_any = s32[17,16]{1,0:T(8,128)S(1)} fusion(s32[1,16]{1,0:T(1,128)S(1)} %bitcast.46, s32[16,16]{1,0:T(8,128)} %param.15), kind=kLoop, calls=%fused_computation.13 | loop fusion | flops 272 | bytes 2176 | tf_op jit(solution)/shard_map/add | solution.py:599
  2.0 1.6 %shard_map.93 = (s32[42]{0:T(128)S(1)}, bf16[7,2,2,128,128]{4,3,2,1,0:T(8,128)(2,1)}, bf16[7,2,2,128,128]{4,3,2,1,0:T(8,128)(2,1)}) custom-call(s32[17,16]{1,0:T(8,128)S(1)} %pad_add_fusion.table_ref.table_any), custom_call_target="tpu_custom_call" | custom-call | bytes 4194304 | tf_op jit(solution)/shard_map/pallas_call | solution.py:602
  3.6 1.0 %shard_map.95 = (bf16[4,128,128]{2,1,0:T(8,128)(2,1)S(1)}, bf16[2,128,128]{2,1,0:T(8,128)(2,1)S(1)}) custom-call(s32[42]{0:T(128)S(1)} %get-tuple-element.422.info_ref, bf16[256,128]{1,0:T(8,128)(2,1)} %key_ref.5, bf16[256,128]{1,0:T(8,128)(2,1)} %value_ref.3, bf16[256,128]{1,0:T(8,128)(2,1)} %collective-permute-done.9.refs_2_.key_other, ...), custom_call_target="tpu_custom_call" | custom-call | bytes 327680 | tf_op jit(solution)/shard_map/pallas_call | solution.py:614
  4.7 3.1 %collective-permute-start.11 = (bf16[4,128,128]{2,1,0:T(8,128)(2,1)S(1)}, bf16[4,128,128]{2,1,0:T(8,128)(2,1)S(1)}, u32[]{:S(2)}, u32[]{:S(2)}) collective-permute-start(bf16[4,128,128]{2,1,0:T(8,128)(2,1)S(1)} %get-tuple-element.291), channel_id=1, source_target_pairs={{0,8},{4,20},{8,0},{12,28},{16,24},{20,4},{24,16},{28,12},{1,9},{5... | collective-permute-start | bytes 393224 | tf_op jit(solution)/shard_map/ppermute | solution.py:589
  7.8 2.5 %collective-permute-start.12 = (bf16[2,128,128]{2,1,0:T(8,128)(2,1)S(1)}, bf16[2,128,128]{2,1,0:T(8,128)(2,1)S(1)}, u32[]{:S(2)}, u32[]{:S(2)}) collective-permute-start(bf16[2,128,128]{2,1,0:T(8,128)(2,1)S(1)} %get-tuple-element.292), channel_id=1, source_target_pairs={{0,24},{4,28},{8,16},{12,20},{16,8},{20,12},{24,0},{28,4},{1,25},{... | collective-permute-start | bytes 196616 | tf_op jit(solution)/shard_map/ppermute | solution.py:580
  10.2 0.9 %copy-done.1 = bf16[256,512]{1,0:T(8,128)(2,1)S(1)} copy-done((bf16[256,512]{1,0:T(8,128)(2,1)S(1)}, bf16[256,512]{1,0:T(8,128)(2,1)}, u32[]{:S(2)}) %copy-start.1) | copy-done | bytes 262168
  11.2 1.6 %shard_map.94 = (f32[1,1024]{1,0:T(1,128)S(1)}, f32[1,1024]{1,0:T(1,128)S(1)}, f32[128,1024]{1,0:T(8,128)S(1)}, bf16[128,1024]{1,0:T(8,128)(2,1)S(1)}) custom-call(s32[42]{0:T(128)S(1)} %get-tuple-element.422.info_ref, bf16[256,512]{1,0:T(8,128)(2,1)S(1)} %copy-done, bf16[256,512]{1,0:T(8,128)(2,1)S(1)} %copy-done.1, bf16[256,128]{1,0:T(8,128)(2,1)} %key_ref.5, ...), custom_call_target="tpu_custom_call" | custom-call | flops 1610612736 | bytes 524288 | tf_op jit(solution)/shard_map/pallas_call | solution.py:647
  12.8 2.2 %collective-permute-done.12.refs_1_ = bf16[2,128,128]{2,1,0:T(8,128)(2,1)S(1)} collective-permute-done((bf16[2,128,128]{2,1,0:T(8,128)(2,1)S(1)}, bf16[2,128,128]{2,1,0:T(8,128)(2,1)S(1)}, u32[]{:S(2)}, u32[]{:S(2)}) %collective-permute-start.12) | collective-permute-done | bytes 65568 | tf_op jit(solution)/shard_map/ppermute | solution.py:580
  15.0 0.5 %collective-permute-start.13 = (bf16[4,128,128]{2,1,0:T(8,128)(2,1)S(1)}, bf16[4,128,128]{2,1,0:T(8,128)(2,1)S(1)}, u32[]{:S(2)}, u32[]{:S(2)}) collective-permute-start(bf16[4,128,128]{2,1,0:T(8,128)(2,1)S(1)} %collective-permute-done.11.refs_0_), channel_id=1, source_target_pairs={{0,4},{4,0},{8,12},{12,8},{16,20},{20,16},{24,28},{28,24},{1,5},{5... | collective-permute-start | bytes 393224 | tf_op jit(solution)/shard_map/ppermute | solution.py:580
  15.6 0.7 %collective-permute-done.14.refs_3_ = bf16[2,128,128]{2,1,0:T(8,128)(2,1)S(1)} collective-permute-done((bf16[2,128,128]{2,1,0:T(8,128)(2,1)S(1)}, bf16[2,128,128]{2,1,0:T(8,128)(2,1)S(1)}, u32[]{:S(2)}, u32[]{:S(2)}) %collective-permute-start.14) | collective-permute-done | bytes 65568 | tf_op jit(solution)/shard_map/ppermute | solution.py:580
  16.3 0.2 collective-permute-done.13.refs_2_
  16.5 2.4 %shard_map.96 = (bf16[4,128,128]{2,1,0:T(8,128)(2,1)S(1)}, f32[1,1024]{1,0:T(1,128)S(1)}, f32[1,1024]{1,0:T(1,128)S(1)}, f32[1,1024]{1,0:T(1,128)S(1)}, bf16[128...) custom-call(s32[42]{0:T(128)S(1)} %get-tuple-element.522, ...), custom_call_target="tpu_custom_call" | custom-call | flops 1610612736 | bytes 524288 | tf_op jit(solution)/shard_map/pallas_call | solution.py:663
  18.9 0.0 copy-start.3
  18.9 0.6 %copy-done.3 = f32[256,128]{1,0:T(8,128)} copy-done((f32[256,128]{1,0:T(8,128)}, f32[256,128]{1,0:T(8,128)S(1)}, u32[]{:S(2)}) %copy-start.3) | copy-done | bytes 131096
  19.6 0.7 %copy-done.5 = f32[256,128]{1,0:T(8,128)} copy-done((f32[256,128]{1,0:T(8,128)}, f32[256,128]{1,0:T(8,128)S(1)}, u32[]{:S(2)}) %copy-start.5) | copy-done | bytes 131096
  20.2 0.4 %collective-permute-start.15 = (bf16[4,128,128]{2,1,0:T(8,128)(2,1)S(1)}, bf16[4,128,128]{2,1,0:T(8,128)(2,1)S(1)}, u32[]{:S(2)}, u32[]{:S(2)}) collective-permute-start(bf16[4,128,128]{2,1,0:T(8,128)(2,1)S(1)} %get-tuple-element.298), channel_id=1, source_target_pairs={{0,4},{4,0},{8,12},{12,8},{16,20},{20,16},{24,28},{28,24},{1,5},{5... | collective-permute-start | bytes 393224 | tf_op jit(solution)/shard_map/ppermute | solution.py:580
  20.6 1.0 %collective-permute-done.15 = bf16[4,128,128]{2,1,0:T(8,128)(2,1)S(1)} collective-permute-done((bf16[4,128,128]{2,1,0:T(8,128)(2,1)S(1)}, bf16[4,128,128]{2,1,0:T(8,128)(2,1)S(1)}, u32[]{:S(2)}, u32[]{:S(2)}) %collective-permute-start.15) | collective-permute-done | bytes 131104 | tf_op jit(solution)/shard_map/ppermute | solution.py:580
  21.6 0.0 copy-start.4
  21.7 1.1 %collective-permute-start.16 = (bf16[4,128,128]{2,1,0:T(8,128)(2,1)S(1)}, bf16[4,128,128]{2,1,0:T(8,128)(2,1)S(1)}, u32[]{:S(2)}, u32[]{:S(2)}) collective-permute-start(bf16[4,128,128]{2,1,0:T(8,128)(2,1)S(1)} %pad_maximum_fusion.refs_2_), channel_id=1, source_target_pairs={{0,8},{4,20},{8,0},{12,28},{16,24},{20,4},{24,16},{28,12},{1,9},{5... | collective-permute-start | bytes 393224 | tf_op jit(solution)/shard_map/ppermute | solution.py:589
  22.7 1.3 %shard_map.97 = (bf16[256,1024]{1,0:T(8,128)(2,1)S(1)}, f32[256,128]{1,0:T(8,128)S(1)}, f32[256,128]{1,0:T(8,128)S(1)}, bf16[2,128,128]{2,1,0:T(8,128)(2,1)S(1)}) custom-call(s32[42]{0:T(128)S(1)} %get-tuple-element.522, bf16[256,512]{1,0:T(8,128)(2,1)S(1)} %copy-done, bf16[256,512]{1,0:T(8,128)(2,1)S(1)} %copy-done.2, ...), custom_call_target="tpu_custom_call", output_to_operand_aliasing={{3}: (10, {})} | custom-call | flops 1207959552 | bytes 524288 | tf_op jit(solution)/shard_map/pallas_call | solution.py:714
  24.1 3.1 %collective-permute-start.17 = (bf16[2,128,128]{2,1,0:T(8,128)(2,1)S(1)}, bf16[2,128,128]{2,1,0:T(8,128)(2,1)S(1)}, u32[]{:S(2)}, u32[]{:S(2)}) collective-permute-start(bf16[2,128,128]{2,1,0:T(8,128)(2,1)S(1)} %get-tuple-element.312), channel_id=1, source_target_pairs={{0,24},{4,28},{8,16},{12,20},{16,8},{20,12},{24,0},{28,4},{1,25},{... | collective-permute-start | bytes 196616 | tf_op jit(solution)/shard_map/ppermute | solution.py:580
  27.2 0.7 %shard_map.99 = (f32[256,128]{1,0:T(8,128)}, f32[256,128]{1,0:T(8,128)}) custom-call(f32[256,128]{1,0:T(8,128)S(1)} %get-tuple-element.310.key_own.refs_0_, f32[256,128]{1,0:T(8,128)S(1)} %get-tuple-element.311.value_own.refs_1_), custom_call_target="tpu_custom_call" | custom-call | bytes 2097152 | tf_op jit(solution)/shard_map/pallas_call | solution.py:736
  27.9 1.9 %shard_map.98 = (bf16[256,512]{1,0:T(8,128)(2,1)}, f32[256,512]{1,0:T(8,128)}) custom-call(s32[42]{0:T(128)S(1)} %get-tuple-element.522, bf16[256,128]{1,0:T(8,128)(2,1)S(1)} %copy-done.10, bf16[256,1024]{1,0:T(8,128)(2,1)S(1)} %get-tuple-element.299.own_dscores, bf16[256,1024]{1,0:T(8,128)(2,1)S(1)} %get-tuple-element.300.slot_dscores, ...), custom_call_target="tpu_custom_call" | custom-call | flops 1073741824 | bytes 1048576 | tf_op jit(solution)/shard_map/pallas_call | solution.py:744
  29.9 0.7 %collective-permute-done.17.refs_4_ = bf16[2,128,128]{2,1,0:T(8,128)(2,1)S(1)} collective-permute-done((bf16[2,128,128]{2,1,0:T(8,128)(2,1)S(1)}, bf16[2,128,128]{2,1,0:T(8,128)(2,1)S(1)}, u32[]{:S(2)}, u32[]{:S(2)}) %collective-permute-start.17) | collective-permute-done | bytes 65568 | tf_op jit(solution)/shard_map/ppermute | solution.py:580
  30.6 0.3 collective-permute-start.19
  30.8 0.2 collective-permute-start.18
  31.1 0.7 %collective-permute-done.19.refs_6_ = bf16[2,128,128]{2,1,0:T(8,128)(2,1)S(1)} collective-permute-done((bf16[2,128,128]{2,1,0:T(8,128)(2,1)S(1)}, bf16[2,128,128]{2,1,0:T(8,128)(2,1)S(1)}, u32[]{:S(2)}, u32[]{:S(2)}) %collective-permute-start.19) | collective-permute-done | bytes 65568 | tf_op jit(solution)/shard_map/ppermute | solution.py:580
  31.8 0.4 %collective-permute-done.18.refs_5_ = bf16[4,128,128]{2,1,0:T(8,128)(2,1)S(1)} collective-permute-done((bf16[4,128,128]{2,1,0:T(8,128)(2,1)S(1)}, bf16[4,128,128]{2,1,0:T(8,128)(2,1)S(1)}, u32[]{:S(2)}, u32[]{:S(2)}) %collective-permute-start.18) | collective-permute-done | bytes 131104 | tf_op jit(solution)/shard_map/ppermute | solution.py:580
  32.2 0.6 %shard_map.100 = (f32[256,128]{1,0:T(8,128)}, f32[256,128]{1,0:T(8,128)}) custom-call(s32[42]{0:T(128)S(1)} %get-tuple-element.522, bf16[7,2,2,128,128]{4,3,2,1,0:T(8,128)(2,1)} %get-tuple-element.309.extra_ref, f32[256,128]{1,0:T(8,128)S(1)} %get-tuple-element.310.key_own.refs_0_, ...), custom_call_target="tpu_custom_call", output_to_operand_aliasing={{0}: (9, {}), {1}: (10, {})} | custom-call | bytes 655360 | tf_op jit(solution)/shard_map/pallas_call | solution.py:771
  (27 shorter events, 0.1 us)
Async XLA Ops:
  0.6 0.7 %copy-start.11 = (s32[16]{0:T(128)S(1)}, s32[16]{0:T(128)}, u32[]{:S(2)}) copy-start(s32[16]{0:T(128)} %param.14) | copy-start | bytes 196
  0.6 9.6 %copy-start = (bf16[256,512]{1,0:T(8,128)(2,1)S(1)}, bf16[256,512]{1,0:T(8,128)(2,1)}, u32[]{:S(2)}) copy-start(bf16[256,512]{1,0:T(8,128)(2,1)} %query_ref.5) | copy-start | bytes 786436
  0.7 3.0 %collective-permute-start.10 = (bf16[256,128]{1,0:T(8,128)(2,1)}, bf16[256,128]{1,0:T(8,128)(2,1)}, u32[]{:S(2)}, u32[]{:S(2)}) collective-permute-start(bf16[256,128]{1,0:T(8,128)(2,1)} %value_ref.3), channel_id=1, source_target_pairs={{0,4},{4,0},{8,12},{12,8},{16,20},{20,16},{24,28},{28,24},{1,5},{5... | collective-permute-start | bytes 196616 | tf_op jit(solution)/shard_map/ppermute | solution.py:580
  1.2 2.5 %collective-permute-start.9 = (bf16[256,128]{1,0:T(8,128)(2,1)}, bf16[256,128]{1,0:T(8,128)(2,1)}, u32[]{:S(2)}, u32[]{:S(2)}) collective-permute-start(bf16[256,128]{1,0:T(8,128)(2,1)} %key_ref.5), channel_id=1, source_target_pairs={{0,4},{4,0},{8,12},{12,8},{16,20},{20,16},{24,28},{28,24},{1,5},{5... | collective-permute-start | bytes 196616 | tf_op jit(solution)/shard_map/ppermute | solution.py:580
  4.7 10.4 %collective-permute-start.11 = (bf16[4,128,128]{2,1,0:T(8,128)(2,1)S(1)}, bf16[4,128,128]{2,1,0:T(8,128)(2,1)S(1)}, u32[]{:S(2)}, u32[]{:S(2)}) collective-permute-start(bf16[4,128,128]{2,1,0:T(8,128)(2,1)S(1)} %get-tuple-element.291), channel_id=1, source_target_pairs={{0,8},{4,20},{8,0},{12,28},{16,24},{20,4},{24,16},{28,12},{1,9},{5... | collective-permute-start | bytes 393224 | tf_op jit(solution)/shard_map/ppermute | solution.py:589
  7.8 7.3 %collective-permute-start.12 = (bf16[2,128,128]{2,1,0:T(8,128)(2,1)S(1)}, bf16[2,128,128]{2,1,0:T(8,128)(2,1)S(1)}, u32[]{:S(2)}, u32[]{:S(2)}) collective-permute-start(bf16[2,128,128]{2,1,0:T(8,128)(2,1)S(1)} %get-tuple-element.292), channel_id=1, source_target_pairs={{0,24},{4,28},{8,16},{12,20},{16,8},{20,12},{24,0},{28,4},{1,25},{... | collective-permute-start | bytes 196616 | tf_op jit(solution)/shard_map/ppermute | solution.py:580
  10.2 1.0 %copy-start.1 = (bf16[256,512]{1,0:T(8,128)(2,1)S(1)}, bf16[256,512]{1,0:T(8,128)(2,1)}, u32[]{:S(2)}) copy-start(bf16[256,512]{1,0:T(8,128)(2,1)} %grad_ref.5) | copy-start | bytes 786436
  11.2 4.4 %copy-start.7 = (bf16[256,128]{1,0:T(8,128)(2,1)S(1)}, bf16[256,128]{1,0:T(8,128)(2,1)}, u32[]{:S(2)}) copy-start(bf16[256,128]{1,0:T(8,128)(2,1)} %value_ref.3) | copy-start | bytes 196612
  11.2 4.4 %copy-start.9 = (bf16[256,128]{1,0:T(8,128)(2,1)S(1)}, bf16[256,128]{1,0:T(8,128)(2,1)}, u32[]{:S(2)}) copy-start(bf16[256,128]{1,0:T(8,128)(2,1)} %key_ref.5) | copy-start | bytes 196612
  15.0 1.3 %collective-permute-start.14 = (bf16[2,128,128]{2,1,0:T(8,128)(2,1)S(1)}, bf16[2,128,128]{2,1,0:T(8,128)(2,1)S(1)}, u32[]{:S(2)}, u32[]{:S(2)}) collective-permute-start(bf16[2,128,128]{2,1,0:T(8,128)(2,1)S(1)} %collective-permute-done.12.refs_1_), channel_id=1, source_target_pairs={{0,4},{4,0},{8,12},{12,8},{16,20},{20,16},{24,28},{28,24},{1,5},{5... | collective-permute-start | bytes 196616 | tf_op jit(solution)/shard_map/ppermute | solution.py:580
  15.0 1.5 %collective-permute-start.13 = (bf16[4,128,128]{2,1,0:T(8,128)(2,1)S(1)}, bf16[4,128,128]{2,1,0:T(8,128)(2,1)S(1)}, u32[]{:S(2)}, u32[]{:S(2)}) collective-permute-start(bf16[4,128,128]{2,1,0:T(8,128)(2,1)S(1)} %collective-permute-done.11.refs_0_), channel_id=1, source_target_pairs={{0,4},{4,0},{8,12},{12,8},{16,20},{20,16},{24,28},{28,24},{1,5},{5... | collective-permute-start | bytes 393224 | tf_op jit(solution)/shard_map/ppermute | solution.py:580
  18.9 0.7 %copy-start.3 = (f32[256,128]{1,0:T(8,128)}, f32[256,128]{1,0:T(8,128)S(1)}, u32[]{:S(2)}) copy-start(f32[256,128]{1,0:T(8,128)S(1)} %get-tuple-element.296.key_full) | copy-start | bytes 393220
  19.6 0.7 %copy-start.5 = (f32[256,128]{1,0:T(8,128)}, f32[256,128]{1,0:T(8,128)S(1)}, u32[]{:S(2)}) copy-start(f32[256,128]{1,0:T(8,128)S(1)} %get-tuple-element.297.value_full) | copy-start | bytes 393220
  20.2 1.3 %collective-permute-start.15 = (bf16[4,128,128]{2,1,0:T(8,128)(2,1)S(1)}, bf16[4,128,128]{2,1,0:T(8,128)(2,1)S(1)}, u32[]{:S(2)}, u32[]{:S(2)}) collective-permute-start(bf16[4,128,128]{2,1,0:T(8,128)(2,1)S(1)} %get-tuple-element.298), channel_id=1, source_target_pairs={{0,4},{4,0},{8,12},{12,8},{16,20},{20,16},{24,28},{28,24},{1,5},{5... | collective-permute-start | bytes 393224 | tf_op jit(solution)/shard_map/ppermute | solution.py:580
  20.6 2.1 %copy-start.2 = (bf16[256,512]{1,0:T(8,128)(2,1)S(1)}, bf16[256,512]{1,0:T(8,128)(2,1)}, u32[]{:S(2)}) copy-start(bf16[256,512]{1,0:T(8,128)(2,1)} %grad_ref.5) | copy-start | bytes 786436
  21.6 1.1 %copy-start.8 = (bf16[256,128]{1,0:T(8,128)(2,1)S(1)}, bf16[256,128]{1,0:T(8,128)(2,1)}, u32[]{:S(2)}) copy-start(bf16[256,128]{1,0:T(8,128)(2,1)} %value_ref.3) | copy-start | bytes 196612
  21.6 1.2 %copy-start.10 = (bf16[256,128]{1,0:T(8,128)(2,1)S(1)}, bf16[256,128]{1,0:T(8,128)(2,1)}, u32[]{:S(2)}) copy-start(bf16[256,128]{1,0:T(8,128)(2,1)} %key_ref.5) | copy-start | bytes 196612
  21.6 1.1 %copy-start.4 = (f32[256,128]{1,0:T(8,128)S(1)}, f32[256,128]{1,0:T(8,128)}, u32[]{:S(2)}) copy-start(f32[256,128]{1,0:T(8,128)} %copy-done.3) | copy-start | bytes 393220
  21.6 1.1 %copy-start.6 = (f32[256,128]{1,0:T(8,128)S(1)}, f32[256,128]{1,0:T(8,128)}, u32[]{:S(2)}) copy-start(f32[256,128]{1,0:T(8,128)} %copy-done.5) | copy-start | bytes 393220
  21.7 9.2 %collective-permute-start.16 = (bf16[4,128,128]{2,1,0:T(8,128)(2,1)S(1)}, bf16[4,128,128]{2,1,0:T(8,128)(2,1)S(1)}, u32[]{:S(2)}, u32[]{:S(2)}) collective-permute-start(bf16[4,128,128]{2,1,0:T(8,128)(2,1)S(1)} %pad_maximum_fusion.refs_2_), channel_id=1, source_target_pairs={{0,8},{4,20},{8,0},{12,28},{16,24},{20,4},{24,16},{28,12},{1,9},{5... | collective-permute-start | bytes 393224 | tf_op jit(solution)/shard_map/ppermute | solution.py:589
  24.1 6.5 %collective-permute-start.17 = (bf16[2,128,128]{2,1,0:T(8,128)(2,1)S(1)}, bf16[2,128,128]{2,1,0:T(8,128)(2,1)S(1)}, u32[]{:S(2)}, u32[]{:S(2)}) collective-permute-start(bf16[2,128,128]{2,1,0:T(8,128)(2,1)S(1)} %get-tuple-element.312), channel_id=1, source_target_pairs={{0,24},{4,28},{8,16},{12,20},{16,8},{20,12},{24,0},{28,4},{1,25},{... | collective-permute-start | bytes 196616 | tf_op jit(solution)/shard_map/ppermute | solution.py:580
  30.6 1.3 %collective-permute-start.19 = (bf16[2,128,128]{2,1,0:T(8,128)(2,1)S(1)}, bf16[2,128,128]{2,1,0:T(8,128)(2,1)S(1)}, u32[]{:S(2)}, u32[]{:S(2)}) collective-permute-start(bf16[2,128,128]{2,1,0:T(8,128)(2,1)S(1)} %collective-permute-done.17.refs_4_), channel_id=1, source_target_pairs={{0,4},{4,0},{8,12},{12,8},{16,20},{20,16},{24,28},{28,24},{1,5},{5... | collective-permute-start | bytes 196616 | tf_op jit(solution)/shard_map/ppermute | solution.py:580
  30.8 1.3 %collective-permute-start.18 = (bf16[4,128,128]{2,1,0:T(8,128)(2,1)S(1)}, bf16[4,128,128]{2,1,0:T(8,128)(2,1)S(1)}, u32[]{:S(2)}, u32[]{:S(2)}) collective-permute-start(bf16[4,128,128]{2,1,0:T(8,128)(2,1)S(1)} %collective-permute-done.16.refs_3_), channel_id=1, source_target_pairs={{0,4},{4,0},{8,12},{12,8},{16,20},{20,16},{24,28},{28,24},{1,5},{5... | collective-permute-start | bytes 393224 | tf_op jit(solution)/shard_map/ppermute | solution.py:580

commit v7 on v6

--- a/solution.py
+++ b/solution.py
@@ -45,8 +45,8 @@
     return [(step, step + 1) for step in range(1, chips - 1, 2)]
 
 
-def list_kernel(tile_total, tiles, slots, table_ref, info_ref, spare_ref, spare_sums_ref, any_ref):
-    del spare_ref, spare_sums_ref
+def list_kernel(tile_total, tiles, slots, table_ref, info_ref, spare_ref, any_ref):
+    del spare_ref
     rank = lax.axis_index("seq")
 
     def ids(position):
@@ -599,15 +599,14 @@
     table = table + jnp.pad(tile_ids[None], ((tile_total, 0), (0, 0)))
     key_other, value_other = swap(key_rows, 1), swap(value_rows, 1)
     chip_rows = (key_rows, value_rows, key_other, value_other)
-    info, spare, spare_sums = call(
+    info, spare = call(
         functools.partial(list_kernel, tile_total, tiles, slots),
         [SMEM_SPEC],
         (
             shape((info_size(tile_total, tiles, slots),), jnp.int32),
             shape(buffer, bf16),
-            shape(buffer, bf16),
         ),
-        (SMEM_SPEC, ANY_SPEC, ANY_SPEC),
+        (SMEM_SPEC, ANY_SPEC),
         scratch=(pltpu.SMEM((tile_total,), jnp.int32),),
         moved=4 * 1024 * 1024,
     )(table)
@@ -767,7 +766,7 @@
         pair = jnp.stack([total, swap(total, 1)])
         return lax.dynamic_update_index_in_dim(totals, pair, index - 1, 0)
 
-    extra = lax.fori_loop(1, used, reduce_more, spare_sums)
+    extra = lax.fori_loop(1, used, reduce_more, more)
     key_grad, value_grad = call(
         functools.partial(close_kernel, tiles, slots, chips, tile_total),
         [SMEM_SPEC, ANY_SPEC] + [VMEM_SPEC] * (2 + len(sums)) + [ANY_SPEC] * 2,

time: 33.1 us -> 33.8 us (1.021); the launches traced: 32.8 us -> 33.8 us
  waiting for transfers between devices: 6 us -> 9.14 us
  starting transfers between devices: 11.7 us -> 8.62 us
  Pallas kernels: 11.1 us -> 11.8 us
    ppermute x2, waiting for transfers between devices: 0.01 us -> 3.65 us  [trade(): got.append(lax.ppermute(full, 'seq', routes))]
    ppermute x2, starting transfers between devices: 4.14 us -> 0.62 us  [trade(): got.append(lax.ppermute(full, 'seq', routes))]
    pallas_call x1, Pallas kernels: 0.59 us -> 1.28 us  [per_device(): call(functools.partial(close_kernel, tiles, slots, chips, tile_total), [S...]
    ppermute x9, waiting for transfers between devices: 5.99 us -> 5.49 us  [swap(): lax.ppermute(values, 'seq', [(source, source ^ step) for source in range(...]
    ppermute x9, starting transfers between devices: 7.6 us -> 8 us  [swap(): lax.ppermute(values, 'seq', [(source, source ^ step) for source in range(...]
  transfers between devices with their start and end apart: 11 -> 11, of which waited for: 7 -> 6; matrix products, arithmetic and copies ran while one was open for 2% -> 2% of each run, Pallas kernels for 22% -> 21%
where the time goes in v7:
time: 33.8 us
  Pallas kernels  11.8 us (35%)
  waiting for transfers between devices  9.14 us (27%)
  starting transfers between devices  8.62 us (26%)
  local copies, waits for them, and re-layouts  2.64 us (8%)
  between operations  0.87 us (3%)
  other arithmetic  0.75 us (2%)
    ppermute x9, starting transfers between devices, swap(): lax.ppermute(values, 'seq', [(source, source ^ step) for source in range(...  8 us
    ppermute x9, waiting for transfers between devices, swap(): lax.ppermute(values, 'seq', [(source, source ^ step) for source in range(...  5.49 us
    ppermute x2, waiting for transfers between devices, trade(): got.append(lax.ppermute(full, 'seq', routes))  3.65 us
    unnamed x24, local copies, waits for them, and re-layouts  2.64 us
    pallas_call x1, Pallas kernels, per_device(): call(functools.partial(gathered_kernel, chips, tiles, slots, heads, tile_...  2.37 us
    pallas_call x1, Pallas kernels, per_device(): call(functools.partial(queries_kernel, slots, heads), [SMEM_SPEC] + [VMEM...  1.91 us
    pallas_call x1, Pallas kernels, per_device(): call(functools.partial(list_kernel, tile_total, tiles, slots), [SMEM_SPEC...  1.61 us
    pallas_call x1, Pallas kernels, per_device(): call(functools.partial(own_kernel, tiles, slots, heads, tile_total), [SME...  1.56 us
  transfers between devices with their start and end apart: 11, of which 6 were waited for; matrix products, arithmetic and copies ran while one was open for 2% of the time, Pallas kernels for 21%

profile of v7, /device:TPU:0, one launch (start us, length us, event | category | flops | bytes accessed | tf_op | source)
XLA Modules:
  0.0 33.8 jit_solution(11135240588574702609)
XLA Ops:
  0.7 0.5 %collective-permute-start.10 = (bf16[256,128]{1,0:T(8,128)(2,1)}, bf16[256,128]{1,0:T(8,128)(2,1)}, u32[]{:S(2)}, u32[]{:S(2)}) collective-permute-start(bf16[256,128]{1,0:T(8,128)(2,1)} %value_ref.3), channel_id=1, source_target_pairs={{0,4},{4,0},{8,12},{12,8},{16,20},{20,16},{24,28},{28,24},{1,5},{5... | collective-permute-start | bytes 196616 | tf_op jit(solution)/shard_map/ppermute | solution.py:580
  1.2 0.1 collective-permute-start.9
  1.3 0.0 copy-done.11
  1.3 0.7 %pad_add_fusion.table_ref.table_any = s32[17,16]{1,0:T(8,128)S(1)} fusion(s32[1,16]{1,0:T(1,128)S(1)} %bitcast.46, s32[16,16]{1,0:T(8,128)} %param.15), kind=kLoop, calls=%fused_computation.13 | loop fusion | flops 272 | bytes 2176 | tf_op jit(solution)/shard_map/add | solution.py:599
  2.0 1.6 %shard_map.93 = (s32[42]{0:T(128)S(1)}, bf16[7,2,2,128,128]{4,3,2,1,0:T(8,128)(2,1)}) custom-call(s32[17,16]{1,0:T(8,128)S(1)} %pad_add_fusion.table_ref.table_any), custom_call_target="tpu_custom_call" | custom-call | bytes 4194304 | tf_op jit(solution)/shard_map/pallas_call | solution.py:602
  3.6 1.0 %shard_map.95 = (bf16[4,128,128]{2,1,0:T(8,128)(2,1)S(1)}, bf16[2,128,128]{2,1,0:T(8,128)(2,1)S(1)}) custom-call(s32[42]{0:T(128)S(1)} %get-tuple-element.420.info_ref, bf16[256,128]{1,0:T(8,128)(2,1)} %key_ref.5, bf16[256,128]{1,0:T(8,128)(2,1)} %value_ref.3, bf16[256,128]{1,0:T(8,128)(2,1)} %collective-permute-done.9.refs_2_.key_other, ...), custom_call_target="tpu_custom_call" | custom-call | bytes 327680 | tf_op jit(solution)/shard_map/pallas_call | solution.py:613
  4.7 5.1 %collective-permute-start.12 = (bf16[2,128,128]{2,1,0:T(8,128)(2,1)S(1)}, bf16[2,128,128]{2,1,0:T(8,128)(2,1)S(1)}, u32[]{:S(2)}, u32[]{:S(2)}) collective-permute-start(bf16[2,128,128]{2,1,0:T(8,128)(2,1)S(1)} %get-tuple-element.291), channel_id=1, source_target_pairs={{0,24},{4,28},{8,16},{12,20},{16,8},{20,12},{24,0},{28,4},{1,25},{... | collective-permute-start | bytes 196616 | tf_op jit(solution)/shard_map/ppermute | solution.py:580
  9.8 0.9 %copy-done.1 = bf16[256,512]{1,0:T(8,128)(2,1)S(1)} copy-done((bf16[256,512]{1,0:T(8,128)(2,1)S(1)}, bf16[256,512]{1,0:T(8,128)(2,1)}, u32[]{:S(2)}) %copy-start.1) | copy-done | bytes 262168
  10.8 1.6 %shard_map.94 = (f32[1,1024]{1,0:T(1,128)S(1)}, f32[1,1024]{1,0:T(1,128)S(1)}, f32[128,1024]{1,0:T(8,128)S(1)}, bf16[128,1024]{1,0:T(8,128)(2,1)S(1)}) custom-call(s32[42]{0:T(128)S(1)} %get-tuple-element.420.info_ref, bf16[256,512]{1,0:T(8,128)(2,1)S(1)} %copy-done, bf16[256,512]{1,0:T(8,128)(2,1)S(1)} %copy-done.1, bf16[256,128]{1,0:T(8,128)(2,1)} %key_ref.5, ...), custom_call_target="tpu_custom_call" | custom-call | flops 1610612736 | bytes 524288 | tf_op jit(solution)/shard_map/pallas_call | solution.py:646
  12.4 0.1 collective-permute-start.14
  12.5 3.6 %collective-permute-done.11.refs_0_ = bf16[4,128,128]{2,1,0:T(8,128)(2,1)S(1)} collective-permute-done((bf16[4,128,128]{2,1,0:T(8,128)(2,1)S(1)}, bf16[4,128,128]{2,1,0:T(8,128)(2,1)S(1)}, u32[]{:S(2)}, u32[]{:S(2)}) %collective-permute-start.11) | collective-permute-done | bytes 131104 | tf_op jit(solution)/shard_map/ppermute | solution.py:589
  16.2 1.3 %collective-permute-done.13.refs_2_ = bf16[4,128,128]{2,1,0:T(8,128)(2,1)S(1)} collective-permute-done((bf16[4,128,128]{2,1,0:T(8,128)(2,1)S(1)}, bf16[4,128,128]{2,1,0:T(8,128)(2,1)S(1)}, u32[]{:S(2)}, u32[]{:S(2)}) %collective-permute-start.13) | collective-permute-done | bytes 131104 | tf_op jit(solution)/shard_map/ppermute | solution.py:580
  17.5 2.4 %shard_map.96 = (bf16[4,128,128]{2,1,0:T(8,128)(2,1)S(1)}, f32[1,1024]{1,0:T(1,128)S(1)}, f32[1,1024]{1,0:T(1,128)S(1)}, f32[1,1024]{1,0:T(1,128)S(1)}, bf16[128...) custom-call(s32[42]{0:T(128)S(1)} %get-tuple-element.520, ...), custom_call_target="tpu_custom_call" | custom-call | flops 1610612736 | bytes 524288 | tf_op jit(solution)/shard_map/pallas_call | solution.py:662
  19.8 0.0 copy-start.3
  19.9 0.6 %copy-done.3 = f32[256,128]{1,0:T(8,128)} copy-done((f32[256,128]{1,0:T(8,128)}, f32[256,128]{1,0:T(8,128)S(1)}, u32[]{:S(2)}) %copy-start.3) | copy-done | bytes 131096
  20.5 0.7 %copy-done.5 = f32[256,128]{1,0:T(8,128)} copy-done((f32[256,128]{1,0:T(8,128)}, f32[256,128]{1,0:T(8,128)S(1)}, u32[]{:S(2)}) %copy-start.5) | copy-done | bytes 131096
  21.2 0.1 collective-permute-start.15
  21.3 1.2 %collective-permute-done.15 = bf16[4,128,128]{2,1,0:T(8,128)(2,1)S(1)} collective-permute-done((bf16[4,128,128]{2,1,0:T(8,128)(2,1)S(1)}, bf16[4,128,128]{2,1,0:T(8,128)(2,1)S(1)}, u32[]{:S(2)}, u32[]{:S(2)}) %collective-permute-start.15) | collective-permute-done | bytes 131104 | tf_op jit(solution)/shard_map/ppermute | solution.py:580
  22.6 0.6 %collective-permute-start.16 = (bf16[4,128,128]{2,1,0:T(8,128)(2,1)S(1)}, bf16[4,128,128]{2,1,0:T(8,128)(2,1)S(1)}, u32[]{:S(2)}, u32[]{:S(2)}) collective-permute-start(bf16[4,128,128]{2,1,0:T(8,128)(2,1)S(1)} %pad_maximum_fusion.refs_2_), channel_id=1, source_target_pairs={{0,8},{4,20},{8,0},{12,28},{16,24},{20,4},{24,16},{28,12},{1,9},{5... | collective-permute-start | bytes 393224 | tf_op jit(solution)/shard_map/ppermute | solution.py:589
  23.2 0.1 copy-done.8
  23.3 0.0 copy-done.10
  23.4 0.1 copy-done.4
  23.5 0.1 copy-done.6
  23.5 1.3 %shard_map.97 = (bf16[256,1024]{1,0:T(8,128)(2,1)S(1)}, f32[256,128]{1,0:T(8,128)S(1)}, f32[256,128]{1,0:T(8,128)S(1)}, bf16[2,128,128]{2,1,0:T(8,128)(2,1)S(1)}) custom-call(s32[42]{0:T(128)S(1)} %get-tuple-element.520, bf16[256,512]{1,0:T(8,128)(2,1)S(1)} %copy-done, bf16[256,512]{1,0:T(8,128)(2,1)S(1)} %copy-done.2, ...), custom_call_target="tpu_custom_call", output_to_operand_aliasing={{3}: (10, {})} | custom-call | flops 1207959552 | bytes 524288 | tf_op jit(solution)/shard_map/pallas_call | solution.py:713
  24.9 1.6 %collective-permute-start.17 = (bf16[2,128,128]{2,1,0:T(8,128)(2,1)S(1)}, bf16[2,128,128]{2,1,0:T(8,128)(2,1)S(1)}, u32[]{:S(2)}, u32[]{:S(2)}) collective-permute-start(bf16[2,128,128]{2,1,0:T(8,128)(2,1)S(1)} %get-tuple-element.310), channel_id=1, source_target_pairs={{0,24},{4,28},{8,16},{12,20},{16,8},{20,12},{24,0},{28,4},{1,25},{... | collective-permute-start | bytes 196616 | tf_op jit(solution)/shard_map/ppermute | solution.py:580
  26.4 0.7 %shard_map.99 = (f32[256,128]{1,0:T(8,128)}, f32[256,128]{1,0:T(8,128)}) custom-call(f32[256,128]{1,0:T(8,128)S(1)} %get-tuple-element.308.key_own.refs_0_, f32[256,128]{1,0:T(8,128)S(1)} %get-tuple-element.309.value_own.refs_1_), custom_call_target="tpu_custom_call" | custom-call | bytes 2097152 | tf_op jit(solution)/shard_map/pallas_call | solution.py:735
  27.1 1.9 %shard_map.98 = (bf16[256,512]{1,0:T(8,128)(2,1)}, f32[256,512]{1,0:T(8,128)}) custom-call(s32[42]{0:T(128)S(1)} %get-tuple-element.520, bf16[256,128]{1,0:T(8,128)(2,1)S(1)} %copy-done.10, bf16[256,1024]{1,0:T(8,128)(2,1)S(1)} %get-tuple-element.298.own_dscores, bf16[256,1024]{1,0:T(8,128)(2,1)S(1)} %get-tuple-element.299.slot_dscores, ...), custom_call_target="tpu_custom_call" | custom-call | flops 1073741824 | bytes 1048576 | tf_op jit(solution)/shard_map/pallas_call | solution.py:743
  29.1 2.0 %collective-permute-done.17.refs_4_ = bf16[2,128,128]{2,1,0:T(8,128)(2,1)S(1)} collective-permute-done((bf16[2,128,128]{2,1,0:T(8,128)(2,1)S(1)}, bf16[2,128,128]{2,1,0:T(8,128)(2,1)S(1)}, u32[]{:S(2)}, u32[]{:S(2)}) %collective-permute-start.17) | collective-permute-done | bytes 65568 | tf_op jit(solution)/shard_map/ppermute | solution.py:580
  31.1 0.5 %collective-permute-start.18 = (bf16[4,128,128]{2,1,0:T(8,128)(2,1)S(1)}, bf16[4,128,128]{2,1,0:T(8,128)(2,1)S(1)}, u32[]{:S(2)}, u32[]{:S(2)}) collective-permute-start(bf16[4,128,128]{2,1,0:T(8,128)(2,1)S(1)} %collective-permute-done.16.refs_3_), channel_id=1, source_target_pairs={{0,4},{4,0},{8,12},{12,8},{16,20},{20,16},{24,28},{28,24},{1,5},{5... | collective-permute-start | bytes 393224 | tf_op jit(solution)/shard_map/ppermute | solution.py:580
  31.6 0.7 %collective-permute-done.19.refs_6_ = bf16[2,128,128]{2,1,0:T(8,128)(2,1)S(1)} collective-permute-done((bf16[2,128,128]{2,1,0:T(8,128)(2,1)S(1)}, bf16[2,128,128]{2,1,0:T(8,128)(2,1)S(1)}, u32[]{:S(2)}, u32[]{:S(2)}) %collective-permute-start.19) | collective-permute-done | bytes 65568 | tf_op jit(solution)/shard_map/ppermute | solution.py:580
  32.3 0.2 collective-permute-done.18.refs_5_
  32.6 1.3 %shard_map.100 = (f32[256,128]{1,0:T(8,128)}, f32[256,128]{1,0:T(8,128)}) custom-call(s32[42]{0:T(128)S(1)} %get-tuple-element.520, bf16[7,2,2,128,128]{4,3,2,1,0:T(8,128)(2,1)} %get-tuple-element.307.extra_ref, f32[256,128]{1,0:T(8,128)S(1)} %get-tuple-element.308.key_own.refs_0_, ...), custom_call_target="tpu_custom_call", output_to_operand_aliasing={{0}: (9, {}), {1}: (10, {})} | custom-call | bytes 655360 | tf_op jit(solution)/shard_map/pallas_call | solution.py:770
  (27 shorter events, 0.1 us)
Async XLA Ops:
  0.6 0.7 %copy-start.11 = (s32[16]{0:T(128)S(1)}, s32[16]{0:T(128)}, u32[]{:S(2)}) copy-start(s32[16]{0:T(128)} %param.14) | copy-start | bytes 196
  0.6 9.2 %copy-start = (bf16[256,512]{1,0:T(8,128)(2,1)S(1)}, bf16[256,512]{1,0:T(8,128)(2,1)}, u32[]{:S(2)}) copy-start(bf16[256,512]{1,0:T(8,128)(2,1)} %query_ref.5) | copy-start | bytes 786436
  0.7 3.0 %collective-permute-start.10 = (bf16[256,128]{1,0:T(8,128)(2,1)}, bf16[256,128]{1,0:T(8,128)(2,1)}, u32[]{:S(2)}, u32[]{:S(2)}) collective-permute-start(bf16[256,128]{1,0:T(8,128)(2,1)} %value_ref.3), channel_id=1, source_target_pairs={{0,4},{4,0},{8,12},{12,8},{16,20},{20,16},{24,28},{28,24},{1,5},{5... | collective-permute-start | bytes 196616 | tf_op jit(solution)/shard_map/ppermute | solution.py:580
  1.2 2.5 %collective-permute-start.9 = (bf16[256,128]{1,0:T(8,128)(2,1)}, bf16[256,128]{1,0:T(8,128)(2,1)}, u32[]{:S(2)}, u32[]{:S(2)}) collective-permute-start(bf16[256,128]{1,0:T(8,128)(2,1)} %key_ref.5), channel_id=1, source_target_pairs={{0,4},{4,0},{8,12},{12,8},{16,20},{20,16},{24,28},{28,24},{1,5},{5... | collective-permute-start | bytes 196616 | tf_op jit(solution)/shard_map/ppermute | solution.py:580
  4.7 7.7 %collective-permute-start.12 = (bf16[2,128,128]{2,1,0:T(8,128)(2,1)S(1)}, bf16[2,128,128]{2,1,0:T(8,128)(2,1)S(1)}, u32[]{:S(2)}, u32[]{:S(2)}) collective-permute-start(bf16[2,128,128]{2,1,0:T(8,128)(2,1)S(1)} %get-tuple-element.291), channel_id=1, source_target_pairs={{0,24},{4,28},{8,16},{12,20},{16,8},{20,12},{24,0},{28,4},{1,25},{... | collective-permute-start | bytes 196616 | tf_op jit(solution)/shard_map/ppermute | solution.py:580
  9.8 6.3 %collective-permute-start.11 = (bf16[4,128,128]{2,1,0:T(8,128)(2,1)S(1)}, bf16[4,128,128]{2,1,0:T(8,128)(2,1)S(1)}, u32[]{:S(2)}, u32[]{:S(2)}) collective-permute-start(bf16[4,128,128]{2,1,0:T(8,128)(2,1)S(1)} %get-tuple-element.290), channel_id=1, source_target_pairs={{0,8},{4,20},{8,0},{12,28},{16,24},{20,4},{24,16},{28,12},{1,9},{5... | collective-permute-start | bytes 393224 | tf_op jit(solution)/shard_map/ppermute | solution.py:589
  9.8 1.0 %copy-start.1 = (bf16[256,512]{1,0:T(8,128)(2,1)S(1)}, bf16[256,512]{1,0:T(8,128)(2,1)}, u32[]{:S(2)}) copy-start(bf16[256,512]{1,0:T(8,128)(2,1)} %grad_ref.5) | copy-start | bytes 786436
  10.7 5.4 %copy-start.7 = (bf16[256,128]{1,0:T(8,128)(2,1)S(1)}, bf16[256,128]{1,0:T(8,128)(2,1)}, u32[]{:S(2)}) copy-start(bf16[256,128]{1,0:T(8,128)(2,1)} %value_ref.3) | copy-start | bytes 196612
  10.7 5.4 %copy-start.9 = (bf16[256,128]{1,0:T(8,128)(2,1)S(1)}, bf16[256,128]{1,0:T(8,128)(2,1)}, u32[]{:S(2)}) copy-start(bf16[256,128]{1,0:T(8,128)(2,1)} %key_ref.5) | copy-start | bytes 196612
  12.4 3.8 %collective-permute-start.14 = (bf16[2,128,128]{2,1,0:T(8,128)(2,1)S(1)}, bf16[2,128,128]{2,1,0:T(8,128)(2,1)S(1)}, u32[]{:S(2)}, u32[]{:S(2)}) collective-permute-start(bf16[2,128,128]{2,1,0:T(8,128)(2,1)S(1)} %collective-permute-done.12.refs_1_), channel_id=1, source_target_pairs={{0,4},{4,0},{8,12},{12,8},{16,20},{20,16},{24,28},{28,24},{1,5},{5... | collective-permute-start | bytes 196616 | tf_op jit(solution)/shard_map/ppermute | solution.py:580
  16.1 1.3 %collective-permute-start.13 = (bf16[4,128,128]{2,1,0:T(8,128)(2,1)S(1)}, bf16[4,128,128]{2,1,0:T(8,128)(2,1)S(1)}, u32[]{:S(2)}, u32[]{:S(2)}) collective-permute-start(bf16[4,128,128]{2,1,0:T(8,128)(2,1)S(1)} %collective-permute-done.11.refs_0_), channel_id=1, source_target_pairs={{0,4},{4,0},{8,12},{12,8},{16,20},{20,16},{24,28},{28,24},{1,5},{5... | collective-permute-start | bytes 393224 | tf_op jit(solution)/shard_map/ppermute | solution.py:580
  19.8 0.7 %copy-start.3 = (f32[256,128]{1,0:T(8,128)}, f32[256,128]{1,0:T(8,128)S(1)}, u32[]{:S(2)}) copy-start(f32[256,128]{1,0:T(8,128)S(1)} %get-tuple-element.295.key_full) | copy-start | bytes 393220
  20.5 0.7 %copy-start.5 = (f32[256,128]{1,0:T(8,128)}, f32[256,128]{1,0:T(8,128)S(1)}, u32[]{:S(2)}) copy-start(f32[256,128]{1,0:T(8,128)S(1)} %get-tuple-element.296.value_full) | copy-start | bytes 393220
  21.2 1.3 %collective-permute-start.15 = (bf16[4,128,128]{2,1,0:T(8,128)(2,1)S(1)}, bf16[4,128,128]{2,1,0:T(8,128)(2,1)S(1)}, u32[]{:S(2)}, u32[]{:S(2)}) collective-permute-start(bf16[4,128,128]{2,1,0:T(8,128)(2,1)S(1)} %get-tuple-element.297), channel_id=1, source_target_pairs={{0,4},{4,0},{8,12},{12,8},{16,20},{20,16},{24,28},{28,24},{1,5},{5... | collective-permute-start | bytes 393224 | tf_op jit(solution)/shard_map/ppermute | solution.py:580
  21.3 1.9 %copy-start.2 = (bf16[256,512]{1,0:T(8,128)(2,1)S(1)}, bf16[256,512]{1,0:T(8,128)(2,1)}, u32[]{:S(2)}) copy-start(bf16[256,512]{1,0:T(8,128)(2,1)} %grad_ref.5) | copy-start | bytes 786436
  22.5 0.8 %copy-start.8 = (bf16[256,128]{1,0:T(8,128)(2,1)S(1)}, bf16[256,128]{1,0:T(8,128)(2,1)}, u32[]{:S(2)}) copy-start(bf16[256,128]{1,0:T(8,128)(2,1)} %value_ref.3) | copy-start | bytes 196612
  22.5 0.9 %copy-start.10 = (bf16[256,128]{1,0:T(8,128)(2,1)S(1)}, bf16[256,128]{1,0:T(8,128)(2,1)}, u32[]{:S(2)}) copy-start(bf16[256,128]{1,0:T(8,128)(2,1)} %key_ref.5) | copy-start | bytes 196612
  22.5 0.9 %copy-start.4 = (f32[256,128]{1,0:T(8,128)S(1)}, f32[256,128]{1,0:T(8,128)}, u32[]{:S(2)}) copy-start(f32[256,128]{1,0:T(8,128)} %copy-done.3) | copy-start | bytes 393220
  22.6 1.0 %copy-start.6 = (f32[256,128]{1,0:T(8,128)S(1)}, f32[256,128]{1,0:T(8,128)}, u32[]{:S(2)}) copy-start(f32[256,128]{1,0:T(8,128)} %copy-done.5) | copy-start | bytes 393220
  22.6 8.5 %collective-permute-start.16 = (bf16[4,128,128]{2,1,0:T(8,128)(2,1)S(1)}, bf16[4,128,128]{2,1,0:T(8,128)(2,1)S(1)}, u32[]{:S(2)}, u32[]{:S(2)}) collective-permute-start(bf16[4,128,128]{2,1,0:T(8,128)(2,1)S(1)} %pad_maximum_fusion.refs_2_), channel_id=1, source_target_pairs={{0,8},{4,20},{8,0},{12,28},{16,24},{20,4},{24,16},{28,12},{1,9},{5... | collective-permute-start | bytes 393224 | tf_op jit(solution)/shard_map/ppermute | solution.py:589
  24.9 6.2 %collective-permute-start.17 = (bf16[2,128,128]{2,1,0:T(8,128)(2,1)S(1)}, bf16[2,128,128]{2,1,0:T(8,128)(2,1)S(1)}, u32[]{:S(2)}, u32[]{:S(2)}) collective-permute-start(bf16[2,128,128]{2,1,0:T(8,128)(2,1)S(1)} %get-tuple-element.310), channel_id=1, source_target_pairs={{0,24},{4,28},{8,16},{12,20},{16,8},{20,12},{24,0},{28,4},{1,25},{... | collective-permute-start | bytes 196616 | tf_op jit(solution)/shard_map/ppermute | solution.py:580
  31.1 1.3 %collective-permute-start.19 = (bf16[2,128,128]{2,1,0:T(8,128)(2,1)S(1)}, bf16[2,128,128]{2,1,0:T(8,128)(2,1)S(1)}, u32[]{:S(2)}, u32[]{:S(2)}) collective-permute-start(bf16[2,128,128]{2,1,0:T(8,128)(2,1)S(1)} %collective-permute-done.17.refs_4_), channel_id=1, source_target_pairs={{0,4},{4,0},{8,12},{12,8},{16,20},{20,16},{24,28},{28,24},{1,5},{5... | collective-permute-start | bytes 196616 | tf_op jit(solution)/shard_map/ppermute | solution.py:580
  31.1 1.5 %collective-permute-start.18 = (bf16[4,128,128]{2,1,0:T(8,128)(2,1)S(1)}, bf16[4,128,128]{2,1,0:T(8,128)(2,1)S(1)}, u32[]{:S(2)}, u32[]{:S(2)}) collective-permute-start(bf16[4,128,128]{2,1,0:T(8,128)(2,1)S(1)} %collective-permute-done.16.refs_3_), channel_id=1, source_target_pairs={{0,4},{4,0},{8,12},{12,8},{16,20},{20,16},{24,28},{28,24},{1,5},{5... | collective-permute-start | bytes 393224 | tf_op jit(solution)/shard_map/ppermute | solution.py:580
